TPU v7x, 32 devices: a whole 2x2x4 slice. The times are simulated.
32 devices in a mesh: dec: 8 (over y, x, core), ch: 4 (over z).
Axes of the slice: x: 2, y: 2, z: 4, core: 2. Of those that a mesh axis runs over, the one named last changes fastest.
Arguments:
- frame_cotangent: bfloat16 [64, 160, 8192], P('dec', None, 'ch'), may hold values from -5 to 5
- rollout_utterance: int32 [64], P('dec'), may hold values from 0 to 7, as said below
- frame_offset: int32 [64], P('dec'), may hold values from 0 to 32
- utterance_frames: int32 [8], P('dec'), may hold values from 1 to 128, 768 in all
- normed_input: bfloat16 [8, 128, 1024], P('dec', None, 'ch'), may hold values from -6 to 6
- expand_weight: bfloat16 [1024, 2, 1024], P(None, None, 'ch'), may hold values from -0.1875 to 0.1875
- depth_kernel: bfloat16 [9, 1024], P(None, 'ch'), may hold values from -2 to 2
- norm_scale: float32 [1024], P('ch'), may hold values from 0.1 to 1.9
- norm_shift: float32 [1024], P('ch'), may hold values from -3 to 3
- project_weight: bfloat16 [1024, 1024], replicated, may hold values from -0.1875 to 0.1875
- adapter_weight: bfloat16 [1024, 8192], P(None, 'ch'), may hold values from -0.0625 to 0.0625
Outputs:
- grad_stream: bfloat16 [8, 128, 1024], P('dec', None, 'ch')
- grad_normed: bfloat16 [8, 128, 1024], P('dec', None, 'ch')
Inputs may be any that keep to these rules, and one draw needn't show every extreme that they name: `rollout_utterance`: each utterance is named by exactly 8 rollouts; utterances k * 1 to (k + 1) - 1 are owned by index k of dec; among the 8 rollouts of one index of dec at most 1 name utterances of one owner, and some owner is named exactly 1 times; the rollouts of index k of dec always name some utterance of the owner (k + 4) mod 8.
All inputs are finite; a program needn't handle non-finite values. No bound on the sum of `utterance_frames` on one device may be relied on, other than what follows from the above.
Results may differ from a plain program's by a relative error of at most 0.03.
Values may be sent and summed in bfloat16 or wider, within the bound.
No kernel may reach another device: no remote copies, remote signals or barrier semaphores. Data moves between devices by JAX's collectives and lax.ppermute only.
A program may use at most 128 MiB of HBM per device.

v0:
```python
import jax
import jax.numpy as jnp
from jax import lax
from jax.sharding import PartitionSpec as P


def body(
    frame_cotangent,
    rollout_utterance,
    frame_offset,
    utterance_frames,
    normed_input,
    expand_weight,
    depth_kernel,
    norm_scale,
    norm_shift,
    project_weight,
    adapter_weight,
):
    local_rolls, seq_len, d_local = frame_cotangent.shape
    u_local, frames, c_local = normed_input.shape
    width = expand_weight.shape[0]
    taps = depth_kernel.shape[0]
    row_count = u_local * frames
    slabs = jax.vmap(lambda window, first: lax.dynamic_slice_in_dim(window, first, frames, 0))(
        frame_cotangent, frame_offset
    )
    flat_slabs = slabs.reshape(local_rolls, frames * d_local)
    target = jnp.arange(lax.axis_size("dec") * u_local, dtype=jnp.int32)
    select = (target[:, None] == rollout_utterance[None, :]).astype(jnp.bfloat16)
    rounded = lax.optimization_barrier(
        jnp.dot(select, flat_slabs, preferred_element_type=jnp.float32).astype(jnp.bfloat16)
    )
    received = lax.psum_scatter(
        rounded.astype(jnp.float32).astype(jnp.bfloat16), "dec", scatter_dimension=0, tiled=True
    ).astype(jnp.float32)
    frame_index = jnp.arange(frames, dtype=jnp.int32)
    mask = (frame_index[None, :] < utterance_frames[:, None]).astype(jnp.float32)
    frame_grad = (received.reshape(u_local, frames, d_local) * mask[:, :, None]).astype(
        jnp.bfloat16
    )
    grad_rows = frame_grad.reshape(row_count, d_local)
    block = adapter_weight
    stream_cols = lax.psum_scatter(
        lax.dot_general(
            block, grad_rows, (((1,), (1,)), ((), ())), preferred_element_type=jnp.float32
        ).astype(jnp.bfloat16),
        "ch",
        scatter_dimension=0,
        tiled=True,
    ).astype(jnp.float32)
    grad_stream = stream_cols.T.astype(jnp.bfloat16)
    expand_flat = expand_weight.reshape(width, 2 * c_local)
    piece = lax.all_gather(normed_input, "ch", axis=2, tiled=True)
    span = piece.shape[2]
    block = expand_flat
    expanded = jnp.dot(piece.reshape(row_count, span), block, preferred_element_type=jnp.float32)
    value = expanded[:, :c_local]
    gate = expanded[:, c_local:]
    sig_gate = jax.nn.sigmoid(gate)
    mask_rows = mask.reshape(row_count, 1)
    glu = (mask_rows * value * sig_gate).reshape(u_local, frames, c_local)
    kernel = depth_kernel.astype(jnp.float32)
    half = (taps - 1) // 2
    padded = jnp.pad(glu, ((0, 0), (half, half), (0, 0)))
    depth = jnp.zeros((u_local, frames, c_local), jnp.float32)
    for step in range(taps):
        depth = depth + kernel[step] * padded[:, step : step + frames, :]
    shifted = depth * norm_scale + norm_shift
    ch_start = lax.axis_index("ch") * c_local
    own_rows = lax.dynamic_slice_in_dim(project_weight, ch_start, c_local, 0)
    grad_swish = lax.dot_general(
        lax.all_gather(grad_stream, "ch", axis=1, tiled=True),
        own_rows,
        (((1,), (1,)), ((), ())),
        preferred_element_type=jnp.float32,
    )
    grad_swish = grad_swish.reshape(u_local, frames, c_local)
    sig_shift = jax.nn.sigmoid(shifted)
    grad_depth = grad_swish * sig_shift * (1.0 + shifted * (1.0 - sig_shift)) * norm_scale
    padded_back = jnp.pad(grad_depth, ((0, 0), (half, half), (0, 0)))
    grad_glu = jnp.zeros((u_local, frames, c_local), jnp.float32)
    for step in range(taps):
        grad_glu = (
            grad_glu + kernel[step] * padded_back[:, taps - 1 - step : taps - 1 - step + frames, :]
        )
    grad_glu = grad_glu.reshape(row_count, c_local) * mask_rows
    grad_value = grad_glu * sig_gate
    grad_gate = grad_glu * value * sig_gate * (1.0 - sig_gate)
    grad_expanded = jnp.concatenate([grad_value, grad_gate], axis=1).astype(jnp.bfloat16)
    block = expand_flat
    input_cols = lax.psum_scatter(
        lax.dot_general(
            block, grad_expanded, (((1,), (1,)), ((), ())), preferred_element_type=jnp.float32
        ).astype(jnp.bfloat16),
        "ch",
        scatter_dimension=0,
        tiled=True,
    ).astype(jnp.float32)
    grad_normed = input_cols.T.astype(jnp.bfloat16)
    return (
        grad_stream.reshape(u_local, frames, c_local),
        grad_normed.reshape(u_local, frames, c_local),
    )


def solution(mesh):
    return jax.shard_map(
        body,
        mesh=mesh,
        in_specs=(
            P("dec", None, "ch"),
            P("dec"),
            P("dec"),
            P("dec"),
            P("dec", None, "ch"),
            P(None, None, "ch"),
            P(None, "ch"),
            P("ch"),
            P("ch"),
            P(),
            P(None, "ch"),
        ),
        out_specs=(P("dec", None, "ch"), P("dec", None, "ch")),
        check_vma=False,
    )
```

profile of v0, /device:TPU:0, one launch (start us, length us, event | category | flops | bytes accessed | tf_op | source)
XLA Modules:
  0.0 211.9 jit_solution(5154354168152791260)
XLA Ops:
  7.2 0.8 fusion.30
  8.0 30.8 %while.1 = (s32[]{:T(128)}, bf16[8,160,2048]{2,1,0:T(8,128)(2,1)}, s32[8,3]{0,1:T(4,128)S(1)}, bf16[8,128,2048]{2,1,0:T(8,128)(2,1)}, s32[]{:T(128)}) while((s32[]{:T(128)}, bf16[8,160,2048]{2,1,0:T(8,128)(2,1)}, s32[8,3]{0,1:T(4,128)S(1)}, bf16[8,128,2048]{2,1,0:T(8,128)(2,1)}, s32[]{:T(128)}) %tuple.32), condition=%wide.while_cond, body=%wide.while_body.sunk | while | flops 2 | bytes 1049717 | solution.py:25
  8.1 0.5 fusion.41
  8.7 3.2 %dynamic-slice_dynamic-update-slice_fusion.2 = bf16[8,128,2048]{2,1,0:T(8,128)(2,1)} fusion(bf16[8,128,2048]{2,1,0:T(8,128)(2,1)} %get-tuple-element.68, s32[]{:T(128)S(6)} %copy.18, bf16[8,160,2048]{2,1,0:T(8,128)(2,1)} %get-tuple-element.71, s32[]{:T(128)} %bitcast.68, s32[]{:T(128)} %bitcast.69), kind=kLoop, calls=%fused_computation.clone.1 | loop fusion | bytes 1049604 | tf_op jit(solution)/shard_map/vmap()/gather
  12.0 0.5 fusion.41
  12.5 3.3 %dynamic-slice_dynamic-update-slice_fusion.2 = bf16[8,128,2048]{2,1,0:T(8,128)(2,1)} fusion(bf16[8,128,2048]{2,1,0:T(8,128)(2,1)} %get-tuple-element.68, s32[]{:T(128)S(6)} %copy.18, bf16[8,160,2048]{2,1,0:T(8,128)(2,1)} %get-tuple-element.71, s32[]{:T(128)} %bitcast.68, s32[]{:T(128)} %bitcast.69), kind=kLoop, calls=%fused_computation.clone.1 | loop fusion | bytes 1049604 | tf_op jit(solution)/shard_map/vmap()/gather
  15.8 0.5 fusion.41
  16.3 3.3 %dynamic-slice_dynamic-update-slice_fusion.2 = bf16[8,128,2048]{2,1,0:T(8,128)(2,1)} fusion(bf16[8,128,2048]{2,1,0:T(8,128)(2,1)} %get-tuple-element.68, s32[]{:T(128)S(6)} %copy.18, bf16[8,160,2048]{2,1,0:T(8,128)(2,1)} %get-tuple-element.71, s32[]{:T(128)} %bitcast.68, s32[]{:T(128)} %bitcast.69), kind=kLoop, calls=%fused_computation.clone.1 | loop fusion | bytes 1049604 | tf_op jit(solution)/shard_map/vmap()/gather
  19.7 0.5 fusion.41
  20.2 3.3 %dynamic-slice_dynamic-update-slice_fusion.2 = bf16[8,128,2048]{2,1,0:T(8,128)(2,1)} fusion(bf16[8,128,2048]{2,1,0:T(8,128)(2,1)} %get-tuple-element.68, s32[]{:T(128)S(6)} %copy.18, bf16[8,160,2048]{2,1,0:T(8,128)(2,1)} %get-tuple-element.71, s32[]{:T(128)} %bitcast.68, s32[]{:T(128)} %bitcast.69), kind=kLoop, calls=%fused_computation.clone.1 | loop fusion | bytes 1049604 | tf_op jit(solution)/shard_map/vmap()/gather
  23.5 0.5 fusion.41
  24.1 3.3 %dynamic-slice_dynamic-update-slice_fusion.2 = bf16[8,128,2048]{2,1,0:T(8,128)(2,1)} fusion(bf16[8,128,2048]{2,1,0:T(8,128)(2,1)} %get-tuple-element.68, s32[]{:T(128)S(6)} %copy.18, bf16[8,160,2048]{2,1,0:T(8,128)(2,1)} %get-tuple-element.71, s32[]{:T(128)} %bitcast.68, s32[]{:T(128)} %bitcast.69), kind=kLoop, calls=%fused_computation.clone.1 | loop fusion | bytes 1049604 | tf_op jit(solution)/shard_map/vmap()/gather
  27.9 3.3 %dynamic-slice_dynamic-update-slice_fusion.2 = bf16[8,128,2048]{2,1,0:T(8,128)(2,1)} fusion(bf16[8,128,2048]{2,1,0:T(8,128)(2,1)} %get-tuple-element.68, s32[]{:T(128)S(6)} %copy.18, bf16[8,160,2048]{2,1,0:T(8,128)(2,1)} %get-tuple-element.71, s32[]{:T(128)} %bitcast.68, s32[]{:T(128)} %bitcast.69), kind=kLoop, calls=%fused_computation.clone.1 | loop fusion | bytes 1049604 | tf_op jit(solution)/shard_map/vmap()/gather
  31.8 3.2 %dynamic-slice_dynamic-update-slice_fusion.2 = bf16[8,128,2048]{2,1,0:T(8,128)(2,1)} fusion(bf16[8,128,2048]{2,1,0:T(8,128)(2,1)} %get-tuple-element.68, s32[]{:T(128)S(6)} %copy.18, bf16[8,160,2048]{2,1,0:T(8,128)(2,1)} %get-tuple-element.71, s32[]{:T(128)} %bitcast.68, s32[]{:T(128)} %bitcast.69), kind=kLoop, calls=%fused_computation.clone.1 | loop fusion | bytes 1049604 | tf_op jit(solution)/shard_map/vmap()/gather
  35.6 3.3 %dynamic-slice_dynamic-update-slice_fusion.2 = bf16[8,128,2048]{2,1,0:T(8,128)(2,1)} fusion(bf16[8,128,2048]{2,1,0:T(8,128)(2,1)} %get-tuple-element.68, s32[]{:T(128)S(6)} %copy.18, bf16[8,160,2048]{2,1,0:T(8,128)(2,1)} %get-tuple-element.71, s32[]{:T(128)} %bitcast.68, s32[]{:T(128)} %bitcast.69), kind=kLoop, calls=%fused_computation.clone.1 | loop fusion | bytes 1049604 | tf_op jit(solution)/shard_map/vmap()/gather
  38.9 4.5 %copy.13 = bf16[1,8,128,2048]{3,1,2,0:T(8,128)(2,1)S(1)} copy(bf16[1,8,128,2048]{3,2,1,0:T(8,128)(2,1)} %bitcast.74) | data formatting | bytes 8388608
  43.4 3.2 %convolution_convert_fusion = bf16[8,262144]{1,0:T(8,128)(2,1)} fusion(bf16[8,262144]{1,0:T(8,128)(2,1)S(1)} %bitcast.71, s32[8]{0:T(128)S(1)} %copy-done.3), kind=kOutput, calls=%fused_computation.2 | convolution fusion | flops 35651648 | bytes 8388640 | tf_op jit(solution)/shard_map/dot_general | solution.py:32
  47.3 0.6 dynamic-slice.4
  47.9 0.6 fusion.34
  48.5 81.9 %all-reduce.6.cloned.1.call-done = bf16[8,262144]{1,0:T(8,128)(2,1)} async-done(((bf16[8,262144]{1,0:T(8,128)(2,1)}), bf16[8,262144]{1,0:T(8,128)(2,1)}) %all-reduce.6.cloned.1.call-update) | async-done | bytes 4194320
  130.5 12.0 %fusion.5 = f32[262144]{0:T(1024)S(1)} fusion(bf16[8,262144]{1,0:T(8,128)(2,1)} %all-reduce.6.cloned.1.call-done, u32[]{:T(128)} %bitcast.24), kind=kLoop, calls=%fused_computation.12 | loop fusion | flops 262144 | bytes 1572868 | tf_op jit(solution)/shard_map/reshape | solution.py:39
  142.5 1.1 reshape.134
  143.6 4.7 %fusion = bf16[1024,128]{0,1:T(8,128)(2,1)} fusion(bf16[1024,2048]{1,0:T(8,128)(2,1)} %param.21, f32[128,2048]{1,0:T(8,128)} %reshape.134, f32[128]{0:T(128)S(1)} %compare_convert_fusion), kind=kOutput, calls=%fused_computation.5 | convolution fusion | flops 537526272 | bytes 5505536 | tf_op jit(solution)/shard_map/dot_general | solution.py:45
  148.5 15.0 %all_gather.7 = bf16[1,128,1024]{2,1,0:T(8,128)(2,1)} all-gather(bf16[1,128,256]{2,1,0:T(8,128)(2,1)S(1)} %copy-done.1), channel_id=1, replica_groups=mesh['dec'=8,'ch'=4] {'ch'}, dimensions={2}, use_global_device_ids=true | all-gather | bytes 327680 | tf_op jit(solution)/shard_map/all_gather | solution.py:54
  163.5 1.4 copy.14
  164.9 1.3 fusion.8
  166.3 2.3 %reduce-scatter.3.cloned.1.call-done = bf16[256,128]{0,1:T(8,128)(2,1)} async-done(((bf16[1024,128]{0,1:T(8,128)(2,1)}), bf16[256,128]{0,1:T(8,128)(2,1)}) %reduce-scatter.3.cloned.1.call-update) | async-done | bytes 65552 | tf_op jit(solution)/shard_map/reduce_scatter | solution.py:44
  168.6 14.7 %all_gather.6 = bf16[128,1024]{1,0:T(8,128)(2,1)S(1)} all-gather(bf16[128,256]{1,0:T(8,128)(2,1)} %bitcast.76), channel_id=1, replica_groups=mesh['dec'=8,'ch'=4] {'ch'}, dimensions={1}, use_global_device_ids=true | all-gather | bytes 327680 | tf_op jit(solution)/shard_map/all_gather | solution.py:73
  183.2 1.1 fusion.4
  184.4 0.9 multiply_convert_fusion.3
  185.3 1.2 fusion.1
  186.5 18.9 %reduce-scatter.5.cloned.1.call-done = bf16[256,128]{0,1:T(8,128)(2,1)} async-done(((bf16[1024,128]{0,1:T(8,128)(2,1)}), bf16[256,128]{0,1:T(8,128)(2,1)}) %reduce-scatter.5.cloned.1.call-update) | async-done | bytes 65552 | tf_op jit(solution)/shard_map/reduce_scatter | solution.py:92
  (33 shorter events, 2.5 us)
Async XLA Ops:
  7.2 176.1 %copy-start = (bf16[1024,1024]{1,0:T(8,128)(2,1)S(1)}, bf16[1024,1024]{1,0:T(8,128)(2,1)}, u32[]{:S(2)}) copy-start(bf16[1024,1024]{1,0:T(8,128)(2,1)} %param.20) | copy-start | bytes 6291460
  7.2 123.3 %all-reduce.6.cloned.1.call-start = ((), (), s32[]{:S(2)}) async-start(), calls=%async_computation.4 | async-start | bytes 8388608
  38.9 4.5 %copy-start.3 = (s32[8]{0:T(128)S(1)}, s32[8]{0:T(128)}, u32[]{:S(2)}) copy-start(s32[8]{0:T(128)} %param.12) | copy-start | bytes 100
  46.6 0.7 copy-start.4
  46.6 1.3 copy-start.2
  46.6 122.0 %reduce-scatter.3.cloned.1.call-start = ((), (), s32[]{:S(2)}) async-start(), calls=%async_computation.2 | async-start | bytes 327680 | tf_op jit(solution)/shard_map/reduce_scatter | solution.py:44
  142.5 6.0 %copy-start.1 = (bf16[1,128,256]{2,1,0:T(8,128)(2,1)S(1)}, bf16[1,128,256]{2,1,0:T(8,128)(2,1)}, u32[]{:S(2)}) copy-start(bf16[1,128,256]{2,1,0:T(8,128)(2,1)} %param.15) | copy-start | bytes 196612
  148.4 57.0 %reduce-scatter.5.cloned.1.call-start = ((), (), s32[]{:S(2)}) async-start(), calls=%async_computation.3 | async-start | bytes 327680 | tf_op jit(solution)/shard_map/reduce_scatter | solution.py:92
Sparse Core Ops, SparseCore 0:
  46.7 83.6 all-reduce.5
  148.5 20.0 reduce-scatter.2
  186.6 18.7 reduce-scatter.4
where the time goes:
time: 213 us; the launch traced here: 212 us
  waiting for transfers between devices  103 us (48%)
  local copies, waits for them, and re-layouts  39.1 us (18%)
  blocking collectives  29.7 us (14%)
  between operations  14.5 us (7%)
  other arithmetic  13.8 us (6%)
  matrix products  11.5 us (5%)
    unnamed x4, waiting for transfers between devices  82 us
    gather x24, local copies, waits for them, and re-layouts  30.8 us
    reduce_scatter x1, waiting for transfers between devices, body(): lax.psum_scatter(lax.dot_general(block, grad_expanded, (((1,), (1,)), (()...  18.9 us
    all_gather x1, blocking collectives, body(): piece = lax.all_gather(normed_input, 'ch', axis=2, tiled=True)  15 us
    all_gather x1, blocking collectives, body(): lax.all_gather(grad_stream, 'ch', axis=1, tiled=True)  14.7 us
    reshape x1, other arithmetic, body(): received.reshape(u_local, frames, d_local) * mask[:, :, None]  12 us
    unnamed x14, local copies, waits for them, and re-layouts  6.56 us
    dot_general x1, matrix products, body(): lax.dot_general(block, grad_rows, (((1,), (1,)), ((), ())), preferred_ele...  4.75 us
  transfers between devices with their start and end apart: 3, of which 3 were waited for; matrix products, arithmetic and copies ran while one was open for 2% of the time, Pallas kernels for 0%

commit v1 on v0

v1 whole, which is shorter than its diff:
```python
import functools

import jax
import jax.numpy as jnp
from jax import lax
from jax.experimental import pallas as pl
from jax.experimental.pallas import tpu as pltpu
from jax.sharding import PartitionSpec as P

F32 = jnp.float32
BF16 = jnp.bfloat16
NT = (((1,), (1,)), ((), ()))
NN = (((1,), (0,)), ((), ()))
ROW_TILE = 16
LANES = 128
COLS = 256
VMEM = pl.BlockSpec(memory_space=pltpu.VMEM)
SMEM = pl.BlockSpec(memory_space=pltpu.SMEM)


def dot(a, b, dims):
    return lax.dot_general(a, b, dims, preferred_element_type=F32)


def adapter_kernel(flip, frames, index, utts, offsets, windows, weight, out, slabs, product, sem):
    targets = out.shape[0]
    rolls, seq_len, _ = windows.shape
    span = slabs.shape[0] // targets
    dec = index[0]

    def pick(step):
        target = ((dec // 2) ^ step) * 2 + ((dec % 2) ^ flip)
        found, first = jnp.int32(-1), jnp.int32(0)
        for roll in range(rolls):
            hit = utts[roll] == target
            found = jnp.where(hit, roll, found)
            first = jnp.where(hit, offsets[roll], first)
        start = jnp.minimum(first // ROW_TILE * ROW_TILE, seq_len - span)
        return found, start, first - start

    picks = [pick(step) for step in range(targets)]

    def copy(step):
        found, start, _ = picks[step]
        return pltpu.make_async_copy(
            windows.at[jnp.maximum(found, 0), pl.ds(pl.multiple_of(start, ROW_TILE), span), :],
            slabs.at[pl.ds(step * span, span), :],
            sem.at[step],
        )

    @pl.when(pl.program_id(0) == 0)
    def _():
        for step in range(targets):
            copy(step).start()
        for step in range(targets):
            copy(step).wait()

    result = dot(slabs[...], weight[...], NT)
    for lane in range(COLS // LANES):
        product[lane, :, :] = result[:, lane * LANES : (lane + 1) * LANES]
    for step in range(targets):
        found, _, shift = picks[step]
        for lane in range(COLS // LANES):
            rows = product[lane, pl.ds(step * span + shift, frames), :]
            out[step, :, lane * LANES : (lane + 1) * LANES] = jnp.where(found >= 0, rows, 0.0).astype(BF16)


def adapter(flip, targets, frames, index, utts, offsets, windows, weight):
    rolls, seq_len, d_local = windows.shape
    width = weight.shape[0]
    span = frames + ROW_TILE
    return pl.pallas_call(
        functools.partial(adapter_kernel, flip, frames),
        grid=(width // COLS,),
        out_shape=jax.ShapeDtypeStruct((targets, frames, width), BF16),
        in_specs=[
            SMEM,
            SMEM,
            SMEM,
            pl.BlockSpec(memory_space=pl.ANY),
            pl.BlockSpec((COLS, d_local), lambda n: (n, 0)),
        ],
        out_specs=pl.BlockSpec((targets, frames, COLS), lambda n: (0, 0, n)),
        scratch_shapes=[
            pltpu.VMEM((targets * span, d_local), BF16),
            pltpu.VMEM((COLS // LANES, targets * span, LANES), F32),
            pltpu.SemaphoreType.DMA((targets,)),
        ],
        compiler_params=pltpu.CompilerParams(vmem_limit_bytes=24 << 20),
        cost_estimate=pl.CostEstimate(
            flops=2 * targets * span * d_local * width,
            bytes_accessed=2 * (targets * span * d_local + width * d_local + targets * frames * width),
            transcendentals=0,
        ),
        name="adapter_other" if flip else "adapter_own",
    )(index, utts, offsets, windows, weight)


def pair_sum_kernel(own, other, *outs):
    for step, out in enumerate(outs):
        out[...] = (own[step].astype(F32) + other[step].astype(F32)).astype(BF16)


def pair_sum(own, other):
    targets, frames, width = own.shape
    return pl.pallas_call(
        pair_sum_kernel,
        out_shape=[jax.ShapeDtypeStruct((frames, width), BF16)] * targets,
        in_specs=[VMEM] * 2,
        out_specs=[VMEM] * targets,
        compiler_params=pltpu.CompilerParams(vmem_limit_bytes=24 << 20),
        name="pair_sum",
    )(own, other)


def swish_kernel(parts, index, valid, project, *refs):
    blocks, outs, stream = refs[:parts], refs[parts:-1], refs[-1]
    frames, width = stream.shape
    c_local = outs[0].shape[1] // 2
    total = blocks[0][...].astype(F32)
    for block in blocks[1:]:
        total = total + block[...].astype(F32)
    rows = lax.broadcasted_iota(jnp.int32, (frames, width), 0)
    stream[...] = jnp.where(rows < valid[0], total, 0.0).astype(BF16)
    ch = index[1]
    for step, out in enumerate(outs):
        at = pl.ds(pl.multiple_of((ch ^ step) * c_local, c_local), c_local)
        out[:, :c_local] = stream[:, at].astype(out.dtype)
        out[:, c_local:] = dot(stream[...], project[at, :], NT).astype(out.dtype)


def swish(index, valid, project, blocks, groups):
    frames, width = blocks[0].shape
    c_local = width // groups
    return pl.pallas_call(
        functools.partial(swish_kernel, len(blocks)),
        out_shape=[jax.ShapeDtypeStruct((frames, 2 * c_local), F32 if step == 0 else BF16) for step in range(groups)],
        in_specs=[SMEM, SMEM, VMEM] + [VMEM] * len(blocks),
        out_specs=[VMEM] * groups,
        scratch_shapes=[pltpu.VMEM((frames, width), BF16)],
        compiler_params=pltpu.CompilerParams(vmem_limit_bytes=24 << 20),
        name="stream_and_swish",
    )(index, valid, project, *blocks)


def forward_kernel(parts, index, valid, expand, taps_ref, scale, shift, *refs):
    blocks, (value_out, gate_out, slope_out), padded = refs[:parts], refs[parts:-1], refs[-1]
    frames, c_local = value_out.shape
    taps = taps_ref.shape[0]
    half = (taps - 1) // 2
    ch = index[1]
    expanded = jnp.zeros((frames, 2 * c_local), F32)
    for step, block in enumerate(blocks):
        at = pl.ds(pl.multiple_of((ch ^ step) * c_local, c_local), c_local)
        expanded = expanded + dot(block[...], expand[at, :], NN)
    value = expanded[:, :c_local]
    gate = jax.nn.sigmoid(expanded[:, c_local:])
    rows = lax.broadcasted_iota(jnp.int32, (frames, c_local), 0)
    glu = jnp.where(rows < valid[0], value * gate, 0.0)
    edge = padded.shape[0] - frames
    padded[: edge // 2, :] = jnp.zeros((edge // 2, c_local), F32)
    padded[edge // 2 + frames :, :] = jnp.zeros((edge // 2, c_local), F32)
    padded[pl.ds(edge // 2, frames), :] = glu
    depth = jnp.zeros((frames, c_local), F32)
    for tap in range(taps):
        depth = depth + taps_ref[tap : tap + 1, :] * padded[pl.ds(edge // 2 - half + tap, frames), :]
    shifted = depth * scale[...] + shift[...]
    sig = jax.nn.sigmoid(shifted)
    value_out[...] = value
    gate_out[...] = gate
    slope_out[...] = sig * (1.0 + shifted * (1.0 - sig)) * scale[...]


def edge_of(taps):
    return 2 * (-(-((taps - 1) // 2) // 8) * 8)


def forward(index, valid, expand, taps, scale, shift, blocks):
    frames, c_local = blocks[0].shape
    return pl.pallas_call(
        functools.partial(forward_kernel, len(blocks)),
        out_shape=[jax.ShapeDtypeStruct((frames, c_local), F32)] * 3,
        in_specs=[SMEM, SMEM] + [VMEM] * (4 + len(blocks)),
        out_specs=[VMEM] * 3,
        scratch_shapes=[pltpu.VMEM((frames + edge_of(taps.shape[0]), c_local), F32)],
        compiler_params=pltpu.CompilerParams(vmem_limit_bytes=16 << 20),
        name="forward_gates",
    )(index, valid, expand, taps, scale, shift, *blocks)


def backward_kernel(parts, index, valid, expand, taps_ref, value_ref, gate_ref, slope, *refs):
    blocks, stream_out, outs, padded = refs[:parts], refs[parts], refs[parts + 1 : -1], refs[-1]
    frames, c_local = stream_out.shape
    taps = taps_ref.shape[0]
    half = (taps - 1) // 2
    ch = index[1]
    total = blocks[0][...].astype(F32)
    for block in blocks[1:]:
        total = total + block[...].astype(F32)
    stream_out[...] = total[:, :c_local].astype(BF16)
    edge = padded.shape[0] - frames
    padded[: edge // 2, :] = jnp.zeros((edge // 2, c_local), F32)
    padded[edge // 2 + frames :, :] = jnp.zeros((edge // 2, c_local), F32)
    padded[pl.ds(edge // 2, frames), :] = total[:, c_local:] * slope[...]
    grad = jnp.zeros((frames, c_local), F32)
    for tap in range(taps):
        grad = grad + taps_ref[tap : tap + 1, :] * padded[pl.ds(edge // 2 + half - tap, frames), :]
    rows = lax.broadcasted_iota(jnp.int32, (frames, c_local), 0)
    grad = jnp.where(rows < valid[0], grad, 0.0)
    gate = gate_ref[...]
    grad_value = grad * gate
    grad_gate = grad_value * value_ref[...] * (1.0 - gate)
    grad_expanded = jnp.concatenate([grad_value.astype(BF16), grad_gate.astype(BF16)], axis=1)
    for step, out in enumerate(outs):
        at = pl.ds(pl.multiple_of((ch ^ step) * c_local, c_local), c_local)
        out[...] = dot(grad_expanded, expand[at, :], NT).astype(out.dtype)


def backward(index, valid, expand, taps, value, gate, slope, blocks, groups):
    frames, c_local = value.shape
    return pl.pallas_call(
        functools.partial(backward_kernel, len(blocks)),
        out_shape=[jax.ShapeDtypeStruct((frames, c_local), BF16)]
        + [jax.ShapeDtypeStruct((frames, c_local), F32 if step == 0 else BF16) for step in range(groups)],
        in_specs=[SMEM, SMEM] + [VMEM] * (5 + len(blocks)),
        out_specs=[VMEM] * (1 + groups),
        scratch_shapes=[pltpu.VMEM((frames + edge_of(taps.shape[0]), c_local), F32)],
        compiler_params=pltpu.CompilerParams(vmem_limit_bytes=16 << 20),
        name="backward_module",
    )(index, valid, expand, taps, value, gate, slope, *blocks)


def swap(block, axis, count, mask):
    return lax.ppermute(block, axis, [(i, i ^ mask) for i in range(count)])


def body(
    n_dec,
    n_ch,
    frame_cotangent,
    rollout_utterance,
    frame_offset,
    utterance_frames,
    normed_input,
    expand_weight,
    depth_kernel,
    norm_scale,
    norm_shift,
    project_weight,
    adapter_weight,
):
    u_local, frames, c_local = normed_input.shape
    width = expand_weight.shape[0]
    chips = n_dec // 2
    index = jnp.stack([lax.axis_index("dec"), lax.axis_index("ch")]).astype(jnp.int32)
    own_input = normed_input.reshape(frames, c_local)
    inputs = [own_input] + [swap(own_input, "ch", n_ch, step) for step in range(1, n_ch)]
    expand = expand_weight.reshape(width, 2 * c_local)
    taps = depth_kernel.astype(F32)
    scale, shift = norm_scale.reshape(1, c_local), norm_shift.reshape(1, c_local)

    route = (index, rollout_utterance, frame_offset, frame_cotangent, adapter_weight)
    for_other = adapter(1, chips, frames, *route)
    from_other = swap(for_other, "dec", n_dec, 1)
    own = adapter(0, chips, frames, *route)
    sums = pair_sum(own, from_other)
    arrived = [sums[0]] + [swap(sums[step], "dec", n_dec, 2 * step) for step in reversed(range(1, chips))]
    value, gate, slope = forward(index, utterance_frames, expand, taps, scale, shift, inputs)
    halves = swish(index, utterance_frames, project_weight, arrived, n_ch)
    halves = [halves[0]] + [swap(halves[step], "ch", n_ch, step) for step in range(1, n_ch)]
    stream, *parts = backward(index, utterance_frames, expand, taps, value, gate, slope, halves, n_ch)
    total = parts[0]
    for step in range(1, n_ch):
        total = total + swap(parts[step], "ch", n_ch, step).astype(F32)
    return stream[None], total.astype(BF16)[None]


def solution(mesh):
    return jax.shard_map(
        functools.partial(body, mesh.shape["dec"], mesh.shape["ch"]),
        mesh=mesh,
        in_specs=(
            P("dec", None, "ch"),
            P("dec"),
            P("dec"),
            P("dec"),
            P("dec", None, "ch"),
            P(None, None, "ch"),
            P(None, "ch"),
            P("ch"),
            P("ch"),
            P(),
            P(None, "ch"),
        ),
        out_specs=(P("dec", None, "ch"), P("dec", None, "ch")),
        check_vma=False,
    )
```

time: 213 us -> 69.4 us (0.33)
  waiting for transfers between devices: 103 us -> 26.9 us
  local copies, waits for them, and re-layouts: 39.1 us -> 6.25 us
  blocking collectives: 29.7 us -> 0 us
  starting transfers between devices: 0.12 us -> 19.1 us
  Pallas kernels: 0 us -> 14.7 us
  other arithmetic: 13.8 us -> 0.74 us
  between operations: 14.5 us -> 1.45 us
  matrix products: 11.5 us -> 0 us
    unnamed x4 -> x0, waiting for transfers between devices: 82 us -> none
    gather x24 -> x0, local copies, waits for them, and re-layouts: 30.8 us -> none
    all_gather x2 -> x0, blocking collectives: 29.7 us -> none  [the longest x1 15 us: body(): piece = lax.all_gather(normed_input, 'ch', axis=2, tiled=True)]
    ppermute x0 -> x13, waiting for transfers between devices: none -> 26.9 us  [swap(): return lax.ppermute(block, axis, [(i, i ^ mask) for i in range(count)])]
    reduce_scatter x2 -> x0, waiting for transfers between devices: 21.2 us -> none  [the longest x1 18.9 us: body(): lax.psum_scatter(lax.dot_general(block, grad_expanded, (((1,), (1,)), (()...]
    ppermute x0 -> x13, starting transfers between devices: none -> 19.1 us  [swap(): return lax.ppermute(block, axis, [(i, i ^ mask) for i in range(count)])]
    pallas_call x0 -> x6, Pallas kernels: none -> 14.7 us  [the longest x2 10.2 us: adapter(): pl.pallas_call(functools.partial(adapter_kernel, flip, frames), grid=(wid...]
    reshape x2 -> x0, other arithmetic: 12.1 us -> none  [the longest x1 12 us: body(): received.reshape(u_local, frames, d_local) * mask[:, :, None]]
  transfers between devices with their start and end apart: 3 -> 13, of which waited for: 3 -> 6; matrix products, arithmetic and copies ran while one was open for 2% -> 0% of each run, Pallas kernels for 0% -> 11%
where the time goes in v1:
time: 69.4 us; the launch traced here: 69.2 us
  waiting for transfers between devices  26.9 us (39%)
  starting transfers between devices  19.1 us (28%)
  Pallas kernels  14.7 us (21%)
  local copies, waits for them, and re-layouts  6.25 us (9%)
  between operations  1.45 us (2%)
  other arithmetic  0.74 us (1%)
    ppermute x13, waiting for transfers between devices, swap(): return lax.ppermute(block, axis, [(i, i ^ mask) for i in range(count)])  26.9 us
    ppermute x13, starting transfers between devices, swap(): return lax.ppermute(block, axis, [(i, i ^ mask) for i in range(count)])  19.1 us
    pallas_call x2, Pallas kernels, adapter(): pl.pallas_call(functools.partial(adapter_kernel, flip, frames), grid=(wid...  10.2 us
    unnamed x21, local copies, waits for them, and re-layouts  6.25 us
    pallas_call x1, Pallas kernels, backward(): pl.pallas_call(functools.partial(backward_kernel, len(blocks)), out_shape...  1.68 us
    pallas_call x1, Pallas kernels, swish(): pl.pallas_call(functools.partial(swish_kernel, len(blocks)), out_shape=[j...  1.41 us
  transfers between devices with their start and end apart: 13, of which 6 were waited for; matrix products, arithmetic and copies ran while one was open for 0% of the time, Pallas kernels for 11%

profile of v1, /device:TPU:0, one launch (start us, length us, event | category | flops | bytes accessed | tf_op | source)
XLA Modules:
  0.0 69.2 jit_solution(17387552029423774366)
XLA Ops:
  0.6 0.1 pad_add_fusion.index
  0.7 2.5 %copy-done = bf16[8,160,2048]{2,1,0:T(8,128)(2,1)S(1)} copy-done((bf16[8,160,2048]{2,1,0:T(8,128)(2,1)S(1)}, bf16[8,160,2048]{2,1,0:T(8,128)(2,1)}, u32[]{:S(2)}) %copy-start) | copy-done | bytes 5242904
  3.2 2.2 %copy-done.1 = bf16[1024,2048]{1,0:T(8,128)(2,1)S(1)} copy-done((bf16[1024,2048]{1,0:T(8,128)(2,1)S(1)}, bf16[1024,2048]{1,0:T(8,128)(2,1)}, u32[]{:S(2)}) %copy-start.1) | copy-done | bytes 4194328
  5.4 0.7 copy-done.4
  6.0 0.7 copy-done.5
  6.7 5.1 %adapter_other.1 = bf16[4,128,1024]{2,1,0:T(8,128)(2,1)S(1)} custom-call(s32[2]{0:T(128)S(1)} %pad_add_fusion.index, s32[8]{0:T(128)S(1)} %copy-done.4, s32[8]{0:T(128)S(1)} %copy-done.5, bf16[8,160,2048]{2,1,0:T(8,128)(2,1)S(1)} %copy-done, bf16[1024,2048]{1,0:T(8,128)(2,1)S(1)} %copy-done.1), custom_call_target="tpu_custom_call" | custom-call | flops 2415919104 | bytes 7602176 | tf_op jit(solution)/shard_map/adapter_other/pallas_call | solution.py:72
  11.8 0.5 collective-permute-start.3
  12.4 5.1 %adapter_own.1.own = bf16[4,128,1024]{2,1,0:T(8,128)(2,1)S(1)} custom-call(s32[2]{0:T(128)S(1)} %pad_add_fusion.index, s32[8]{0:T(128)S(1)} %copy-done.4, s32[8]{0:T(128)S(1)} %copy-done.5, bf16[8,160,2048]{2,1,0:T(8,128)(2,1)S(1)} %copy-done, bf16[1024,2048]{1,0:T(8,128)(2,1)S(1)} %copy-done.1), custom_call_target="tpu_custom_call" | custom-call | flops 2415919104 | bytes 7602176 | tf_op jit(solution)/shard_map/adapter_own/pallas_call | solution.py:72
  17.6 0.2 pair_sum.1
  17.8 3.6 %collective-permute-start.4 = (bf16[128,1024]{1,0:T(8,128)(2,1)S(1)}, bf16[128,1024]{1,0:T(8,128)(2,1)S(1)}, u32[]{:S(2)}, u32[]{:S(2)}) collective-permute-start(bf16[128,1024]{1,0:T(8,128)(2,1)S(1)} %get-tuple-element.22), channel_id=1, source_target_pairs={{0,24},{4,28},{8,16},{12,20},{16,8},{20,12},{24,0},{28,4},{1,25},{... | collective-permute-start | bytes 786440 | tf_op jit(solution)/shard_map/ppermute | solution.py:234
  21.4 0.5 collective-permute-start.5
  21.9 0.1 collective-permute-start.6
  22.0 2.0 %collective-permute-start = (bf16[128,256]{1,0:T(8,128)(2,1)S(1)}, bf16[128,256]{1,0:T(8,128)(2,1)S(1)}, u32[]{:S(2)}, u32[]{:S(2)}) collective-permute-start(bf16[128,256]{1,0:T(8,128)(2,1)S(1)} %bitcast.12), channel_id=1, source_target_pairs={{0,1},{1,0},{2,3},{3,2},{4,5},{5,4},{6,7},{7,6},{8,9},{9,8},{10,11... | collective-permute-start | bytes 196616 | tf_op jit(solution)/shard_map/ppermute | solution.py:234
  24.6 3.9 %collective-permute-done.4.refs_1_ = bf16[128,1024]{1,0:T(8,128)(2,1)S(1)} collective-permute-done((bf16[128,1024]{1,0:T(8,128)(2,1)S(1)}, bf16[128,1024]{1,0:T(8,128)(2,1)S(1)}, u32[]{:S(2)}, u32[]{:S(2)}) %collective-permute-start.4) | collective-permute-done | bytes 262176 | tf_op jit(solution)/shard_map/ppermute | solution.py:234
  28.6 5.3 %collective-permute-done.5.refs_2_ = bf16[128,1024]{1,0:T(8,128)(2,1)S(1)} collective-permute-done((bf16[128,1024]{1,0:T(8,128)(2,1)S(1)}, bf16[128,1024]{1,0:T(8,128)(2,1)S(1)}, u32[]{:S(2)}, u32[]{:S(2)}) %collective-permute-start.5) | collective-permute-done | bytes 262176 | tf_op jit(solution)/shard_map/ppermute | solution.py:234
  33.9 0.3 collective-permute-done.6.refs_3_
  34.2 1.4 %stream_and_swish.1 = (f32[128,512]{1,0:T(8,128)S(1)}, bf16[128,512]{1,0:T(8,128)(2,1)S(1)}, bf16[128,512]{1,0:T(8,128)(2,1)S(1)}, bf16[128,512]{1,0:T(8,128)(2,1)S(1)}) custom-call(s32[2]{0:T(128)S(1)} %pad_add_fusion.index, s32[1]{0:T(128)S(6)} %copy.14.valid, bf16[1024,1024]{1,0:T(8,128)(2,1)S(1)} %copy-done.2, ...), custom_call_target="tpu_custom_call" | custom-call | tf_op jit(solution)/shard_map/stream_and_swish/pallas_call | solution.py:135
  35.6 1.6 %collective-permute-start.7 = (bf16[128,512]{1,0:T(8,128)(2,1)S(1)}, bf16[128,512]{1,0:T(8,128)(2,1)S(1)}, u32[]{:S(2)}, u32[]{:S(2)}) collective-permute-start(bf16[128,512]{1,0:T(8,128)(2,1)S(1)} %get-tuple-element.26), channel_id=1, source_target_pairs={{0,1},{1,0},{2,3},{3,2},{4,5},{5,4},{6,7},{7,6},{8,9},{9,8},{10,11... | collective-permute-start | bytes 393224 | tf_op jit(solution)/shard_map/ppermute | solution.py:234
  37.3 2.6 %collective-permute-start.8 = (bf16[128,512]{1,0:T(8,128)(2,1)S(1)}, bf16[128,512]{1,0:T(8,128)(2,1)S(1)}, u32[]{:S(2)}, u32[]{:S(2)}) collective-permute-start(bf16[128,512]{1,0:T(8,128)(2,1)S(1)} %get-tuple-element.27), channel_id=1, source_target_pairs={{0,2},{1,3},{2,0},{3,1},{4,6},{5,7},{6,4},{7,5},{8,10},{9,11},{10,... | collective-permute-start | bytes 393224 | tf_op jit(solution)/shard_map/ppermute | solution.py:234
  39.9 0.2 collective-permute-start.9
  40.1 1.7 %collective-permute-start.1 = (bf16[128,256]{1,0:T(8,128)(2,1)S(1)}, bf16[128,256]{1,0:T(8,128)(2,1)S(1)}, u32[]{:S(2)}, u32[]{:S(2)}) collective-permute-start(bf16[128,256]{1,0:T(8,128)(2,1)S(1)} %bitcast.13), channel_id=1, source_target_pairs={{0,2},{1,3},{2,0},{3,1},{4,6},{5,7},{6,4},{7,5},{8,10},{9,11},{10,... | collective-permute-start | bytes 196616 | tf_op jit(solution)/shard_map/ppermute | solution.py:234
  41.8 1.9 %collective-permute-start.2 = (bf16[128,256]{1,0:T(8,128)(2,1)S(1)}, bf16[128,256]{1,0:T(8,128)(2,1)S(1)}, u32[]{:S(2)}, u32[]{:S(2)}) collective-permute-start(bf16[128,256]{1,0:T(8,128)(2,1)S(1)} %bitcast.14), channel_id=1, source_target_pairs={{0,3},{1,2},{2,1},{3,0},{4,7},{5,6},{6,5},{7,4},{8,11},{9,10},{10,... | collective-permute-start | bytes 196616 | tf_op jit(solution)/shard_map/ppermute | solution.py:234
  43.7 0.2 copy.13
  43.9 12.7 %collective-permute-done.1.refs_2_ = bf16[128,256]{1,0:T(8,128)(2,1)S(1)} collective-permute-done((bf16[128,256]{1,0:T(8,128)(2,1)S(1)}, bf16[128,256]{1,0:T(8,128)(2,1)S(1)}, u32[]{:S(2)}, u32[]{:S(2)}) %collective-permute-start.1) | collective-permute-done | bytes 65568 | tf_op jit(solution)/shard_map/ppermute | solution.py:234
  56.6 1.1 %forward_gates.1 = (f32[128,256]{1,0:T(8,128)S(1)}, f32[128,256]{1,0:T(8,128)S(1)}, f32[128,256]{1,0:T(8,128)S(1)}) custom-call(s32[2]{0:T(128)S(1)} %pad_add_fusion.index, s32[1]{0:T(128)S(6)} %copy.14.valid, bf16[1024,512]{1,0:T(8,128)(2,1)S(1)} %bitcast.10, f32[9,256]{1,0:T(8,128)S(1)} %convert_element_type.15.taps_ref, f32[1,256]{1,0:T(1,128)S(1)} %bitcast.16, ...), custom_call_target="tpu_custom_call" | custom-call | tf_op jit(solution)/shard_map/forward_gates/pallas_call | solution.py:180
  57.7 1.7 %backward_module.1 = (bf16[128,256]{1,0:T(8,128)(2,1)}, f32[128,256]{1,0:T(8,128)S(1)}, bf16[128,256]{1,0:T(8,128)(2,1)S(1)}, bf16[128,256]{1,0:T(8,128)(2,1)S(1)}, bf16[128,256]{1,0:T(8,128)(2,1)S(1)}) custom-call(s32[2]{0:T(128)S(1)} %pad_add_fusion.index, s32[1]{0:T(128)S(6)} %copy.14.valid, bf16[1024,512]{1,0:T(8,128)(2,1)S(1)} %bitcast.11, ...), custom_call_target="tpu_custom_call" | custom-call | tf_op jit(solution)/shard_map/backward_module/pallas_call | solution.py:221
  59.4 1.2 %collective-permute-start.10 = (bf16[128,256]{1,0:T(8,128)(2,1)S(1)}, bf16[128,256]{1,0:T(8,128)(2,1)S(1)}, u32[]{:S(2)}, u32[]{:S(2)}) collective-permute-start(bf16[128,256]{1,0:T(8,128)(2,1)S(1)} %get-tuple-element.31), channel_id=1, source_target_pairs={{0,1},{1,0},{2,3},{3,2},{4,5},{5,4},{6,7},{7,6},{8,9},{9,8},{10,11... | collective-permute-start | bytes 196616 | tf_op jit(solution)/shard_map/ppermute | solution.py:234
  60.7 1.8 %collective-permute-start.11 = (bf16[128,256]{1,0:T(8,128)(2,1)S(1)}, bf16[128,256]{1,0:T(8,128)(2,1)S(1)}, u32[]{:S(2)}, u32[]{:S(2)}) collective-permute-start(bf16[128,256]{1,0:T(8,128)(2,1)S(1)} %get-tuple-element.32), channel_id=1, source_target_pairs={{0,2},{1,3},{2,0},{3,1},{4,6},{5,7},{6,4},{7,5},{8,10},{9,11},{10,... | collective-permute-start | bytes 196616 | tf_op jit(solution)/shard_map/ppermute | solution.py:234
  62.5 1.4 %collective-permute-start.12 = (bf16[128,256]{1,0:T(8,128)(2,1)S(1)}, bf16[128,256]{1,0:T(8,128)(2,1)S(1)}, u32[]{:S(2)}, u32[]{:S(2)}) collective-permute-start(bf16[128,256]{1,0:T(8,128)(2,1)S(1)} %get-tuple-element.33), channel_id=1, source_target_pairs={{0,3},{1,2},{2,1},{3,0},{4,7},{5,6},{6,5},{7,4},{8,11},{9,10},{10,... | collective-permute-start | bytes 196616 | tf_op jit(solution)/shard_map/ppermute | solution.py:234
  63.8 2.9 %collective-permute-done.11 = bf16[128,256]{1,0:T(8,128)(2,1)S(1)} collective-permute-done((bf16[128,256]{1,0:T(8,128)(2,1)S(1)}, bf16[128,256]{1,0:T(8,128)(2,1)S(1)}, u32[]{:S(2)}, u32[]{:S(2)}) %collective-permute-start.11) | collective-permute-done | bytes 65568 | tf_op jit(solution)/shard_map/ppermute | solution.py:234
  66.8 1.8 %collective-permute-done.12 = bf16[128,256]{1,0:T(8,128)(2,1)S(1)} collective-permute-done((bf16[128,256]{1,0:T(8,128)(2,1)S(1)}, bf16[128,256]{1,0:T(8,128)(2,1)S(1)}, u32[]{:S(2)}, u32[]{:S(2)}) %collective-permute-start.12) | collective-permute-done | bytes 65568 | tf_op jit(solution)/shard_map/ppermute | solution.py:234
  68.5 0.7 fusion
  (24 shorter events, 0.1 us)
Async XLA Ops:
  0.7 2.5 %copy-start = (bf16[8,160,2048]{2,1,0:T(8,128)(2,1)S(1)}, bf16[8,160,2048]{2,1,0:T(8,128)(2,1)}, u32[]{:S(2)}) copy-start(bf16[8,160,2048]{2,1,0:T(8,128)(2,1)} %windows.3) | copy-start | bytes 15728644
  3.2 2.2 %copy-start.1 = (bf16[1024,2048]{1,0:T(8,128)(2,1)S(1)}, bf16[1024,2048]{1,0:T(8,128)(2,1)}, u32[]{:S(2)}) copy-start(bf16[1024,2048]{1,0:T(8,128)(2,1)} %weight.3) | copy-start | bytes 12582916
  5.4 0.7 copy-start.4
  6.0 0.7 copy-start.5
  11.8 10.2 %copy-start.3 = (bf16[1,128,256]{2,1,0:T(8,128)(2,1)S(1)}, bf16[1,128,256]{2,1,0:T(8,128)(2,1)}, u32[]{:S(2)}) copy-start(bf16[1,128,256]{2,1,0:T(8,128)(2,1)} %param.15) | copy-start | bytes 196612
  11.8 22.4 %copy-start.2 = (bf16[1024,1024]{1,0:T(8,128)(2,1)S(1)}, bf16[1024,1024]{1,0:T(8,128)(2,1)}, u32[]{:S(2)}) copy-start(bf16[1024,1024]{1,0:T(8,128)(2,1)} %project.1) | copy-start | bytes 6291460
  11.8 5.7 %collective-permute-start.3 = (bf16[4,128,1024]{2,1,0:T(8,128)(2,1)S(1)}, bf16[4,128,1024]{2,1,0:T(8,128)(2,1)S(1)}, u32[]{:S(2)}, u32[]{:S(2)}) collective-permute-start(bf16[4,128,1024]{2,1,0:T(8,128)(2,1)S(1)} %adapter_other.1), channel_id=1, source_target_pairs={{0,4},{4,0},{8,12},{12,8},{16,20},{20,16},{24,28},{28,24},{1,5},{5... | collective-permute-start | bytes 3145736 | tf_op jit(solution)/shard_map/ppermute | solution.py:234
  17.5 26.2 %copy-start.8 = (bf16[1024,2,256]{2,1,0:T(2,128)(2,1)S(1)}, bf16[1024,2,256]{2,1,0:T(2,128)(2,1)}, u32[]{:S(2)}) copy-start(bf16[1024,2,256]{2,1,0:T(2,128)(2,1)} %param.16) | copy-start | bytes 3145732
  17.5 26.4 %copy-start.9 = (bf16[9,256]{1,0:T(8,128)(2,1)S(1)}, bf16[9,256]{1,0:T(8,128)(2,1)}, u32[]{:S(2)}) copy-start(bf16[9,256]{1,0:T(8,128)(2,1)} %param.17) | copy-start | bytes 13828
  17.5 39.1 %copy-start.6 = (f32[256]{0:T(256)S(1)}, f32[256]{0:T(256)}, u32[]{:S(2)}) copy-start(f32[256]{0:T(256)} %param.18) | copy-start | bytes 3076
  17.5 39.1 %copy-start.7 = (f32[256]{0:T(256)S(1)}, f32[256]{0:T(256)}, u32[]{:S(2)}) copy-start(f32[256]{0:T(256)} %param.19) | copy-start | bytes 3076
  17.8 10.8 %collective-permute-start.4 = (bf16[128,1024]{1,0:T(8,128)(2,1)S(1)}, bf16[128,1024]{1,0:T(8,128)(2,1)S(1)}, u32[]{:S(2)}, u32[]{:S(2)}) collective-permute-start(bf16[128,1024]{1,0:T(8,128)(2,1)S(1)} %get-tuple-element.22), channel_id=1, source_target_pairs={{0,24},{4,28},{8,16},{12,20},{16,8},{20,12},{24,0},{28,4},{1,25},{... | collective-permute-start | bytes 786440 | tf_op jit(solution)/shard_map/ppermute | solution.py:234
  21.4 12.6 %collective-permute-start.5 = (bf16[128,1024]{1,0:T(8,128)(2,1)S(1)}, bf16[128,1024]{1,0:T(8,128)(2,1)S(1)}, u32[]{:S(2)}, u32[]{:S(2)}) collective-permute-start(bf16[128,1024]{1,0:T(8,128)(2,1)S(1)} %get-tuple-element.23), channel_id=1, source_target_pairs={{0,16},{4,20},{8,24},{12,28},{16,0},{20,4},{24,8},{28,12},{1,17},{... | collective-permute-start | bytes 786440 | tf_op jit(solution)/shard_map/ppermute | solution.py:234
  21.9 12.3 %collective-permute-start.6 = (bf16[128,1024]{1,0:T(8,128)(2,1)S(1)}, bf16[128,1024]{1,0:T(8,128)(2,1)S(1)}, u32[]{:S(2)}, u32[]{:S(2)}) collective-permute-start(bf16[128,1024]{1,0:T(8,128)(2,1)S(1)} %get-tuple-element.24), channel_id=1, source_target_pairs={{0,8},{4,12},{8,0},{12,4},{16,24},{20,28},{24,16},{28,20},{1,9},{5... | collective-permute-start | bytes 786440 | tf_op jit(solution)/shard_map/ppermute | solution.py:234
  22.0 19.8 %collective-permute-start = (bf16[128,256]{1,0:T(8,128)(2,1)S(1)}, bf16[128,256]{1,0:T(8,128)(2,1)S(1)}, u32[]{:S(2)}, u32[]{:S(2)}) collective-permute-start(bf16[128,256]{1,0:T(8,128)(2,1)S(1)} %bitcast.12), channel_id=1, source_target_pairs={{0,1},{1,0},{2,3},{3,2},{4,5},{5,4},{6,7},{7,6},{8,9},{9,8},{10,11... | collective-permute-start | bytes 196616 | tf_op jit(solution)/shard_map/ppermute | solution.py:234
  35.6 22.1 %collective-permute-start.7 = (bf16[128,512]{1,0:T(8,128)(2,1)S(1)}, bf16[128,512]{1,0:T(8,128)(2,1)S(1)}, u32[]{:S(2)}, u32[]{:S(2)}) collective-permute-start(bf16[128,512]{1,0:T(8,128)(2,1)S(1)} %get-tuple-element.26), channel_id=1, source_target_pairs={{0,1},{1,0},{2,3},{3,2},{4,5},{5,4},{6,7},{7,6},{8,9},{9,8},{10,11... | collective-permute-start | bytes 393224 | tf_op jit(solution)/shard_map/ppermute | solution.py:234
  37.3 20.5 %collective-permute-start.8 = (bf16[128,512]{1,0:T(8,128)(2,1)S(1)}, bf16[128,512]{1,0:T(8,128)(2,1)S(1)}, u32[]{:S(2)}, u32[]{:S(2)}) collective-permute-start(bf16[128,512]{1,0:T(8,128)(2,1)S(1)} %get-tuple-element.27), channel_id=1, source_target_pairs={{0,2},{1,3},{2,0},{3,1},{4,6},{5,7},{6,4},{7,5},{8,10},{9,11},{10,... | collective-permute-start | bytes 393224 | tf_op jit(solution)/shard_map/ppermute | solution.py:234
  39.9 17.9 %collective-permute-start.9 = (bf16[128,512]{1,0:T(8,128)(2,1)S(1)}, bf16[128,512]{1,0:T(8,128)(2,1)S(1)}, u32[]{:S(2)}, u32[]{:S(2)}) collective-permute-start(bf16[128,512]{1,0:T(8,128)(2,1)S(1)} %get-tuple-element.28), channel_id=1, source_target_pairs={{0,3},{1,2},{2,1},{3,0},{4,7},{5,6},{6,5},{7,4},{8,11},{9,10},{10,... | collective-permute-start | bytes 393224 | tf_op jit(solution)/shard_map/ppermute | solution.py:234
  40.1 16.5 %collective-permute-start.1 = (bf16[128,256]{1,0:T(8,128)(2,1)S(1)}, bf16[128,256]{1,0:T(8,128)(2,1)S(1)}, u32[]{:S(2)}, u32[]{:S(2)}) collective-permute-start(bf16[128,256]{1,0:T(8,128)(2,1)S(1)} %bitcast.13), channel_id=1, source_target_pairs={{0,2},{1,3},{2,0},{3,1},{4,6},{5,7},{6,4},{7,5},{8,10},{9,11},{10,... | collective-permute-start | bytes 196616 | tf_op jit(solution)/shard_map/ppermute | solution.py:234
  41.8 14.8 %collective-permute-start.2 = (bf16[128,256]{1,0:T(8,128)(2,1)S(1)}, bf16[128,256]{1,0:T(8,128)(2,1)S(1)}, u32[]{:S(2)}, u32[]{:S(2)}) collective-permute-start(bf16[128,256]{1,0:T(8,128)(2,1)S(1)} %bitcast.14), channel_id=1, source_target_pairs={{0,3},{1,2},{2,1},{3,0},{4,7},{5,6},{6,5},{7,4},{8,11},{9,10},{10,... | collective-permute-start | bytes 196616 | tf_op jit(solution)/shard_map/ppermute | solution.py:234
  59.4 4.4 %collective-permute-start.10 = (bf16[128,256]{1,0:T(8,128)(2,1)S(1)}, bf16[128,256]{1,0:T(8,128)(2,1)S(1)}, u32[]{:S(2)}, u32[]{:S(2)}) collective-permute-start(bf16[128,256]{1,0:T(8,128)(2,1)S(1)} %get-tuple-element.31), channel_id=1, source_target_pairs={{0,1},{1,0},{2,3},{3,2},{4,5},{5,4},{6,7},{7,6},{8,9},{9,8},{10,11... | collective-permute-start | bytes 196616 | tf_op jit(solution)/shard_map/ppermute | solution.py:234
  60.7 6.1 %collective-permute-start.11 = (bf16[128,256]{1,0:T(8,128)(2,1)S(1)}, bf16[128,256]{1,0:T(8,128)(2,1)S(1)}, u32[]{:S(2)}, u32[]{:S(2)}) collective-permute-start(bf16[128,256]{1,0:T(8,128)(2,1)S(1)} %get-tuple-element.32), channel_id=1, source_target_pairs={{0,2},{1,3},{2,0},{3,1},{4,6},{5,7},{6,4},{7,5},{8,10},{9,11},{10,... | collective-permute-start | bytes 196616 | tf_op jit(solution)/shard_map/ppermute | solution.py:234
  62.5 6.1 %collective-permute-start.12 = (bf16[128,256]{1,0:T(8,128)(2,1)S(1)}, bf16[128,256]{1,0:T(8,128)(2,1)S(1)}, u32[]{:S(2)}, u32[]{:S(2)}) collective-permute-start(bf16[128,256]{1,0:T(8,128)(2,1)S(1)} %get-tuple-element.33), channel_id=1, source_target_pairs={{0,3},{1,2},{2,1},{3,0},{4,7},{5,6},{6,5},{7,4},{8,11},{9,10},{10,... | collective-permute-start | bytes 196616 | tf_op jit(solution)/shard_map/ppermute | solution.py:234

commit v2 on v1

v2 whole, which is shorter than its diff:
```python
import functools

import jax
import jax.numpy as jnp
from jax import lax
from jax.experimental import pallas as pl
from jax.experimental.pallas import tpu as pltpu
from jax.sharding import PartitionSpec as P

F32 = jnp.float32
BF16 = jnp.bfloat16
NT = (((1,), (1,)), ((), ()))
NN = (((1,), (0,)), ((), ()))
ROW_TILE = 16
LANES = 128
COLS = 256
VMEM = pl.BlockSpec(memory_space=pltpu.VMEM)
SMEM = pl.BlockSpec(memory_space=pltpu.SMEM)
HBM = pl.BlockSpec(memory_space=pltpu.HBM)
HALVES = 2
OTHER_VMEM = 48
OWN_VMEM = 48


def dot(a, b, dims):
    return lax.dot_general(a, b, dims, preferred_element_type=F32)


def matmul_cost(rows, depth, columns):
    return pl.CostEstimate(
        flops=2 * rows * depth * columns,
        bytes_accessed=2 * (rows * depth + depth * columns + rows * columns),
        transcendentals=0,
    )


def picks_of(meta, flip, targets, last_start):
    dec = lax.axis_index("dec")
    picks = []
    for step in range(targets):
        target = ((dec // 2) ^ step) * 2 + ((dec % 2) ^ flip)
        found, first = jnp.int32(-1), jnp.int32(0)
        for roll in range(meta.shape[1]):
            hit = meta[0, roll] == target
            found = jnp.where(hit, roll, found)
            first = jnp.where(hit, meta[1, roll], first)
        start = jnp.minimum(first // ROW_TILE * ROW_TILE, last_start)
        picks.append((found, start, first - start))
    return picks


def multiply(slabs, rows, product):
    result = dot(slabs[...], rows[...], NT)
    for lane in range(COLS // LANES):
        product[lane, :, :] = result[:, lane * LANES : (lane + 1) * LANES]


def cut_rows(product, out, picks, chunk):
    targets, frames, _ = out.shape
    span = product.shape[1] // targets
    for step in range(targets):
        found, _, shift = picks[step]
        for lane in range(COLS // LANES):
            rows = product[lane, pl.ds(step * span + shift, frames), :]
            at = chunk * COLS + lane * LANES
            out[step, :, at : at + LANES] = jnp.where(found >= 0, rows, 0.0).astype(BF16)


def weight_copies(weight_hbm, head, tail, sem):
    return [
        pltpu.make_async_copy(
            weight_hbm.at[pl.ds(chunk * COLS, COLS), :],
            tail.at[pl.ds((chunk - 1) * COLS, COLS), :] if chunk else head,
            sem.at[chunk],
        )
        for chunk in range(weight_hbm.shape[0] // COLS)
    ]


def other_kernel(routes, windows, weight, out, own, head, meta, slabs, tail, *refs):
    products, (meta_sem, sem, weight_sem) = refs[:2], refs[2:]
    targets = out.shape[0]
    span = slabs.shape[0] // targets
    last_start = windows.shape[1] - span

    def slab_copies(flip, picks, held):
        return [
            pltpu.make_async_copy(
                windows.at[jnp.maximum(found, 0), pl.ds(pl.multiple_of(start, ROW_TILE), span), :],
                held.at[pl.ds(step * span, span), :],
                sem.at[flip, step],
            )
            for step, (found, start, _) in enumerate(picks)
        ]

    route_copy = pltpu.make_async_copy(routes, meta, meta_sem)
    weights = weight_copies(weight, head, tail, weight_sem)
    route_copy.start()
    weights[0].start()
    route_copy.wait()
    picks = picks_of(meta, 1, targets, last_start)
    copies = slab_copies(1, picks, slabs)
    own_copies = slab_copies(0, picks_of(meta, 0, targets, last_start), own)
    for copy in copies + weights[1:] + own_copies:
        copy.start()
    for copy in copies:
        copy.wait()
    for chunk, copy in enumerate(weights):
        copy.wait()
        multiply(slabs, tail.at[pl.ds((chunk - 1) * COLS, COLS), :] if chunk else head, products[chunk % 2])
        cut_rows(products[chunk % 2], out, picks, chunk)
    for copy in own_copies:
        copy.wait()


def adapter_other(frames, routes, windows, weight):
    _, _, d_local = windows.shape
    width = weight.shape[0]
    targets = lax.axis_size("dec") // 2
    span = frames + ROW_TILE
    return pl.pallas_call(
        other_kernel,
        out_shape=[
            jax.ShapeDtypeStruct((targets, frames, width), BF16),
            jax.ShapeDtypeStruct((targets * span, d_local), BF16),
            jax.ShapeDtypeStruct((COLS, d_local), BF16),
        ],
        in_specs=[HBM] * 3,
        out_specs=[VMEM] * 3,
        scratch_shapes=[
            pltpu.SMEM(routes.shape, jnp.int32),
            pltpu.VMEM((targets * span, d_local), BF16),
            pltpu.VMEM((width - COLS, d_local), BF16),
            pltpu.VMEM((COLS // LANES, targets * span, LANES), F32),
            pltpu.VMEM((COLS // LANES, targets * span, LANES), F32),
            pltpu.SemaphoreType.DMA,
            pltpu.SemaphoreType.DMA((2, targets)),
            pltpu.SemaphoreType.DMA((width // COLS,)),
        ],
        compiler_params=pltpu.CompilerParams(vmem_limit_bytes=OTHER_VMEM << 20),
        cost_estimate=matmul_cost(targets * span, d_local, width),
        name="adapter_other",
    )(routes, windows, weight)


def own_kernel(last_start, routes, slabs, head, weight, out, meta, tail, *refs):
    products, (meta_sem, weight_sem) = refs[:2], refs[2:]
    route_copy = pltpu.make_async_copy(routes, meta, meta_sem)
    weights = weight_copies(weight, head, tail, weight_sem)[1:]
    route_copy.start()
    for copy in weights:
        copy.start()
    multiply(slabs, head, products[0])
    route_copy.wait()
    picks = picks_of(meta, 0, out.shape[0], last_start)
    for chunk, copy in enumerate(weights):
        copy.wait()
        multiply(slabs, tail.at[pl.ds(chunk * COLS, COLS), :], products[(chunk + 1) % 2])
        cut_rows(products[chunk % 2], out, picks, chunk)
    cut_rows(products[len(weights) % 2], out, picks, len(weights))


def adapter_own(frames, seq_len, routes, slabs, head, weight):
    width, d_local = weight.shape
    targets = lax.axis_size("dec") // 2
    span = frames + ROW_TILE
    return pl.pallas_call(
        functools.partial(own_kernel, seq_len - span),
        out_shape=jax.ShapeDtypeStruct((targets, frames, width), BF16),
        in_specs=[HBM] + [VMEM] * 2 + [HBM],
        out_specs=VMEM,
        scratch_shapes=[
            pltpu.SMEM(routes.shape, jnp.int32),
            pltpu.VMEM((width - COLS, d_local), BF16),
            pltpu.VMEM((COLS // LANES, targets * span, LANES), F32),
            pltpu.VMEM((COLS // LANES, targets * span, LANES), F32),
            pltpu.SemaphoreType.DMA,
            pltpu.SemaphoreType.DMA((width // COLS,)),
        ],
        compiler_params=pltpu.CompilerParams(vmem_limit_bytes=OWN_VMEM << 20),
        cost_estimate=matmul_cost(targets * span, d_local, width),
        name="adapter_own",
    )(routes, slabs, head, weight)


def pair_sum_kernel(own, other, *outs):
    targets, frames, _ = own.shape
    size = frames // HALVES
    for at, out in enumerate(outs):
        half, step = divmod(at, targets)
        rows = pl.ds(half * size, size)
        out[...] = (own[step, rows, :].astype(F32) + other[step, rows, :].astype(F32)).astype(BF16)


def pair_sum(own, other):
    targets, frames, width = own.shape
    outs = pl.pallas_call(
        pair_sum_kernel,
        out_shape=[jax.ShapeDtypeStruct((frames // HALVES, width), BF16)] * (targets * HALVES),
        in_specs=[VMEM] * 2,
        out_specs=[VMEM] * (targets * HALVES),
        compiler_params=pltpu.CompilerParams(vmem_limit_bytes=24 << 20),
        name="pair_sum",
    )(own, other)
    return [outs[half * targets : (half + 1) * targets] for half in range(HALVES)]


def swish_kernel(parts, first, valid, project, *refs):
    blocks, outs, stream = refs[:parts], refs[parts:-1], refs[-1]
    frames, width = stream.shape
    c_local = outs[0].shape[1] // 2
    total = blocks[0][...].astype(F32)
    for block in blocks[1:]:
        total = total + block[...].astype(F32)
    rows = first + lax.broadcasted_iota(jnp.int32, (frames, width), 0)
    stream[...] = jnp.where(rows < valid[0], total, 0.0).astype(BF16)
    ch = lax.axis_index("ch")
    for step, out in enumerate(outs):
        at = pl.ds(pl.multiple_of((ch ^ step) * c_local, c_local), c_local)
        out[:, :c_local] = stream[:, at].astype(out.dtype)
        out[:, c_local:] = dot(stream[...], project[step], NN).astype(out.dtype)


def swish(first, valid, project, blocks):
    frames, width = blocks[0].shape
    groups, _, c_local = project.shape
    return pl.pallas_call(
        functools.partial(swish_kernel, len(blocks), first),
        out_shape=[jax.ShapeDtypeStruct((frames, 2 * c_local), F32 if step == 0 else BF16) for step in range(groups)],
        in_specs=[SMEM, VMEM] + [VMEM] * len(blocks),
        out_specs=[VMEM] * groups,
        scratch_shapes=[pltpu.VMEM((frames, width), BF16)],
        compiler_params=pltpu.CompilerParams(vmem_limit_bytes=24 << 20),
        cost_estimate=matmul_cost(frames, width, width),
        name="stream_and_swish",
    )(valid, project, *blocks)


def spread_rows(padded, rows):
    frames, c_local = rows.shape
    edge = (padded.shape[0] - frames) // 2
    padded[:edge, :] = jnp.zeros((edge, c_local), F32)
    padded[edge + frames :, :] = jnp.zeros((edge, c_local), F32)
    padded[pl.ds(edge, frames), :] = rows


def edge_of(taps):
    return -(-((taps - 1) // 2) // 8) * 8


def forward_kernel(parts, valid, expand, project, taps_ref, scale, shift, *refs):
    blocks, (value_out, gate_out, slope_out, project_t, expand_t, padded) = refs[:parts], refs[parts:]
    frames, c_local = value_out.shape
    taps = taps_ref.shape[0]
    half = (taps - 1) // 2
    edge = (padded.shape[0] - frames) // 2
    ch = lax.axis_index("ch")
    expanded = jnp.zeros((frames, 2 * c_local), F32)
    for step, block in enumerate(blocks):
        at = pl.ds(pl.multiple_of((ch ^ step) * c_local, c_local), c_local)
        expanded = expanded + dot(block[...], expand[at, :], NN)
        project_t[step, :, :] = project[at, :].T
        expand_t[step, :, :] = expand[at, :].T
    value = expanded[:, :c_local]
    gate = jax.nn.sigmoid(expanded[:, c_local:])
    rows = lax.broadcasted_iota(jnp.int32, (frames, c_local), 0)
    spread_rows(padded, jnp.where(rows < valid[0], value * gate, 0.0))
    depth = jnp.zeros((frames, c_local), F32)
    for tap in range(taps):
        depth = depth + taps_ref[tap : tap + 1, :] * padded[pl.ds(edge - half + tap, frames), :]
    shifted = depth * scale[...] + shift[...]
    sig = jax.nn.sigmoid(shifted)
    value_out[...] = value
    gate_out[...] = gate
    slope_out[...] = sig * (1.0 + shifted * (1.0 - sig)) * scale[...]


def forward(valid, expand, project, taps, scale, shift, blocks):
    frames, c_local = blocks[0].shape
    groups, width = len(blocks), project.shape[1]
    return pl.pallas_call(
        functools.partial(forward_kernel, groups),
        out_shape=[jax.ShapeDtypeStruct((frames, c_local), F32)] * 3
        + [jax.ShapeDtypeStruct((groups, width, c_local), BF16), jax.ShapeDtypeStruct((groups, 2 * c_local, c_local), BF16)],
        in_specs=[SMEM] + [VMEM] * (5 + groups),
        out_specs=[VMEM] * 5,
        scratch_shapes=[pltpu.VMEM((frames + 2 * edge_of(taps.shape[0]), c_local), F32)],
        compiler_params=pltpu.CompilerParams(vmem_limit_bytes=24 << 20),
        cost_estimate=matmul_cost(frames, 4 * width, 2 * c_local),
        name="forward_gates",
    )(valid, expand, project, taps, scale, shift, *blocks)


def backward_kernel(parts, valid, expand_t, taps_ref, value_ref, gate_ref, slope, *refs):
    blocks, stream_out, outs, padded = refs[: parts * HALVES], refs[parts * HALVES], refs[parts * HALVES + 1 : -1], refs[-1]
    frames, c_local = stream_out.shape
    size = frames // HALVES
    taps = taps_ref.shape[0]
    half = (taps - 1) // 2
    edge = (padded.shape[0] - frames) // 2
    spread_rows(padded, jnp.zeros((frames, c_local), F32))
    for at in range(HALVES):
        total = blocks[at * parts][...].astype(F32)
        for block in blocks[at * parts + 1 : (at + 1) * parts]:
            total = total + block[...].astype(F32)
        rows = pl.ds(at * size, size)
        stream_out[rows, :] = total[:, :c_local].astype(BF16)
        padded[pl.ds(edge + at * size, size), :] = total[:, c_local:] * slope[rows, :]
    grad = jnp.zeros((frames, c_local), F32)
    for tap in range(taps):
        grad = grad + taps_ref[tap : tap + 1, :] * padded[pl.ds(edge + half - tap, frames), :]
    rows = lax.broadcasted_iota(jnp.int32, (frames, c_local), 0)
    grad = jnp.where(rows < valid[0], grad, 0.0)
    gate = gate_ref[...]
    grad_value = grad * gate
    grad_gate = grad_value * value_ref[...] * (1.0 - gate)
    grad_expanded = jnp.concatenate([grad_value.astype(BF16), grad_gate.astype(BF16)], axis=1)
    for step, out in enumerate(outs):
        out[...] = dot(grad_expanded, expand_t[step], NN).astype(out.dtype)


def backward(valid, expand_t, taps, value, gate, slope, halves):
    frames, c_local = value.shape
    groups = expand_t.shape[0]
    return pl.pallas_call(
        functools.partial(backward_kernel, groups),
        out_shape=[jax.ShapeDtypeStruct((frames, c_local), BF16)]
        + [jax.ShapeDtypeStruct((frames, c_local), F32 if step == 0 else BF16) for step in range(groups)],
        in_specs=[SMEM] + [VMEM] * (5 + groups * HALVES),
        out_specs=[VMEM] * (1 + groups),
        scratch_shapes=[pltpu.VMEM((frames + 2 * edge_of(taps.shape[0]), c_local), F32)],
        compiler_params=pltpu.CompilerParams(vmem_limit_bytes=16 << 20),
        cost_estimate=matmul_cost(frames, 2 * c_local, c_local * groups),
        name="backward_module",
    )(valid, expand_t, taps, value, gate, slope, *[block for half in halves for block in half])


def swap(block, axis, count, mask):
    return lax.ppermute(block, axis, [(i, i ^ mask) for i in range(count)])


def body(
    n_dec,
    n_ch,
    frame_cotangent,
    rollout_utterance,
    frame_offset,
    utterance_frames,
    normed_input,
    expand_weight,
    depth_kernel,
    norm_scale,
    norm_shift,
    project_weight,
    adapter_weight,
):
    u_local, frames, c_local = normed_input.shape
    width = expand_weight.shape[0]
    chips = n_dec // 2
    own_input = normed_input.reshape(frames, c_local)
    inputs = [own_input] + [swap(own_input, "ch", n_ch, step) for step in range(1, n_ch)]
    expand = expand_weight.reshape(width, 2 * c_local)
    taps = depth_kernel.astype(F32)
    scale, shift = norm_scale.reshape(1, c_local), norm_shift.reshape(1, c_local)

    seq_len = frame_cotangent.shape[1]
    routes = jnp.stack([rollout_utterance, frame_offset])
    for_other, own_slabs, head = adapter_other(frames, routes, frame_cotangent, adapter_weight)
    from_other = swap(for_other, "dec", n_dec, 1)
    own = adapter_own(frames, seq_len, routes, own_slabs, head, adapter_weight)
    own, inputs = lax.optimization_barrier((own, inputs))
    sums = pair_sum(own, from_other)
    arrived = [
        [half[0]] + [swap(half[step], "dec", n_dec, 2 * step) for step in reversed(range(1, chips))] for half in sums
    ]
    value, gate, slope, project_t, expand_t = forward(
        utterance_frames, expand, project_weight, taps, scale, shift, inputs
    )
    halves = []
    for at, half in enumerate(arrived):
        sent = swish(at * frames // HALVES, utterance_frames, project_t, half)
        halves.append([sent[0]] + [swap(sent[step], "ch", n_ch, step) for step in range(1, n_ch)])
    stream, *parts = backward(utterance_frames, expand_t, taps, value, gate, slope, halves)
    total = parts[0]
    for step in range(1, n_ch):
        total = total + swap(parts[step], "ch", n_ch, step).astype(F32)
    return stream[None], total.astype(BF16)[None]


def solution(mesh):
    return jax.shard_map(
        functools.partial(body, mesh.shape["dec"], mesh.shape["ch"]),
        mesh=mesh,
        in_specs=(
            P("dec", None, "ch"),
            P("dec"),
            P("dec"),
            P("dec"),
            P("dec", None, "ch"),
            P(None, None, "ch"),
            P(None, "ch"),
            P("ch"),
            P("ch"),
            P(),
            P(None, "ch"),
        ),
        out_specs=(P("dec", None, "ch"), P("dec", None, "ch")),
        check_vma=False,
    )
```

time: 69.4 us -> 58.5 us (0.84)
  waiting for transfers between devices: 26.9 us -> 8.91 us
  starting transfers between devices: 19.1 us -> 28.9 us
  local copies, waits for them, and re-layouts: 6.25 us -> 0.25 us
  Pallas kernels: 14.7 us -> 17.4 us
    ppermute x13 -> x19, waiting for transfers between devices: 26.9 us -> 8.91 us  [swap(): return lax.ppermute(block, axis, [(i, i ^ mask) for i in range(count)])]
    ppermute x13 -> x19, starting transfers between devices: 19.1 us -> 28.9 us  [swap(): return lax.ppermute(block, axis, [(i, i ^ mask) for i in range(count)])]
    unnamed x21 -> x13, local copies, waits for them, and re-layouts: 6.25 us -> 0.25 us
    pallas_call x6 -> x7, Pallas kernels: 14.7 us -> 17.4 us  [the longest x1 8.25 us: adapter_other(): pl.pallas_call(other_kernel, out_shape=[jax.ShapeDtypeStruct((targets, fr...]
  transfers between devices with their start and end apart: 13 -> 19, of which waited for: 6 -> 6; matrix products, arithmetic and copies ran while one was open for 0% -> 0% of each run, Pallas kernels for 11% -> 14%
where the time goes in v2:
time: 58.5 us; the launch traced here: 58.3 us
  starting transfers between devices  28.9 us (49%)
  Pallas kernels  17.4 us (30%)
  waiting for transfers between devices  8.91 us (15%)
  between operations  1.47 us (3%)
  other arithmetic  1.35 us (2%)
    ppermute x19, starting transfers between devices, swap(): return lax.ppermute(block, axis, [(i, i ^ mask) for i in range(count)])  28.9 us
    ppermute x19, waiting for transfers between devices, swap(): return lax.ppermute(block, axis, [(i, i ^ mask) for i in range(count)])  8.91 us
    pallas_call x1, Pallas kernels, adapter_other(): pl.pallas_call(other_kernel, out_shape=[jax.ShapeDtypeStruct((targets, fr...  8.25 us
    pallas_call x1, Pallas kernels, adapter_own(): pl.pallas_call(functools.partial(own_kernel, seq_len - span), out_shape=j...  5.84 us
  transfers between devices with their start and end apart: 19, of which 6 were waited for; matrix products, arithmetic and copies ran while one was open for 0% of the time, Pallas kernels for 14%

profile of v2, /device:TPU:0, one launch (start us, length us, event | category | flops | bytes accessed | tf_op | source)
XLA Modules:
  0.0 58.3 jit_solution(5902792782589824741)
XLA Ops:
  0.6 0.7 %pad_add_fusion.routes = s32[2,8]{1,0:T(2,128)S(1)} fusion(s32[1,8]{1,0:T(1,128)} %bitcast.18, s32[1,8]{1,0:T(1,128)} %bitcast.19), kind=kLoop, calls=%fused_computation.2 | loop fusion | flops 16 | bytes 128 | tf_op jit(solution)/shard_map/stack | solution.py:367
  1.3 8.2 %adapter_other.1 = (bf16[4,128,1024]{2,1,0:T(8,128)(2,1)S(1)}, bf16[576,2048]{1,0:T(8,128)(2,1)S(1)}, bf16[256,2048]{1,0:T(8,128)(2,1)S(1)}) custom-call(s32[2,8]{1,0:T(2,128)S(1)} %pad_add_fusion.routes, bf16[8,160,2048]{2,1,0:T(8,128)(2,1)} %windows.1, bf16[1024,2048]{1,0:T(8,128)(2,1)} %weight.3), custom_call_target="tpu_custom_call" | custom-call | flops 2415919104 | bytes 7733248 | tf_op jit(solution)/shard_map/adapter_other/pallas_call | solution.py:121
  9.6 0.5 collective-permute-start.3
  10.1 4.7 %collective-permute-start.2 = (bf16[128,256]{1,0:T(8,128)(2,1)S(1)}, bf16[128,256]{1,0:T(8,128)(2,1)S(1)}, u32[]{:S(2)}, u32[]{:S(2)}) collective-permute-start(bf16[128,256]{1,0:T(8,128)(2,1)S(1)} %bitcast.11), channel_id=1, source_target_pairs={{0,3},{1,2},{2,1},{3,0},{4,7},{5,6},{6,5},{7,4},{8,11},{9,10},{10,... | collective-permute-start | bytes 196616 | tf_op jit(solution)/shard_map/ppermute | solution.py:339
  14.8 0.6 %collective-permute-start = (bf16[128,256]{1,0:T(8,128)(2,1)S(1)}, bf16[128,256]{1,0:T(8,128)(2,1)S(1)}, u32[]{:S(2)}, u32[]{:S(2)}) collective-permute-start(bf16[128,256]{1,0:T(8,128)(2,1)S(1)} %bitcast.13), channel_id=1, source_target_pairs={{0,1},{1,0},{2,3},{3,2},{4,5},{5,4},{6,7},{7,6},{8,9},{9,8},{10,11... | collective-permute-start | bytes 196616 | tf_op jit(solution)/shard_map/ppermute | solution.py:339
  15.4 5.8 %adapter_own.1.own = bf16[4,128,1024]{2,1,0:T(8,128)(2,1)S(1)} custom-call(s32[2,8]{1,0:T(2,128)S(1)} %pad_add_fusion.routes, bf16[576,2048]{1,0:T(8,128)(2,1)S(1)} %get-tuple-element.36.slabs, bf16[256,2048]{1,0:T(8,128)(2,1)S(1)} %get-tuple-element.37.head, bf16[1024,2048]{1,0:T(8,128)(2,1)} %weight.3), custom_call_target="tpu_custom_call" | custom-call | flops 2415919104 | bytes 7733248 | tf_op jit(solution)/shard_map/adapter_own/pallas_call | solution.py:167
  21.3 0.2 pair_sum.1
  21.6 2.6 %collective-permute-start.10 = (bf16[64,1024]{1,0:T(8,128)(2,1)S(1)}, bf16[64,1024]{1,0:T(8,128)(2,1)S(1)}, u32[]{:S(2)}, u32[]{:S(2)}) collective-permute-start(bf16[64,1024]{1,0:T(8,128)(2,1)S(1)} %get-tuple-element.58), channel_id=1, source_target_pairs={{0,24},{4,28},{8,16},{12,20},{16,8},{20,12},{24,0},{28,4},{1,25},{... | collective-permute-start | bytes 393224 | tf_op jit(solution)/shard_map/ppermute | solution.py:339
  24.2 0.5 collective-permute-start.11
  24.8 0.4 collective-permute-start.12
  25.1 2.6 %collective-permute-start.4 = (bf16[64,1024]{1,0:T(8,128)(2,1)S(1)}, bf16[64,1024]{1,0:T(8,128)(2,1)S(1)}, u32[]{:S(2)}, u32[]{:S(2)}) collective-permute-start(bf16[64,1024]{1,0:T(8,128)(2,1)S(1)} %get-tuple-element.50), channel_id=1, source_target_pairs={{0,24},{4,28},{8,16},{12,20},{16,8},{20,12},{24,0},{28,4},{1,25},{... | collective-permute-start | bytes 393224 | tf_op jit(solution)/shard_map/ppermute | solution.py:339
  27.7 0.5 collective-permute-start.5
  28.2 2.3 %collective-permute-start.6 = (bf16[64,1024]{1,0:T(8,128)(2,1)S(1)}, bf16[64,1024]{1,0:T(8,128)(2,1)S(1)}, u32[]{:S(2)}, u32[]{:S(2)}) collective-permute-start(bf16[64,1024]{1,0:T(8,128)(2,1)S(1)} %get-tuple-element.52), channel_id=1, source_target_pairs={{0,8},{4,12},{8,0},{12,4},{16,24},{20,28},{24,16},{28,20},{1,9},{5... | collective-permute-start | bytes 393224 | tf_op jit(solution)/shard_map/ppermute | solution.py:339
  31.2 0.2 copy.13
  31.5 1.1 %forward_gates.1 = (f32[128,256]{1,0:T(8,128)S(1)}, f32[128,256]{1,0:T(8,128)S(1)}, f32[128,256]{1,0:T(8,128)S(1)}, bf16[4,1024,256]{2,1,0:T(8,128)(2,1)S(1)}, bf16[4,512,256]{2,1,0:T(8,128)(2,1)S(1)}) custom-call(s32[1]{0:T(128)S(6)} %copy.14.valid, bf16[1024,512]{1,0:T(8,128)(2,1)S(1)} %bitcast.10, bf16[1024,1024]{1,0:T(8,128)(2,1)S(1)} %copy-done, ...), custom_call_target="tpu_custom_call" | custom-call | flops 536870912 | bytes 5373952 | tf_op jit(solution)/shard_map/forward_gates/pallas_call | solution.py:281
  32.6 0.5 stream_and_swish.3
  33.1 1.3 %collective-permute-start.13 = (bf16[64,512]{1,0:T(8,128)(2,1)S(1)}, bf16[64,512]{1,0:T(8,128)(2,1)S(1)}, u32[]{:S(2)}, u32[]{:S(2)}) collective-permute-start(bf16[64,512]{1,0:T(8,128)(2,1)S(1)} %get-tuple-element.62), channel_id=1, source_target_pairs={{0,1},{1,0},{2,3},{3,2},{4,5},{5,4},{6,7},{7,6},{8,9},{9,8},{10,11... | collective-permute-start | bytes 196616 | tf_op jit(solution)/shard_map/ppermute | solution.py:339
  34.4 2.9 %collective-permute-start.14 = (bf16[64,512]{1,0:T(8,128)(2,1)S(1)}, bf16[64,512]{1,0:T(8,128)(2,1)S(1)}, u32[]{:S(2)}, u32[]{:S(2)}) collective-permute-start(bf16[64,512]{1,0:T(8,128)(2,1)S(1)} %get-tuple-element.63), channel_id=1, source_target_pairs={{0,2},{1,3},{2,0},{3,1},{4,6},{5,7},{6,4},{7,5},{8,10},{9,11},{10,... | collective-permute-start | bytes 196616 | tf_op jit(solution)/shard_map/ppermute | solution.py:339
  37.3 1.1 %collective-permute-start.15 = (bf16[64,512]{1,0:T(8,128)(2,1)S(1)}, bf16[64,512]{1,0:T(8,128)(2,1)S(1)}, u32[]{:S(2)}, u32[]{:S(2)}) collective-permute-start(bf16[64,512]{1,0:T(8,128)(2,1)S(1)} %get-tuple-element.64), channel_id=1, source_target_pairs={{0,3},{1,2},{2,1},{3,0},{4,7},{5,6},{6,5},{7,4},{8,11},{9,10},{10,... | collective-permute-start | bytes 196616 | tf_op jit(solution)/shard_map/ppermute | solution.py:339
  38.4 0.5 stream_and_swish.2
  38.9 3.3 %collective-permute-start.8 = (bf16[64,512]{1,0:T(8,128)(2,1)S(1)}, bf16[64,512]{1,0:T(8,128)(2,1)S(1)}, u32[]{:S(2)}, u32[]{:S(2)}) collective-permute-start(bf16[64,512]{1,0:T(8,128)(2,1)S(1)} %get-tuple-element.55), channel_id=1, source_target_pairs={{0,2},{1,3},{2,0},{3,1},{4,6},{5,7},{6,4},{7,5},{8,10},{9,11},{10,... | collective-permute-start | bytes 196616 | tf_op jit(solution)/shard_map/ppermute | solution.py:339
  42.2 1.1 %collective-permute-start.9 = (bf16[64,512]{1,0:T(8,128)(2,1)S(1)}, bf16[64,512]{1,0:T(8,128)(2,1)S(1)}, u32[]{:S(2)}, u32[]{:S(2)}) collective-permute-start(bf16[64,512]{1,0:T(8,128)(2,1)S(1)} %get-tuple-element.56), channel_id=1, source_target_pairs={{0,3},{1,2},{2,1},{3,0},{4,7},{5,6},{6,5},{7,4},{8,11},{9,10},{10,... | collective-permute-start | bytes 196616 | tf_op jit(solution)/shard_map/ppermute | solution.py:339
  43.3 0.2 collective-permute-done.15.refs_7_
  43.5 1.5 %collective-permute-done.7.refs_1_ = bf16[64,512]{1,0:T(8,128)(2,1)S(1)} collective-permute-done((bf16[64,512]{1,0:T(8,128)(2,1)S(1)}, bf16[64,512]{1,0:T(8,128)(2,1)S(1)}, u32[]{:S(2)}, u32[]{:S(2)}) %collective-permute-start.7) | collective-permute-done | bytes 65568 | tf_op jit(solution)/shard_map/ppermute | solution.py:339
  45.0 1.7 %collective-permute-done.8.refs_2_ = bf16[64,512]{1,0:T(8,128)(2,1)S(1)} collective-permute-done((bf16[64,512]{1,0:T(8,128)(2,1)S(1)}, bf16[64,512]{1,0:T(8,128)(2,1)S(1)}, u32[]{:S(2)}, u32[]{:S(2)}) %collective-permute-start.8) | collective-permute-done | bytes 65568 | tf_op jit(solution)/shard_map/ppermute | solution.py:339
  46.7 1.6 %collective-permute-done.9.refs_3_ = bf16[64,512]{1,0:T(8,128)(2,1)S(1)} collective-permute-done((bf16[64,512]{1,0:T(8,128)(2,1)S(1)}, bf16[64,512]{1,0:T(8,128)(2,1)S(1)}, u32[]{:S(2)}, u32[]{:S(2)}) %collective-permute-start.9) | collective-permute-done | bytes 65568 | tf_op jit(solution)/shard_map/ppermute | solution.py:339
  48.3 1.1 %backward_module.1 = (bf16[128,256]{1,0:T(8,128)(2,1)}, f32[128,256]{1,0:T(8,128)S(1)}, bf16[128,256]{1,0:T(8,128)(2,1)S(1)}, bf16[128,256]{1,0:T(8,128)(2,1)S(1)}, bf16[128,256]{1,0:T(8,128)(2,1)S(1)}) custom-call(s32[1]{0:T(128)S(6)} %copy.14.valid, bf16[4,512,256]{2,1,0:T(8,128)(2,1)S(1)} %get-tuple-element.42.expand_t, ...), custom_call_target="tpu_custom_call" | custom-call | flops 134217728 | bytes 1441792 | tf_op jit(solution)/shard_map/backward_module/pallas_call | solution.py:325
  49.4 2.1 %collective-permute-start.17 = (bf16[128,256]{1,0:T(8,128)(2,1)S(1)}, bf16[128,256]{1,0:T(8,128)(2,1)S(1)}, u32[]{:S(2)}, u32[]{:S(2)}) collective-permute-start(bf16[128,256]{1,0:T(8,128)(2,1)S(1)} %get-tuple-element.68), channel_id=1, source_target_pairs={{0,2},{1,3},{2,0},{3,1},{4,6},{5,7},{6,4},{7,5},{8,10},{9,11},{10,... | collective-permute-start | bytes 196616 | tf_op jit(solution)/shard_map/ppermute | solution.py:339
  51.5 2.3 %collective-permute-start.18 = (bf16[128,256]{1,0:T(8,128)(2,1)S(1)}, bf16[128,256]{1,0:T(8,128)(2,1)S(1)}, u32[]{:S(2)}, u32[]{:S(2)}) collective-permute-start(bf16[128,256]{1,0:T(8,128)(2,1)S(1)} %get-tuple-element.69), channel_id=1, source_target_pairs={{0,3},{1,2},{2,1},{3,0},{4,7},{5,6},{6,5},{7,4},{8,11},{9,10},{10,... | collective-permute-start | bytes 196616 | tf_op jit(solution)/shard_map/ppermute | solution.py:339
  53.8 3.0 %collective-permute-done.17 = bf16[128,256]{1,0:T(8,128)(2,1)S(1)} collective-permute-done((bf16[128,256]{1,0:T(8,128)(2,1)S(1)}, bf16[128,256]{1,0:T(8,128)(2,1)S(1)}, u32[]{:S(2)}, u32[]{:S(2)}) %collective-permute-start.17) | collective-permute-done | bytes 65568 | tf_op jit(solution)/shard_map/ppermute | solution.py:339
  56.8 0.9 %collective-permute-done.18 = bf16[128,256]{1,0:T(8,128)(2,1)S(1)} collective-permute-done((bf16[128,256]{1,0:T(8,128)(2,1)S(1)}, bf16[128,256]{1,0:T(8,128)(2,1)S(1)}, u32[]{:S(2)}, u32[]{:S(2)}) %collective-permute-start.18) | collective-permute-done | bytes 65568 | tf_op jit(solution)/shard_map/ppermute | solution.py:339
  57.6 0.7 %fusion = bf16[1,128,256]{2,1,0:T(8,128)(2,1)} fusion(bf16[128,256]{1,0:T(8,128)(2,1)S(1)} %collective-permute-done.18, bf16[128,256]{1,0:T(8,128)(2,1)S(1)} %collective-permute-done.17, f32[128,256]{1,0:T(8,128)S(1)} %get-tuple-element.66, bf16[128,256]{1,0:T(8,128)(2,1)S(1)} %collective-permute-done.16), kind=kLoop, calls=%fused_computation.1 | loop fusion | flops 229376 | bytes 393216 | tf_op jit(solution)/shard_map/broadcast_in_dim | solution.py:387
  (29 shorter events, 0.1 us)
Async XLA Ops:
  1.3 8.8 %copy-start.1 = (bf16[1,128,256]{2,1,0:T(8,128)(2,1)S(1)}, bf16[1,128,256]{2,1,0:T(8,128)(2,1)}, u32[]{:S(2)}) copy-start(bf16[1,128,256]{2,1,0:T(8,128)(2,1)} %param.15) | copy-start | bytes 196612
  9.6 11.8 %collective-permute-start.3 = (bf16[4,128,1024]{2,1,0:T(8,128)(2,1)S(1)}, bf16[4,128,1024]{2,1,0:T(8,128)(2,1)S(1)}, u32[]{:S(2)}, u32[]{:S(2)}) collective-permute-start(bf16[4,128,1024]{2,1,0:T(8,128)(2,1)S(1)} %get-tuple-element.48), channel_id=1, source_target_pairs={{0,4},{4,0},{8,12},{12,8},{16,20},{20,16},{24,28},{28,24},{1,5},{5... | collective-permute-start | bytes 3145736 | tf_op jit(solution)/shard_map/ppermute | solution.py:339
  10.1 11.2 %collective-permute-start.2 = (bf16[128,256]{1,0:T(8,128)(2,1)S(1)}, bf16[128,256]{1,0:T(8,128)(2,1)S(1)}, u32[]{:S(2)}, u32[]{:S(2)}) collective-permute-start(bf16[128,256]{1,0:T(8,128)(2,1)S(1)} %bitcast.11), channel_id=1, source_target_pairs={{0,3},{1,2},{2,1},{3,0},{4,7},{5,6},{6,5},{7,4},{8,11},{9,10},{10,... | collective-permute-start | bytes 196616 | tf_op jit(solution)/shard_map/ppermute | solution.py:339
  14.8 6.5 %collective-permute-start.1 = (bf16[128,256]{1,0:T(8,128)(2,1)S(1)}, bf16[128,256]{1,0:T(8,128)(2,1)S(1)}, u32[]{:S(2)}, u32[]{:S(2)}) collective-permute-start(bf16[128,256]{1,0:T(8,128)(2,1)S(1)} %bitcast.12), channel_id=1, source_target_pairs={{0,2},{1,3},{2,0},{3,1},{4,6},{5,7},{6,4},{7,5},{8,10},{9,11},{10,... | collective-permute-start | bytes 196616 | tf_op jit(solution)/shard_map/ppermute | solution.py:339
  14.8 6.5 %collective-permute-start = (bf16[128,256]{1,0:T(8,128)(2,1)S(1)}, bf16[128,256]{1,0:T(8,128)(2,1)S(1)}, u32[]{:S(2)}, u32[]{:S(2)}) collective-permute-start(bf16[128,256]{1,0:T(8,128)(2,1)S(1)} %bitcast.13), channel_id=1, source_target_pairs={{0,1},{1,0},{2,3},{3,2},{4,5},{5,4},{6,7},{7,6},{8,9},{9,8},{10,11... | collective-permute-start | bytes 196616 | tf_op jit(solution)/shard_map/ppermute | solution.py:339
  15.4 15.8 %copy-start.5 = (bf16[9,256]{1,0:T(8,128)(2,1)S(1)}, bf16[9,256]{1,0:T(8,128)(2,1)}, u32[]{:S(2)}) copy-start(bf16[9,256]{1,0:T(8,128)(2,1)} %param.17) | copy-start | bytes 13828
  15.4 15.8 %copy-start.4 = (bf16[1024,2,256]{2,1,0:T(2,128)(2,1)S(1)}, bf16[1024,2,256]{2,1,0:T(2,128)(2,1)}, u32[]{:S(2)}) copy-start(bf16[1024,2,256]{2,1,0:T(2,128)(2,1)} %param.16) | copy-start | bytes 3145732
  21.3 10.2 %copy-start = (bf16[1024,1024]{1,0:T(8,128)(2,1)S(1)}, bf16[1024,1024]{1,0:T(8,128)(2,1)}, u32[]{:S(2)}) copy-start(bf16[1024,1024]{1,0:T(8,128)(2,1)} %project.1) | copy-start | bytes 6291460
  21.3 10.2 %copy-start.2 = (f32[256]{0:T(256)S(1)}, f32[256]{0:T(256)}, u32[]{:S(2)}) copy-start(f32[256]{0:T(256)} %param.18) | copy-start | bytes 3076
  21.3 10.2 %copy-start.3 = (f32[256]{0:T(256)S(1)}, f32[256]{0:T(256)}, u32[]{:S(2)}) copy-start(f32[256]{0:T(256)} %param.19) | copy-start | bytes 3076
  21.6 6.7 %collective-permute-start.10 = (bf16[64,1024]{1,0:T(8,128)(2,1)S(1)}, bf16[64,1024]{1,0:T(8,128)(2,1)S(1)}, u32[]{:S(2)}, u32[]{:S(2)}) collective-permute-start(bf16[64,1024]{1,0:T(8,128)(2,1)S(1)} %get-tuple-element.58), channel_id=1, source_target_pairs={{0,24},{4,28},{8,16},{12,20},{16,8},{20,12},{24,0},{28,4},{1,25},{... | collective-permute-start | bytes 393224 | tf_op jit(solution)/shard_map/ppermute | solution.py:339
  24.2 8.3 %collective-permute-start.11 = (bf16[64,1024]{1,0:T(8,128)(2,1)S(1)}, bf16[64,1024]{1,0:T(8,128)(2,1)S(1)}, u32[]{:S(2)}, u32[]{:S(2)}) collective-permute-start(bf16[64,1024]{1,0:T(8,128)(2,1)S(1)} %get-tuple-element.59), channel_id=1, source_target_pairs={{0,16},{4,20},{8,24},{12,28},{16,0},{20,4},{24,8},{28,12},{1,17},{... | collective-permute-start | bytes 393224 | tf_op jit(solution)/shard_map/ppermute | solution.py:339
  24.8 7.8 %collective-permute-start.12 = (bf16[64,1024]{1,0:T(8,128)(2,1)S(1)}, bf16[64,1024]{1,0:T(8,128)(2,1)S(1)}, u32[]{:S(2)}, u32[]{:S(2)}) collective-permute-start(bf16[64,1024]{1,0:T(8,128)(2,1)S(1)} %get-tuple-element.60), channel_id=1, source_target_pairs={{0,8},{4,12},{8,0},{12,4},{16,24},{20,28},{24,16},{28,20},{1,9},{5... | collective-permute-start | bytes 393224 | tf_op jit(solution)/shard_map/ppermute | solution.py:339
  25.1 12.1 %collective-permute-start.4 = (bf16[64,1024]{1,0:T(8,128)(2,1)S(1)}, bf16[64,1024]{1,0:T(8,128)(2,1)S(1)}, u32[]{:S(2)}, u32[]{:S(2)}) collective-permute-start(bf16[64,1024]{1,0:T(8,128)(2,1)S(1)} %get-tuple-element.50), channel_id=1, source_target_pairs={{0,24},{4,28},{8,16},{12,20},{16,8},{20,12},{24,0},{28,4},{1,25},{... | collective-permute-start | bytes 393224 | tf_op jit(solution)/shard_map/ppermute | solution.py:339
  27.7 10.6 %collective-permute-start.5 = (bf16[64,1024]{1,0:T(8,128)(2,1)S(1)}, bf16[64,1024]{1,0:T(8,128)(2,1)S(1)}, u32[]{:S(2)}, u32[]{:S(2)}) collective-permute-start(bf16[64,1024]{1,0:T(8,128)(2,1)S(1)} %get-tuple-element.51), channel_id=1, source_target_pairs={{0,16},{4,20},{8,24},{12,28},{16,0},{20,4},{24,8},{28,12},{1,17},{... | collective-permute-start | bytes 393224 | tf_op jit(solution)/shard_map/ppermute | solution.py:339
  28.2 10.1 %collective-permute-start.6 = (bf16[64,1024]{1,0:T(8,128)(2,1)S(1)}, bf16[64,1024]{1,0:T(8,128)(2,1)S(1)}, u32[]{:S(2)}, u32[]{:S(2)}) collective-permute-start(bf16[64,1024]{1,0:T(8,128)(2,1)S(1)} %get-tuple-element.52), channel_id=1, source_target_pairs={{0,8},{4,12},{8,0},{12,4},{16,24},{20,28},{24,16},{28,20},{1,9},{5... | collective-permute-start | bytes 393224 | tf_op jit(solution)/shard_map/ppermute | solution.py:339
  33.1 9.1 %collective-permute-start.13 = (bf16[64,512]{1,0:T(8,128)(2,1)S(1)}, bf16[64,512]{1,0:T(8,128)(2,1)S(1)}, u32[]{:S(2)}, u32[]{:S(2)}) collective-permute-start(bf16[64,512]{1,0:T(8,128)(2,1)S(1)} %get-tuple-element.62), channel_id=1, source_target_pairs={{0,1},{1,0},{2,3},{3,2},{4,5},{5,4},{6,7},{7,6},{8,9},{9,8},{10,11... | collective-permute-start | bytes 196616 | tf_op jit(solution)/shard_map/ppermute | solution.py:339
  34.4 8.9 %collective-permute-start.14 = (bf16[64,512]{1,0:T(8,128)(2,1)S(1)}, bf16[64,512]{1,0:T(8,128)(2,1)S(1)}, u32[]{:S(2)}, u32[]{:S(2)}) collective-permute-start(bf16[64,512]{1,0:T(8,128)(2,1)S(1)} %get-tuple-element.63), channel_id=1, source_target_pairs={{0,2},{1,3},{2,0},{3,1},{4,6},{5,7},{6,4},{7,5},{8,10},{9,11},{10,... | collective-permute-start | bytes 196616 | tf_op jit(solution)/shard_map/ppermute | solution.py:339
  37.3 6.2 %collective-permute-start.15 = (bf16[64,512]{1,0:T(8,128)(2,1)S(1)}, bf16[64,512]{1,0:T(8,128)(2,1)S(1)}, u32[]{:S(2)}, u32[]{:S(2)}) collective-permute-start(bf16[64,512]{1,0:T(8,128)(2,1)S(1)} %get-tuple-element.64), channel_id=1, source_target_pairs={{0,3},{1,2},{2,1},{3,0},{4,7},{5,6},{6,5},{7,4},{8,11},{9,10},{10,... | collective-permute-start | bytes 196616 | tf_op jit(solution)/shard_map/ppermute | solution.py:339
  38.8 6.2 %collective-permute-start.7 = (bf16[64,512]{1,0:T(8,128)(2,1)S(1)}, bf16[64,512]{1,0:T(8,128)(2,1)S(1)}, u32[]{:S(2)}, u32[]{:S(2)}) collective-permute-start(bf16[64,512]{1,0:T(8,128)(2,1)S(1)} %get-tuple-element.54), channel_id=1, source_target_pairs={{0,1},{1,0},{2,3},{3,2},{4,5},{5,4},{6,7},{7,6},{8,9},{9,8},{10,11... | collective-permute-start | bytes 196616 | tf_op jit(solution)/shard_map/ppermute | solution.py:339
  38.9 7.8 %collective-permute-start.8 = (bf16[64,512]{1,0:T(8,128)(2,1)S(1)}, bf16[64,512]{1,0:T(8,128)(2,1)S(1)}, u32[]{:S(2)}, u32[]{:S(2)}) collective-permute-start(bf16[64,512]{1,0:T(8,128)(2,1)S(1)} %get-tuple-element.55), channel_id=1, source_target_pairs={{0,2},{1,3},{2,0},{3,1},{4,6},{5,7},{6,4},{7,5},{8,10},{9,11},{10,... | collective-permute-start | bytes 196616 | tf_op jit(solution)/shard_map/ppermute | solution.py:339
  42.2 6.1 %collective-permute-start.9 = (bf16[64,512]{1,0:T(8,128)(2,1)S(1)}, bf16[64,512]{1,0:T(8,128)(2,1)S(1)}, u32[]{:S(2)}, u32[]{:S(2)}) collective-permute-start(bf16[64,512]{1,0:T(8,128)(2,1)S(1)} %get-tuple-element.56), channel_id=1, source_target_pairs={{0,3},{1,2},{2,1},{3,0},{4,7},{5,6},{6,5},{7,4},{8,11},{9,10},{10,... | collective-permute-start | bytes 196616 | tf_op jit(solution)/shard_map/ppermute | solution.py:339
  49.4 4.4 %collective-permute-start.16 = (bf16[128,256]{1,0:T(8,128)(2,1)S(1)}, bf16[128,256]{1,0:T(8,128)(2,1)S(1)}, u32[]{:S(2)}, u32[]{:S(2)}) collective-permute-start(bf16[128,256]{1,0:T(8,128)(2,1)S(1)} %get-tuple-element.67), channel_id=1, source_target_pairs={{0,1},{1,0},{2,3},{3,2},{4,5},{5,4},{6,7},{7,6},{8,9},{9,8},{10,11... | collective-permute-start | bytes 196616 | tf_op jit(solution)/shard_map/ppermute | solution.py:339
  49.4 7.4 %collective-permute-start.17 = (bf16[128,256]{1,0:T(8,128)(2,1)S(1)}, bf16[128,256]{1,0:T(8,128)(2,1)S(1)}, u32[]{:S(2)}, u32[]{:S(2)}) collective-permute-start(bf16[128,256]{1,0:T(8,128)(2,1)S(1)} %get-tuple-element.68), channel_id=1, source_target_pairs={{0,2},{1,3},{2,0},{3,1},{4,6},{5,7},{6,4},{7,5},{8,10},{9,11},{10,... | collective-permute-start | bytes 196616 | tf_op jit(solution)/shard_map/ppermute | solution.py:339
  51.5 6.2 %collective-permute-start.18 = (bf16[128,256]{1,0:T(8,128)(2,1)S(1)}, bf16[128,256]{1,0:T(8,128)(2,1)S(1)}, u32[]{:S(2)}, u32[]{:S(2)}) collective-permute-start(bf16[128,256]{1,0:T(8,128)(2,1)S(1)} %get-tuple-element.69), channel_id=1, source_target_pairs={{0,3},{1,2},{2,1},{3,0},{4,7},{5,6},{6,5},{7,4},{8,11},{9,10},{10,... | collective-permute-start | bytes 196616 | tf_op jit(solution)/shard_map/ppermute | solution.py:339

commit v3 on v2

--- a/solution.py
+++ b/solution.py
@@ -13,13 +13,13 @@
 NN = (((1,), (0,)), ((), ()))
 ROW_TILE = 16
 LANES = 128
-COLS = 256
+PIECES = 2
 VMEM = pl.BlockSpec(memory_space=pltpu.VMEM)
 SMEM = pl.BlockSpec(memory_space=pltpu.SMEM)
 HBM = pl.BlockSpec(memory_space=pltpu.HBM)
 HALVES = 2
-OTHER_VMEM = 48
-OWN_VMEM = 48
+OTHER_VMEM = 45
+OWN_VMEM = 24
 
 
 def dot(a, b, dims):
@@ -50,38 +50,29 @@
 
 
 def multiply(slabs, rows, product):
-    result = dot(slabs[...], rows[...], NT)
-    for lane in range(COLS // LANES):
-        product[lane, :, :] = result[:, lane * LANES : (lane + 1) * LANES]
-
-
-def cut_rows(product, out, picks, chunk):
+    for lane in range(0, product.shape[0], 2):
+        result = dot(slabs[...], rows[lane * LANES : (lane + 2) * LANES, :], NT)
+        product[lane, :, :] = result[:, :LANES]
+        product[lane + 1, :, :] = result[:, LANES:]
+
+
+def cut_rows(product, out, picks, first):
     targets, frames, _ = out.shape
     span = product.shape[1] // targets
-    for step in range(targets):
-        found, _, shift = picks[step]
-        for lane in range(COLS // LANES):
+    for lane in range(product.shape[0]):
+        for step in range(targets):
+            found, _, shift = picks[step]
             rows = product[lane, pl.ds(step * span + shift, frames), :]
-            at = chunk * COLS + lane * LANES
+            at = first + lane * LANES
             out[step, :, at : at + LANES] = jnp.where(found >= 0, rows, 0.0).astype(BF16)
 
 
-def weight_copies(weight_hbm, head, tail, sem):
-    return [
-        pltpu.make_async_copy(
-            weight_hbm.at[pl.ds(chunk * COLS, COLS), :],
-            tail.at[pl.ds((chunk - 1) * COLS, COLS), :] if chunk else head,
-            sem.at[chunk],
-        )
-        for chunk in range(weight_hbm.shape[0] // COLS)
-    ]
-
-
-def other_kernel(routes, windows, weight, out, own, head, meta, slabs, tail, *refs):
-    products, (meta_sem, sem, weight_sem) = refs[:2], refs[2:]
+def other_kernel(routes, windows, weight_hbm, out, own, weight, meta, slabs, *refs):
+    products, (meta_sem, sem, weight_sem) = refs[:PIECES], refs[PIECES:]
     targets = out.shape[0]
     span = slabs.shape[0] // targets
     last_start = windows.shape[1] - span
+    columns = weight.shape[0] // PIECES
 
     def slab_copies(flip, picks, held):
         return [
@@ -94,8 +85,11 @@
         ]
 
     route_copy = pltpu.make_async_copy(routes, meta, meta_sem)
-    weights = weight_copies(weight, head, tail, weight_sem)
     route_copy.start()
+    weights = []
+    for piece in range(PIECES):
+        at = pl.ds(piece * columns, columns)
+        weights.append(pltpu.make_async_copy(weight_hbm.at[at, :], weight.at[at, :], weight_sem.at[piece]))
     weights[0].start()
     route_copy.wait()
     picks = picks_of(meta, 1, targets, last_start)
@@ -105,10 +99,10 @@
         copy.start()
     for copy in copies:
         copy.wait()
-    for chunk, copy in enumerate(weights):
+    for piece, copy in enumerate(weights):
         copy.wait()
-        multiply(slabs, tail.at[pl.ds((chunk - 1) * COLS, COLS), :] if chunk else head, products[chunk % 2])
-        cut_rows(products[chunk % 2], out, picks, chunk)
+        multiply(slabs, weight.at[pl.ds(piece * columns, columns), :], products[piece])
+        cut_rows(products[piece], out, picks, piece * columns)
     for copy in own_copies:
         copy.wait()
 
@@ -123,19 +117,19 @@
         out_shape=[
             jax.ShapeDtypeStruct((targets, frames, width), BF16),
             jax.ShapeDtypeStruct((targets * span, d_local), BF16),
-            jax.ShapeDtypeStruct((COLS, d_local), BF16),
+            jax.ShapeDtypeStruct((width, d_local), BF16),
         ],
         in_specs=[HBM] * 3,
         out_specs=[VMEM] * 3,
         scratch_shapes=[
             pltpu.SMEM(routes.shape, jnp.int32),
             pltpu.VMEM((targets * span, d_local), BF16),
-            pltpu.VMEM((width - COLS, d_local), BF16),
-            pltpu.VMEM((COLS // LANES, targets * span, LANES), F32),
-            pltpu.VMEM((COLS // LANES, targets * span, LANES), F32),
+        ]
+        + [pltpu.VMEM((width // PIECES // LANES, targets * span, LANES), F32)] * PIECES
+        + [
             pltpu.SemaphoreType.DMA,
             pltpu.SemaphoreType.DMA((2, targets)),
-            pltpu.SemaphoreType.DMA((width // COLS,)),
+            pltpu.SemaphoreType.DMA((PIECES,)),
         ],
         compiler_params=pltpu.CompilerParams(vmem_limit_bytes=OTHER_VMEM << 20),
         cost_estimate=matmul_cost(targets * span, d_local, width),
@@ -143,44 +137,36 @@
     )(routes, windows, weight)
 
 
-def own_kernel(last_start, routes, slabs, head, weight, out, meta, tail, *refs):
-    products, (meta_sem, weight_sem) = refs[:2], refs[2:]
+def own_kernel(last_start, routes, slabs, weight, out, meta, *refs):
+    products, meta_sem = refs[:-1], refs[-1]
+    columns = weight.shape[0] // len(products)
     route_copy = pltpu.make_async_copy(routes, meta, meta_sem)
-    weights = weight_copies(weight, head, tail, weight_sem)[1:]
     route_copy.start()
-    for copy in weights:
-        copy.start()
-    multiply(slabs, head, products[0])
+    multiply(slabs, weight.at[pl.ds(0, columns), :], products[0])
     route_copy.wait()
     picks = picks_of(meta, 0, out.shape[0], last_start)
-    for chunk, copy in enumerate(weights):
-        copy.wait()
-        multiply(slabs, tail.at[pl.ds(chunk * COLS, COLS), :], products[(chunk + 1) % 2])
-        cut_rows(products[chunk % 2], out, picks, chunk)
-    cut_rows(products[len(weights) % 2], out, picks, len(weights))
-
-
-def adapter_own(frames, seq_len, routes, slabs, head, weight):
+    for piece, product in enumerate(products):
+        if piece:
+            multiply(slabs, weight.at[pl.ds(piece * columns, columns), :], product)
+        cut_rows(product, out, picks, piece * columns)
+
+
+def adapter_own(frames, seq_len, routes, slabs, weight):
     width, d_local = weight.shape
     targets = lax.axis_size("dec") // 2
     span = frames + ROW_TILE
     return pl.pallas_call(
         functools.partial(own_kernel, seq_len - span),
         out_shape=jax.ShapeDtypeStruct((targets, frames, width), BF16),
-        in_specs=[HBM] + [VMEM] * 2 + [HBM],
+        in_specs=[HBM] + [VMEM] * 2,
         out_specs=VMEM,
-        scratch_shapes=[
-            pltpu.SMEM(routes.shape, jnp.int32),
-            pltpu.VMEM((width - COLS, d_local), BF16),
-            pltpu.VMEM((COLS // LANES, targets * span, LANES), F32),
-            pltpu.VMEM((COLS // LANES, targets * span, LANES), F32),
-            pltpu.SemaphoreType.DMA,
-            pltpu.SemaphoreType.DMA((width // COLS,)),
-        ],
+        scratch_shapes=[pltpu.SMEM(routes.shape, jnp.int32)]
+        + [pltpu.VMEM((width // PIECES // LANES, targets * span, LANES), F32)] * PIECES
+        + [pltpu.SemaphoreType.DMA],
         compiler_params=pltpu.CompilerParams(vmem_limit_bytes=OWN_VMEM << 20),
-        cost_estimate=matmul_cost(targets * span, d_local, width),
+        cost_estimate=matmul_cost(1, 1, 1),
         name="adapter_own",
-    )(routes, slabs, head, weight)
+    )(routes, slabs, weight)
 
 
 def pair_sum_kernel(own, other, *outs):
@@ -214,9 +200,8 @@
         total = total + block[...].astype(F32)
     rows = first + lax.broadcasted_iota(jnp.int32, (frames, width), 0)
     stream[...] = jnp.where(rows < valid[0], total, 0.0).astype(BF16)
-    ch = lax.axis_index("ch")
     for step, out in enumerate(outs):
-        at = pl.ds(pl.multiple_of((ch ^ step) * c_local, c_local), c_local)
+        at = pl.ds(pl.multiple_of(partner(step, len(outs)) * c_local, c_local), c_local)
         out[:, :c_local] = stream[:, at].astype(out.dtype)
         out[:, c_local:] = dot(stream[...], project[step], NN).astype(out.dtype)
 
@@ -248,19 +233,44 @@
     return -(-((taps - 1) // 2) // 8) * 8
 
 
-def forward_kernel(parts, valid, expand, project, taps_ref, scale, shift, *refs):
-    blocks, (value_out, gate_out, slope_out, project_t, expand_t, padded) = refs[:parts], refs[parts:]
+def transpose_kernel(expand, project, expand_t, project_t):
+    groups, _, c_local = project_t.shape
+    for step in range(groups):
+        at = pl.ds(pl.multiple_of(partner(step, groups) * c_local, c_local), c_local)
+        project_t[step, :, :] = project[at, :].T
+        expand_t[step, :, :] = expand[at, :].T
+
+
+def transposed(groups, expand, project):
+    width, span = expand.shape
+    c_local = width // groups
+    return pl.pallas_call(
+        transpose_kernel,
+        out_shape=[
+            jax.ShapeDtypeStruct((groups, span, c_local), BF16),
+            jax.ShapeDtypeStruct((groups, width, c_local), BF16),
+        ],
+        in_specs=[VMEM] * 2,
+        out_specs=[VMEM] * 2,
+        compiler_params=pltpu.CompilerParams(vmem_limit_bytes=24 << 20),
+        cost_estimate=matmul_cost(128, width, 3 * c_local),
+        name="transposed_weights",
+    )(expand, project)
+
+
+def forward_kernel(valid, expand, taps_ref, scale, shift, inputs, value_out, gate_out, slope_out, padded):
     frames, c_local = value_out.shape
     taps = taps_ref.shape[0]
     half = (taps - 1) // 2
     edge = (padded.shape[0] - frames) // 2
-    ch = lax.axis_index("ch")
     expanded = jnp.zeros((frames, 2 * c_local), F32)
-    for step, block in enumerate(blocks):
-        at = pl.ds(pl.multiple_of((ch ^ step) * c_local, c_local), c_local)
-        expanded = expanded + dot(block[...], expand[at, :], NN)
-        project_t[step, :, :] = project[at, :].T
-        expand_t[step, :, :] = expand[at, :].T
+    masks = [0]
+    while len(masks) * frames < inputs.shape[0]:
+        far = inputs.shape[0] // frames // 2 // len(masks)
+        masks += [mask ^ far for mask in masks]
+    for place, mask in enumerate(masks):
+        at = pl.ds(pl.multiple_of((lax.axis_index("ch") ^ mask) * c_local, c_local), c_local)
+        expanded = expanded + dot(inputs[place * frames : (place + 1) * frames, :], expand[at, :], NN)
     value = expanded[:, :c_local]
     gate = jax.nn.sigmoid(expanded[:, c_local:])
     rows = lax.broadcasted_iota(jnp.int32, (frames, c_local), 0)
@@ -275,20 +285,18 @@
     slope_out[...] = sig * (1.0 + shifted * (1.0 - sig)) * scale[...]
 
 
-def forward(valid, expand, project, taps, scale, shift, blocks):
-    frames, c_local = blocks[0].shape
-    groups, width = len(blocks), project.shape[1]
-    return pl.pallas_call(
-        functools.partial(forward_kernel, groups),
-        out_shape=[jax.ShapeDtypeStruct((frames, c_local), F32)] * 3
-        + [jax.ShapeDtypeStruct((groups, width, c_local), BF16), jax.ShapeDtypeStruct((groups, 2 * c_local, c_local), BF16)],
-        in_specs=[SMEM] + [VMEM] * (5 + groups),
-        out_specs=[VMEM] * 5,
+def forward(frames, valid, expand, taps, scale, shift, inputs):
+    width, c_local = expand.shape[0], inputs.shape[1]
+    return pl.pallas_call(
+        forward_kernel,
+        out_shape=[jax.ShapeDtypeStruct((frames, c_local), F32)] * 3,
+        in_specs=[SMEM] + [VMEM] * 5,
+        out_specs=[VMEM] * 3,
         scratch_shapes=[pltpu.VMEM((frames + 2 * edge_of(taps.shape[0]), c_local), F32)],
         compiler_params=pltpu.CompilerParams(vmem_limit_bytes=24 << 20),
-        cost_estimate=matmul_cost(frames, 4 * width, 2 * c_local),
+        cost_estimate=matmul_cost(frames, width, 2 * c_local),
         name="forward_gates",
-    )(valid, expand, project, taps, scale, shift, *blocks)
+    )(valid, expand, taps, scale, shift, inputs)
 
 
 def backward_kernel(parts, valid, expand_t, taps_ref, value_ref, gate_ref, slope, *refs):
@@ -335,8 +343,40 @@
     )(valid, expand_t, taps, value, gate, slope, *[block for half in halves for block in half])
 
 
+def partner(step, groups):
+    return lax.rem(lax.axis_index("ch") + step, groups)
+
+
 def swap(block, axis, count, mask):
     return lax.ppermute(block, axis, [(i, i ^ mask) for i in range(count)])
+
+
+def turns(count):
+    return sorted(range(1, count), key=lambda step: abs(2 * step - count))
+
+
+def turn(block, count, step):
+    return lax.ppermute(block, "ch", [(i, (i + step) % count) for i in range(count)])
+
+
+def z_exchange(blocks):
+    count = len(blocks)
+    return [blocks[0]] + [turn(blocks[step], count, step) for step in turns(count)]
+
+
+def z_gather(block, count, later):
+    held, mask = block, count // 2
+    while mask:
+        arrived = swap(held, "ch", count, mask)
+        if held is block:
+            pass
+        held = jnp.concatenate([held, arrived], axis=0)
+        mask //= 2
+    return held, later
+
+
+def plane_exchange(blocks, count):
+    return [blocks[0]] + [swap(block, "dec", count, 2 * step) for step, block in enumerate(blocks) if step]
 
 
 def body(
@@ -357,33 +397,29 @@
     u_local, frames, c_local = normed_input.shape
     width = expand_weight.shape[0]
     chips = n_dec // 2
-    own_input = normed_input.reshape(frames, c_local)
-    inputs = [own_input] + [swap(own_input, "ch", n_ch, step) for step in range(1, n_ch)]
     expand = expand_weight.reshape(width, 2 * c_local)
     taps = depth_kernel.astype(F32)
     scale, shift = norm_scale.reshape(1, c_local), norm_shift.reshape(1, c_local)
 
     seq_len = frame_cotangent.shape[1]
     routes = jnp.stack([rollout_utterance, frame_offset])
-    for_other, own_slabs, head = adapter_other(frames, routes, frame_cotangent, adapter_weight)
+    for_other, own_slabs, weight = adapter_other(frames, routes, frame_cotangent, adapter_weight)
     from_other = swap(for_other, "dec", n_dec, 1)
-    own = adapter_own(frames, seq_len, routes, own_slabs, head, adapter_weight)
-    own, inputs = lax.optimization_barrier((own, inputs))
-    sums = pair_sum(own, from_other)
-    arrived = [
-        [half[0]] + [swap(half[step], "dec", n_dec, 2 * step) for step in reversed(range(1, chips))] for half in sums
-    ]
-    value, gate, slope, project_t, expand_t = forward(
-        utterance_frames, expand, project_weight, taps, scale, shift, inputs
-    )
+    own = adapter_own(frames, seq_len, routes, own_slabs, weight)
+    first, second = pair_sum(own, from_other)
+    first, own_input = lax.optimization_barrier((first, normed_input.reshape(frames, c_local)))
+    arrived = [plane_exchange(first, n_dec)]
+    inputs, second = z_gather(own_input, n_ch, second)
+    arrived[0], second = lax.optimization_barrier((arrived[0], second))
+    arrived.append(plane_exchange(second, n_dec))
+    expand_t, project_t = transposed(n_ch, expand, project_weight)
+    value, gate, slope = forward(frames, utterance_frames, expand, taps, scale, shift, inputs)
+    value, gate, slope, project_t = lax.optimization_barrier((value, gate, slope, project_t))
     halves = []
     for at, half in enumerate(arrived):
-        sent = swish(at * frames // HALVES, utterance_frames, project_t, half)
-        halves.append([sent[0]] + [swap(sent[step], "ch", n_ch, step) for step in range(1, n_ch)])
+        halves.append(z_exchange(swish(at * frames // HALVES, utterance_frames, project_t, half)))
     stream, *parts = backward(utterance_frames, expand_t, taps, value, gate, slope, halves)
-    total = parts[0]
-    for step in range(1, n_ch):
-        total = total + swap(parts[step], "ch", n_ch, step).astype(F32)
+    total = sum(part.astype(F32) for part in z_exchange(parts))
     return stream[None], total.astype(BF16)[None]
 
 

time: 58.5 us -> 51.4 us (0.88)
  Pallas kernels: 17.4 us -> 12.4 us
  starting transfers between devices: 28.9 us -> 25.8 us
  waiting for transfers between devices: 8.91 us -> 9.91 us
    ppermute x19 -> x9, starting transfers between devices: 28.9 us -> 12.2 us  [swap(): return lax.ppermute(block, axis, [(i, i ^ mask) for i in range(count)])]
    ppermute x0 -> x9, starting transfers between devices: none -> 13.6 us  [turn(): lax.ppermute(block, 'ch', [(i, (i + step) % count) for i in range(count)])]
    ppermute x0 -> x9, waiting for transfers between devices: none -> 6.53 us  [turn(): lax.ppermute(block, 'ch', [(i, (i + step) % count) for i in range(count)])]
    ppermute x19 -> x9, waiting for transfers between devices: 8.91 us -> 3.38 us  [swap(): return lax.ppermute(block, axis, [(i, i ^ mask) for i in range(count)])]
    pallas_call x1, Pallas kernels: 5.84 us -> 3.12 us  [adapter_own(): pl.pallas_call(functools.partial(own_kernel, seq_len - span), out_shape=j...]
    pallas_call x1, Pallas kernels: 8.25 us -> 5.6 us  [adapter_other(): pl.pallas_call(other_kernel, out_shape=[jax.ShapeDtypeStruct((targets, fr...]
    pallas_call x1 -> x2, Pallas kernels: 1.07 us -> 1.42 us  [the longest x1 0.87 us: transposed(): pl.pallas_call(transpose_kernel, out_shape=[jax.ShapeDtypeStruct((groups,...]
  transfers between devices with their start and end apart: 19 -> 18, of which waited for: 6 -> 7; matrix products, arithmetic and copies ran while one was open for 0% -> 0% of each run, Pallas kernels for 14% -> 11%
where the time goes in v3:
time: 51.4 us; the launch traced here: 51.2 us
  starting transfers between devices  25.8 us (50%)
  Pallas kernels  12.4 us (24%)
  waiting for transfers between devices  9.91 us (19%)
  between operations  1.45 us (3%)
  other arithmetic  1.37 us (3%)
    ppermute x9, starting transfers between devices, turn(): lax.ppermute(block, 'ch', [(i, (i + step) % count) for i in range(count)])  13.6 us
    ppermute x9, starting transfers between devices, swap(): return lax.ppermute(block, axis, [(i, i ^ mask) for i in range(count)])  12.2 us
    ppermute x9, waiting for transfers between devices, turn(): lax.ppermute(block, 'ch', [(i, (i + step) % count) for i in range(count)])  6.53 us
    pallas_call x1, Pallas kernels, adapter_other(): pl.pallas_call(other_kernel, out_shape=[jax.ShapeDtypeStruct((targets, fr...  5.6 us
    ppermute x9, waiting for transfers between devices, swap(): return lax.ppermute(block, axis, [(i, i ^ mask) for i in range(count)])  3.38 us
    pallas_call x1, Pallas kernels, adapter_own(): pl.pallas_call(functools.partial(own_kernel, seq_len - span), out_shape=j...  3.12 us
    pallas_call x1, Pallas kernels, backward(): pl.pallas_call(functools.partial(backward_kernel, groups), out_shape=[jax...  1.07 us
  transfers between devices with their start and end apart: 18, of which 7 were waited for; matrix products, arithmetic and copies ran while one was open for 0% of the time, Pallas kernels for 11%

profile of v3, /device:TPU:0, one launch (start us, length us, event | category | flops | bytes accessed | tf_op | source)
XLA Modules:
  0.0 51.2 jit_solution(10941799179645954106)
XLA Ops:
  0.6 0.7 %pad_add_fusion.routes = s32[2,8]{1,0:T(2,128)S(1)} fusion(s32[1,8]{1,0:T(1,128)} %bitcast.18, s32[1,8]{1,0:T(1,128)} %bitcast.19), kind=kLoop, calls=%fused_computation.4 | loop fusion | flops 16 | bytes 128 | tf_op jit(solution)/shard_map/stack | solution.py:405
  1.3 5.6 %adapter_other.1 = (bf16[4,128,1024]{2,1,0:T(8,128)(2,1)S(1)}, bf16[576,2048]{1,0:T(8,128)(2,1)S(1)}, bf16[1024,2048]{1,0:T(8,128)(2,1)S(1)}) custom-call(s32[2,8]{1,0:T(2,128)S(1)} %pad_add_fusion.routes, bf16[8,160,2048]{2,1,0:T(8,128)(2,1)} %windows.1, bf16[1024,2048]{1,0:T(8,128)(2,1)} %weight_hbm.1), custom_call_target="tpu_custom_call" | custom-call | flops 2415919104 | bytes 7733248 | tf_op jit(solution)/shard_map/adapter_other/pallas_call | solution.py:115
  6.9 0.5 %collective-permute-start = (bf16[4,128,1024]{2,1,0:T(8,128)(2,1)S(1)}, bf16[4,128,1024]{2,1,0:T(8,128)(2,1)S(1)}, u32[]{:S(2)}, u32[]{:S(2)}) collective-permute-start(bf16[4,128,1024]{2,1,0:T(8,128)(2,1)S(1)} %get-tuple-element.51), channel_id=1, source_target_pairs={{0,4},{4,0},{8,12},{12,8},{16,20},{20,16},{24,28},{28,24},{1,5},{5... | collective-permute-start | bytes 3145736 | tf_op jit(solution)/shard_map/ppermute | solution.py:351
  7.4 3.1 %adapter_own.1.own = bf16[4,128,1024]{2,1,0:T(8,128)(2,1)S(1)} custom-call(s32[2,8]{1,0:T(2,128)S(1)} %pad_add_fusion.routes, bf16[576,2048]{1,0:T(8,128)(2,1)S(1)} %get-tuple-element.49.slabs, bf16[1024,2048]{1,0:T(8,128)(2,1)S(1)} %get-tuple-element.50.weight), custom_call_target="tpu_custom_call" | custom-call | flops 2 | bytes 6 | tf_op jit(solution)/shard_map/adapter_own/pallas_call | solution.py:158
  10.9 3.7 %collective-permute-start.1 = (bf16[128,256]{1,0:T(8,128)(2,1)S(1)}, bf16[128,256]{1,0:T(8,128)(2,1)S(1)}, u32[]{:S(2)}, u32[]{:S(2)}) collective-permute-start(bf16[128,256]{1,0:T(8,128)(2,1)S(1)} %bitcast.15), channel_id=1, source_target_pairs={{0,2},{1,3},{2,0},{3,1},{4,6},{5,7},{6,4},{7,5},{8,10},{9,11},{10,... | collective-permute-start | bytes 196616 | tf_op jit(solution)/shard_map/ppermute | solution.py:351
  14.6 1.5 %collective-permute-start.3 = (bf16[64,1024]{1,0:T(8,128)(2,1)S(1)}, bf16[64,1024]{1,0:T(8,128)(2,1)S(1)}, u32[]{:S(2)}, u32[]{:S(2)}) collective-permute-start(bf16[64,1024]{1,0:T(8,128)(2,1)S(1)} %get-tuple-element.66), channel_id=1, source_target_pairs={{0,8},{4,12},{8,0},{12,4},{16,24},{20,28},{24,16},{28,20},{1,9},{5... | collective-permute-start | bytes 393224 | tf_op jit(solution)/shard_map/ppermute | solution.py:351
  16.1 1.5 %collective-permute-start.4 = (bf16[64,1024]{1,0:T(8,128)(2,1)S(1)}, bf16[64,1024]{1,0:T(8,128)(2,1)S(1)}, u32[]{:S(2)}, u32[]{:S(2)}) collective-permute-start(bf16[64,1024]{1,0:T(8,128)(2,1)S(1)} %get-tuple-element.67), channel_id=1, source_target_pairs={{0,16},{4,20},{8,24},{12,28},{16,0},{20,4},{24,8},{28,12},{1,17},{... | collective-permute-start | bytes 393224 | tf_op jit(solution)/shard_map/ppermute | solution.py:351
  17.6 0.5 collective-permute-start.5
  18.1 0.6 %collective-permute-done.1 = bf16[128,256]{1,0:T(8,128)(2,1)S(1)} collective-permute-done((bf16[128,256]{1,0:T(8,128)(2,1)S(1)}, bf16[128,256]{1,0:T(8,128)(2,1)S(1)}, u32[]{:S(2)}, u32[]{:S(2)}) %collective-permute-start.1) | collective-permute-done | bytes 65568 | tf_op jit(solution)/shard_map/ppermute | solution.py:351
  18.7 1.0 %collective-permute-start.2 = (bf16[256,256]{1,0:T(8,128)(2,1)S(1)}, bf16[256,256]{1,0:T(8,128)(2,1)S(1)}, u32[]{:S(2)}, u32[]{:S(2)}) collective-permute-start(bf16[256,256]{1,0:T(8,128)(2,1)S(1)} %pad_maximum_fusion.1), channel_id=1, source_target_pairs={{0,1},{1,0},{2,3},{3,2},{4,5},{5,4},{6,7},{7,6},{8,9},{9,8},{10,11... | collective-permute-start | bytes 393224 | tf_op jit(solution)/shard_map/ppermute | solution.py:351
  20.6 0.9 %transposed_weights.1 = (bf16[4,512,256]{2,1,0:T(8,128)(2,1)S(1)}, bf16[4,1024,256]{2,1,0:T(8,128)(2,1)S(1)}) custom-call(bf16[1024,512]{1,0:T(8,128)(2,1)S(1)} %bitcast.10, bf16[1024,1024]{1,0:T(8,128)(2,1)S(1)} %copy-done), custom_call_target="tpu_custom_call" | custom-call | flops 201326592 | bytes 2031616 | tf_op jit(solution)/shard_map/transposed_weights/pallas_call | solution.py:247
  21.5 2.6 %collective-permute-done.4.refs_2_ = bf16[64,1024]{1,0:T(8,128)(2,1)S(1)} collective-permute-done((bf16[64,1024]{1,0:T(8,128)(2,1)S(1)}, bf16[64,1024]{1,0:T(8,128)(2,1)S(1)}, u32[]{:S(2)}, u32[]{:S(2)}) %collective-permute-start.4) | collective-permute-done | bytes 131104 | tf_op jit(solution)/shard_map/ppermute | solution.py:351
  24.2 1.5 %collective-permute-start.10 = (bf16[64,1024]{1,0:T(8,128)(2,1)S(1)}, bf16[64,1024]{1,0:T(8,128)(2,1)S(1)}, u32[]{:S(2)}, u32[]{:S(2)}) collective-permute-start(bf16[64,1024]{1,0:T(8,128)(2,1)S(1)} %get-tuple-element.83), channel_id=1, source_target_pairs={{0,16},{4,20},{8,24},{12,28},{16,0},{20,4},{24,8},{28,12},{1,17},{... | collective-permute-start | bytes 393224 | tf_op jit(solution)/shard_map/ppermute | solution.py:351
  25.7 1.2 %collective-permute-start.11 = (bf16[64,1024]{1,0:T(8,128)(2,1)S(1)}, bf16[64,1024]{1,0:T(8,128)(2,1)S(1)}, u32[]{:S(2)}, u32[]{:S(2)}) collective-permute-start(bf16[64,1024]{1,0:T(8,128)(2,1)S(1)} %get-tuple-element.84), channel_id=1, source_target_pairs={{0,24},{4,28},{8,16},{12,20},{16,8},{20,12},{24,0},{28,4},{1,25},{... | collective-permute-start | bytes 393224 | tf_op jit(solution)/shard_map/ppermute | solution.py:351
  26.9 0.8 %collective-permute-start.9 = (bf16[64,1024]{1,0:T(8,128)(2,1)S(1)}, bf16[64,1024]{1,0:T(8,128)(2,1)S(1)}, u32[]{:S(2)}, u32[]{:S(2)}) collective-permute-start(bf16[64,1024]{1,0:T(8,128)(2,1)S(1)} %get-tuple-element.82), channel_id=1, source_target_pairs={{0,8},{4,12},{8,0},{12,4},{16,24},{20,28},{24,16},{28,20},{1,9},{5... | collective-permute-start | bytes 393224 | tf_op jit(solution)/shard_map/ppermute | solution.py:351
  27.7 0.5 %forward_gates.1 = (f32[128,256]{1,0:T(8,128)S(1)}, f32[128,256]{1,0:T(8,128)S(1)}, f32[128,256]{1,0:T(8,128)S(1)}) custom-call(s32[1]{0:T(128)S(6)} %copy.14.valid, bf16[1024,512]{1,0:T(8,128)(2,1)S(1)} %bitcast.11, f32[9,256]{1,0:T(8,128)S(1)} %convert_element_type.15.taps_ref, f32[1,256]{1,0:T(1,128)S(1)} %bitcast.12, f32[1,256]{1,0:T(1,128)S(1)} %bitcast.13, ...), custom_call_target="tpu_custom_call" | custom-call | flops 134217728 | bytes 1441792 | tf_op jit(solution)/shard_map/forward_gates/pallas_call | solution.py:290
  28.3 0.5 stream_and_swish.2
  28.8 0.7 %collective-permute-start.6 = (bf16[64,512]{1,0:T(8,128)(2,1)S(1)}, bf16[64,512]{1,0:T(8,128)(2,1)S(1)}, u32[]{:S(2)}, u32[]{:S(2)}) collective-permute-start(bf16[64,512]{1,0:T(8,128)(2,1)S(1)} %get-tuple-element.78), channel_id=1, source_target_pairs={{0,2},{1,3},{2,0},{3,1},{4,6},{5,7},{6,4},{7,5},{8,10},{9,11},{10,... | collective-permute-start | bytes 196616 | tf_op jit(solution)/shard_map/ppermute | solution.py:359
  29.4 1.3 %collective-permute-start.7 = (bf16[64,512]{1,0:T(8,128)(2,1)S(1)}, bf16[64,512]{1,0:T(8,128)(2,1)S(1)}, u32[]{:S(2)}, u32[]{:S(2)}) collective-permute-start(bf16[64,512]{1,0:T(8,128)(2,1)S(1)} %get-tuple-element.79), channel_id=1, source_target_pairs={{0,1},{1,2},{2,3},{3,0},{4,5},{5,6},{6,7},{7,4},{8,9},{9,10},{10,1... | collective-permute-start | bytes 196616 | tf_op jit(solution)/shard_map/ppermute | solution.py:359
  30.9 2.4 %collective-permute-start.8 = (bf16[64,512]{1,0:T(8,128)(2,1)S(1)}, bf16[64,512]{1,0:T(8,128)(2,1)S(1)}, u32[]{:S(2)}, u32[]{:S(2)}) collective-permute-start(bf16[64,512]{1,0:T(8,128)(2,1)S(1)} %get-tuple-element.80), channel_id=1, source_target_pairs={{0,3},{1,0},{2,1},{3,2},{4,7},{5,4},{6,5},{7,6},{8,11},{9,8},{10,9... | collective-permute-start | bytes 196616 | tf_op jit(solution)/shard_map/ppermute | solution.py:359
  33.3 0.5 stream_and_swish.3
  33.8 0.8 %collective-permute-start.12 = (bf16[64,512]{1,0:T(8,128)(2,1)S(1)}, bf16[64,512]{1,0:T(8,128)(2,1)S(1)}, u32[]{:S(2)}, u32[]{:S(2)}) collective-permute-start(bf16[64,512]{1,0:T(8,128)(2,1)S(1)} %get-tuple-element.86), channel_id=1, source_target_pairs={{0,2},{1,3},{2,0},{3,1},{4,6},{5,7},{6,4},{7,5},{8,10},{9,11},{10,... | collective-permute-start | bytes 196616 | tf_op jit(solution)/shard_map/ppermute | solution.py:359
  34.5 1.4 %collective-permute-start.13 = (bf16[64,512]{1,0:T(8,128)(2,1)S(1)}, bf16[64,512]{1,0:T(8,128)(2,1)S(1)}, u32[]{:S(2)}, u32[]{:S(2)}) collective-permute-start(bf16[64,512]{1,0:T(8,128)(2,1)S(1)} %get-tuple-element.87), channel_id=1, source_target_pairs={{0,1},{1,2},{2,3},{3,0},{4,5},{5,6},{6,7},{7,4},{8,9},{9,10},{10,1... | collective-permute-start | bytes 196616 | tf_op jit(solution)/shard_map/ppermute | solution.py:359
  35.9 2.4 %collective-permute-start.14 = (bf16[64,512]{1,0:T(8,128)(2,1)S(1)}, bf16[64,512]{1,0:T(8,128)(2,1)S(1)}, u32[]{:S(2)}, u32[]{:S(2)}) collective-permute-start(bf16[64,512]{1,0:T(8,128)(2,1)S(1)} %get-tuple-element.88), channel_id=1, source_target_pairs={{0,3},{1,0},{2,1},{3,2},{4,7},{5,4},{6,5},{7,6},{8,11},{9,8},{10,9... | collective-permute-start | bytes 196616 | tf_op jit(solution)/shard_map/ppermute | solution.py:359
  38.4 2.9 %collective-permute-done.12.refs_5_ = bf16[64,512]{1,0:T(8,128)(2,1)S(1)} collective-permute-done((bf16[64,512]{1,0:T(8,128)(2,1)S(1)}, bf16[64,512]{1,0:T(8,128)(2,1)S(1)}, u32[]{:S(2)}, u32[]{:S(2)}) %collective-permute-start.12) | collective-permute-done | bytes 65568 | tf_op jit(solution)/shard_map/ppermute | solution.py:359
  41.5 1.1 %backward_module.1 = (bf16[128,256]{1,0:T(8,128)(2,1)}, f32[128,256]{1,0:T(8,128)S(1)}, bf16[128,256]{1,0:T(8,128)(2,1)S(1)}, bf16[128,256]{1,0:T(8,128)(2,1)S(1)}, bf16[128,256]{1,0:T(8,128)(2,1)S(1)}) custom-call(s32[1]{0:T(128)S(6)} %copy.14.valid, bf16[4,512,256]{2,1,0:T(8,128)(2,1)S(1)} %get-tuple-element.48.expand_t, ...), custom_call_target="tpu_custom_call" | custom-call | flops 134217728 | bytes 1441792 | tf_op jit(solution)/shard_map/backward_module/pallas_call | solution.py:333
  42.5 0.7 %collective-permute-start.15 = (bf16[128,256]{1,0:T(8,128)(2,1)S(1)}, bf16[128,256]{1,0:T(8,128)(2,1)S(1)}, u32[]{:S(2)}, u32[]{:S(2)}) collective-permute-start(bf16[128,256]{1,0:T(8,128)(2,1)S(1)} %get-tuple-element.91), channel_id=1, source_target_pairs={{0,2},{1,3},{2,0},{3,1},{4,6},{5,7},{6,4},{7,5},{8,10},{9,11},{10,... | collective-permute-start | bytes 196616 | tf_op jit(solution)/shard_map/ppermute | solution.py:359
  43.3 2.8 %collective-permute-start.16 = (bf16[128,256]{1,0:T(8,128)(2,1)S(1)}, bf16[128,256]{1,0:T(8,128)(2,1)S(1)}, u32[]{:S(2)}, u32[]{:S(2)}) collective-permute-start(bf16[128,256]{1,0:T(8,128)(2,1)S(1)} %get-tuple-element.92), channel_id=1, source_target_pairs={{0,1},{1,2},{2,3},{3,0},{4,5},{5,6},{6,7},{7,4},{8,9},{9,10},{10,1... | collective-permute-start | bytes 196616 | tf_op jit(solution)/shard_map/ppermute | solution.py:359
  46.1 1.0 %collective-permute-start.17 = (bf16[128,256]{1,0:T(8,128)(2,1)S(1)}, bf16[128,256]{1,0:T(8,128)(2,1)S(1)}, u32[]{:S(2)}, u32[]{:S(2)}) collective-permute-start(bf16[128,256]{1,0:T(8,128)(2,1)S(1)} %get-tuple-element.93), channel_id=1, source_target_pairs={{0,3},{1,0},{2,1},{3,2},{4,7},{5,4},{6,5},{7,6},{8,11},{9,8},{10,9... | collective-permute-start | bytes 196616 | tf_op jit(solution)/shard_map/ppermute | solution.py:359
  47.1 2.9 %collective-permute-done.15 = bf16[128,256]{1,0:T(8,128)(2,1)S(1)} collective-permute-done((bf16[128,256]{1,0:T(8,128)(2,1)S(1)}, bf16[128,256]{1,0:T(8,128)(2,1)S(1)}, u32[]{:S(2)}, u32[]{:S(2)}) %collective-permute-start.15) | collective-permute-done | bytes 65568 | tf_op jit(solution)/shard_map/ppermute | solution.py:359
  50.0 0.5 collective-permute-done.17
  50.6 0.7 %fusion = bf16[1,128,256]{2,1,0:T(8,128)(2,1)} fusion(bf16[128,256]{1,0:T(8,128)(2,1)S(1)} %collective-permute-done.17, bf16[128,256]{1,0:T(8,128)(2,1)S(1)} %collective-permute-done.16, f32[128,256]{1,0:T(8,128)S(1)} %get-tuple-element.90, bf16[128,256]{1,0:T(8,128)(2,1)S(1)} %collective-permute-done.15), kind=kLoop, calls=%fused_computation.3 | loop fusion | flops 229376 | bytes 393216 | tf_op jit(solution)/shard_map/broadcast_in_dim | solution.py:423
  (30 shorter events, 0.8 us)
Async XLA Ops:
  6.9 3.7 %collective-permute-start = (bf16[4,128,1024]{2,1,0:T(8,128)(2,1)S(1)}, bf16[4,128,1024]{2,1,0:T(8,128)(2,1)S(1)}, u32[]{:S(2)}, u32[]{:S(2)}) collective-permute-start(bf16[4,128,1024]{2,1,0:T(8,128)(2,1)S(1)} %get-tuple-element.51), channel_id=1, source_target_pairs={{0,4},{4,0},{8,12},{12,8},{16,20},{20,16},{24,28},{28,24},{1,5},{5... | collective-permute-start | bytes 3145736 | tf_op jit(solution)/shard_map/ppermute | solution.py:351
  7.4 3.4 %copy-start.4 = (bf16[1,128,256]{2,1,0:T(8,128)(2,1)S(1)}, bf16[1,128,256]{2,1,0:T(8,128)(2,1)}, u32[]{:S(2)}) copy-start(bf16[1,128,256]{2,1,0:T(8,128)(2,1)} %param.15) | copy-start | bytes 196612
  7.4 12.9 %copy-start.3 = (bf16[1024,2,256]{2,1,0:T(2,128)(2,1)S(1)}, bf16[1024,2,256]{2,1,0:T(2,128)(2,1)}, u32[]{:S(2)}) copy-start(bf16[1024,2,256]{2,1,0:T(2,128)(2,1)} %param.16) | copy-start | bytes 3145732
  7.4 13.2 %copy-start.5 = (bf16[9,256]{1,0:T(8,128)(2,1)S(1)}, bf16[9,256]{1,0:T(8,128)(2,1)}, u32[]{:S(2)}) copy-start(bf16[9,256]{1,0:T(8,128)(2,1)} %param.17) | copy-start | bytes 13828
  7.4 13.2 %copy-start = (bf16[1024,1024]{1,0:T(8,128)(2,1)S(1)}, bf16[1024,1024]{1,0:T(8,128)(2,1)}, u32[]{:S(2)}) copy-start(bf16[1024,1024]{1,0:T(8,128)(2,1)} %project.1) | copy-start | bytes 6291460
  10.6 17.1 %copy-start.1 = (f32[256]{0:T(256)S(1)}, f32[256]{0:T(256)}, u32[]{:S(2)}) copy-start(f32[256]{0:T(256)} %param.18) | copy-start | bytes 3076
  10.6 17.1 %copy-start.2 = (f32[256]{0:T(256)S(1)}, f32[256]{0:T(256)}, u32[]{:S(2)}) copy-start(f32[256]{0:T(256)} %param.19) | copy-start | bytes 3076
  10.9 7.8 %collective-permute-start.1 = (bf16[128,256]{1,0:T(8,128)(2,1)S(1)}, bf16[128,256]{1,0:T(8,128)(2,1)S(1)}, u32[]{:S(2)}, u32[]{:S(2)}) collective-permute-start(bf16[128,256]{1,0:T(8,128)(2,1)S(1)} %bitcast.15), channel_id=1, source_target_pairs={{0,2},{1,3},{2,0},{3,1},{4,6},{5,7},{6,4},{7,5},{8,10},{9,11},{10,... | collective-permute-start | bytes 196616 | tf_op jit(solution)/shard_map/ppermute | solution.py:351
  14.6 7.0 %collective-permute-start.3 = (bf16[64,1024]{1,0:T(8,128)(2,1)S(1)}, bf16[64,1024]{1,0:T(8,128)(2,1)S(1)}, u32[]{:S(2)}, u32[]{:S(2)}) collective-permute-start(bf16[64,1024]{1,0:T(8,128)(2,1)S(1)} %get-tuple-element.66), channel_id=1, source_target_pairs={{0,8},{4,12},{8,0},{12,4},{16,24},{20,28},{24,16},{28,20},{1,9},{5... | collective-permute-start | bytes 393224 | tf_op jit(solution)/shard_map/ppermute | solution.py:351
  16.1 8.1 %collective-permute-start.4 = (bf16[64,1024]{1,0:T(8,128)(2,1)S(1)}, bf16[64,1024]{1,0:T(8,128)(2,1)S(1)}, u32[]{:S(2)}, u32[]{:S(2)}) collective-permute-start(bf16[64,1024]{1,0:T(8,128)(2,1)S(1)} %get-tuple-element.67), channel_id=1, source_target_pairs={{0,16},{4,20},{8,24},{12,28},{16,0},{20,4},{24,8},{28,12},{1,17},{... | collective-permute-start | bytes 393224 | tf_op jit(solution)/shard_map/ppermute | solution.py:351
  17.6 6.6 %collective-permute-start.5 = (bf16[64,1024]{1,0:T(8,128)(2,1)S(1)}, bf16[64,1024]{1,0:T(8,128)(2,1)S(1)}, u32[]{:S(2)}, u32[]{:S(2)}) collective-permute-start(bf16[64,1024]{1,0:T(8,128)(2,1)S(1)} %get-tuple-element.68), channel_id=1, source_target_pairs={{0,24},{4,28},{8,16},{12,20},{16,8},{20,12},{24,0},{28,4},{1,25},{... | collective-permute-start | bytes 393224 | tf_op jit(solution)/shard_map/ppermute | solution.py:351
  18.7 9.0 %collective-permute-start.2 = (bf16[256,256]{1,0:T(8,128)(2,1)S(1)}, bf16[256,256]{1,0:T(8,128)(2,1)S(1)}, u32[]{:S(2)}, u32[]{:S(2)}) collective-permute-start(bf16[256,256]{1,0:T(8,128)(2,1)S(1)} %pad_maximum_fusion.1), channel_id=1, source_target_pairs={{0,1},{1,0},{2,3},{3,2},{4,5},{5,4},{6,7},{7,6},{8,9},{9,8},{10,11... | collective-permute-start | bytes 393224 | tf_op jit(solution)/shard_map/ppermute | solution.py:351
  24.2 6.7 %collective-permute-start.10 = (bf16[64,1024]{1,0:T(8,128)(2,1)S(1)}, bf16[64,1024]{1,0:T(8,128)(2,1)S(1)}, u32[]{:S(2)}, u32[]{:S(2)}) collective-permute-start(bf16[64,1024]{1,0:T(8,128)(2,1)S(1)} %get-tuple-element.83), channel_id=1, source_target_pairs={{0,16},{4,20},{8,24},{12,28},{16,0},{20,4},{24,8},{28,12},{1,17},{... | collective-permute-start | bytes 393224 | tf_op jit(solution)/shard_map/ppermute | solution.py:351
  25.7 7.6 %collective-permute-start.11 = (bf16[64,1024]{1,0:T(8,128)(2,1)S(1)}, bf16[64,1024]{1,0:T(8,128)(2,1)S(1)}, u32[]{:S(2)}, u32[]{:S(2)}) collective-permute-start(bf16[64,1024]{1,0:T(8,128)(2,1)S(1)} %get-tuple-element.84), channel_id=1, source_target_pairs={{0,24},{4,28},{8,16},{12,20},{16,8},{20,12},{24,0},{28,4},{1,25},{... | collective-permute-start | bytes 393224 | tf_op jit(solution)/shard_map/ppermute | solution.py:351
  26.9 6.4 %collective-permute-start.9 = (bf16[64,1024]{1,0:T(8,128)(2,1)S(1)}, bf16[64,1024]{1,0:T(8,128)(2,1)S(1)}, u32[]{:S(2)}, u32[]{:S(2)}) collective-permute-start(bf16[64,1024]{1,0:T(8,128)(2,1)S(1)} %get-tuple-element.82), channel_id=1, source_target_pairs={{0,8},{4,12},{8,0},{12,4},{16,24},{20,28},{24,16},{28,20},{1,9},{5... | collective-permute-start | bytes 393224 | tf_op jit(solution)/shard_map/ppermute | solution.py:351
  28.8 7.2 %collective-permute-start.6 = (bf16[64,512]{1,0:T(8,128)(2,1)S(1)}, bf16[64,512]{1,0:T(8,128)(2,1)S(1)}, u32[]{:S(2)}, u32[]{:S(2)}) collective-permute-start(bf16[64,512]{1,0:T(8,128)(2,1)S(1)} %get-tuple-element.78), channel_id=1, source_target_pairs={{0,2},{1,3},{2,0},{3,1},{4,6},{5,7},{6,4},{7,5},{8,10},{9,11},{10,... | collective-permute-start | bytes 196616 | tf_op jit(solution)/shard_map/ppermute | solution.py:359
  29.4 8.9 %collective-permute-start.7 = (bf16[64,512]{1,0:T(8,128)(2,1)S(1)}, bf16[64,512]{1,0:T(8,128)(2,1)S(1)}, u32[]{:S(2)}, u32[]{:S(2)}) collective-permute-start(bf16[64,512]{1,0:T(8,128)(2,1)S(1)} %get-tuple-element.79), channel_id=1, source_target_pairs={{0,1},{1,2},{2,3},{3,0},{4,5},{5,6},{6,7},{7,4},{8,9},{9,10},{10,1... | collective-permute-start | bytes 196616 | tf_op jit(solution)/shard_map/ppermute | solution.py:359
  30.9 7.5 %collective-permute-start.8 = (bf16[64,512]{1,0:T(8,128)(2,1)S(1)}, bf16[64,512]{1,0:T(8,128)(2,1)S(1)}, u32[]{:S(2)}, u32[]{:S(2)}) collective-permute-start(bf16[64,512]{1,0:T(8,128)(2,1)S(1)} %get-tuple-element.80), channel_id=1, source_target_pairs={{0,3},{1,0},{2,1},{3,2},{4,7},{5,4},{6,5},{7,6},{8,11},{9,8},{10,9... | collective-permute-start | bytes 196616 | tf_op jit(solution)/shard_map/ppermute | solution.py:359
  33.8 7.6 %collective-permute-start.12 = (bf16[64,512]{1,0:T(8,128)(2,1)S(1)}, bf16[64,512]{1,0:T(8,128)(2,1)S(1)}, u32[]{:S(2)}, u32[]{:S(2)}) collective-permute-start(bf16[64,512]{1,0:T(8,128)(2,1)S(1)} %get-tuple-element.86), channel_id=1, source_target_pairs={{0,2},{1,3},{2,0},{3,1},{4,6},{5,7},{6,4},{7,5},{8,10},{9,11},{10,... | collective-permute-start | bytes 196616 | tf_op jit(solution)/shard_map/ppermute | solution.py:359
  34.5 6.8 %collective-permute-start.13 = (bf16[64,512]{1,0:T(8,128)(2,1)S(1)}, bf16[64,512]{1,0:T(8,128)(2,1)S(1)}, u32[]{:S(2)}, u32[]{:S(2)}) collective-permute-start(bf16[64,512]{1,0:T(8,128)(2,1)S(1)} %get-tuple-element.87), channel_id=1, source_target_pairs={{0,1},{1,2},{2,3},{3,0},{4,5},{5,6},{6,7},{7,4},{8,9},{9,10},{10,1... | collective-permute-start | bytes 196616 | tf_op jit(solution)/shard_map/ppermute | solution.py:359
  35.9 5.5 %collective-permute-start.14 = (bf16[64,512]{1,0:T(8,128)(2,1)S(1)}, bf16[64,512]{1,0:T(8,128)(2,1)S(1)}, u32[]{:S(2)}, u32[]{:S(2)}) collective-permute-start(bf16[64,512]{1,0:T(8,128)(2,1)S(1)} %get-tuple-element.88), channel_id=1, source_target_pairs={{0,3},{1,0},{2,1},{3,2},{4,7},{5,4},{6,5},{7,6},{8,11},{9,8},{10,9... | collective-permute-start | bytes 196616 | tf_op jit(solution)/shard_map/ppermute | solution.py:359
  42.5 7.5 %collective-permute-start.15 = (bf16[128,256]{1,0:T(8,128)(2,1)S(1)}, bf16[128,256]{1,0:T(8,128)(2,1)S(1)}, u32[]{:S(2)}, u32[]{:S(2)}) collective-permute-start(bf16[128,256]{1,0:T(8,128)(2,1)S(1)} %get-tuple-element.91), channel_id=1, source_target_pairs={{0,2},{1,3},{2,0},{3,1},{4,6},{5,7},{6,4},{7,5},{8,10},{9,11},{10,... | collective-permute-start | bytes 196616 | tf_op jit(solution)/shard_map/ppermute | solution.py:359
  43.3 6.8 %collective-permute-start.16 = (bf16[128,256]{1,0:T(8,128)(2,1)S(1)}, bf16[128,256]{1,0:T(8,128)(2,1)S(1)}, u32[]{:S(2)}, u32[]{:S(2)}) collective-permute-start(bf16[128,256]{1,0:T(8,128)(2,1)S(1)} %get-tuple-element.92), channel_id=1, source_target_pairs={{0,1},{1,2},{2,3},{3,0},{4,5},{5,6},{6,7},{7,4},{8,9},{9,10},{10,1... | collective-permute-start | bytes 196616 | tf_op jit(solution)/shard_map/ppermute | solution.py:359
  46.1 4.5 %collective-permute-start.17 = (bf16[128,256]{1,0:T(8,128)(2,1)S(1)}, bf16[128,256]{1,0:T(8,128)(2,1)S(1)}, u32[]{:S(2)}, u32[]{:S(2)}) collective-permute-start(bf16[128,256]{1,0:T(8,128)(2,1)S(1)} %get-tuple-element.93), channel_id=1, source_target_pairs={{0,3},{1,0},{2,1},{3,2},{4,7},{5,4},{6,5},{7,6},{8,11},{9,8},{10,9... | collective-permute-start | bytes 196616 | tf_op jit(solution)/shard_map/ppermute | solution.py:359

commit v4 on v3

--- a/solution.py
+++ b/solution.py
@@ -17,9 +17,10 @@
 VMEM = pl.BlockSpec(memory_space=pltpu.VMEM)
 SMEM = pl.BlockSpec(memory_space=pltpu.SMEM)
 HBM = pl.BlockSpec(memory_space=pltpu.HBM)
-HALVES = 2
+HALVES = 1
 OTHER_VMEM = 45
 OWN_VMEM = 24
+HOME_VMEM = 48
 
 
 def dot(a, b, dims):
@@ -34,10 +35,10 @@
     )
 
 
-def picks_of(meta, flip, targets, last_start):
+def picks_of(meta, flip, steps, last_start):
     dec = lax.axis_index("dec")
     picks = []
-    for step in range(targets):
+    for step in steps:
         target = ((dec // 2) ^ step) * 2 + ((dec % 2) ^ flip)
         found, first = jnp.int32(-1), jnp.int32(0)
         for roll in range(meta.shape[1]):
@@ -49,6 +50,18 @@
     return picks
 
 
+def slab_copies(windows, picks, held, sem):
+    span = held.shape[0] // len(picks)
+    return [
+        pltpu.make_async_copy(
+            windows.at[jnp.maximum(found, 0), pl.ds(pl.multiple_of(start, ROW_TILE), span), :],
+            held.at[pl.ds(place * span, span), :],
+            sem.at[place],
+        )
+        for place, (found, start, _) in enumerate(picks)
+    ]
+
+
 def multiply(slabs, rows, product):
     for lane in range(0, product.shape[0], 2):
         result = dot(slabs[...], rows[lane * LANES : (lane + 2) * LANES, :], NT)
@@ -56,15 +69,14 @@
         product[lane + 1, :, :] = result[:, LANES:]
 
 
-def cut_rows(product, out, picks, first):
-    targets, frames, _ = out.shape
-    span = product.shape[1] // targets
+def cut_rows(product, outs, picks, first):
+    frames = outs[0].shape[0]
+    span = product.shape[1] // len(picks)
     for lane in range(product.shape[0]):
-        for step in range(targets):
-            found, _, shift = picks[step]
-            rows = product[lane, pl.ds(step * span + shift, frames), :]
+        for place, (found, _, shift) in enumerate(picks):
+            rows = product[lane, pl.ds(place * span + shift, frames), :]
             at = first + lane * LANES
-            out[step, :, at : at + LANES] = jnp.where(found >= 0, rows, 0.0).astype(BF16)
+            outs[place][:, at : at + LANES] = jnp.where(found >= 0, rows, 0.0).astype(BF16)
 
 
 def other_kernel(routes, windows, weight_hbm, out, own, weight, meta, slabs, *refs):
@@ -73,16 +85,6 @@
     span = slabs.shape[0] // targets
     last_start = windows.shape[1] - span
     columns = weight.shape[0] // PIECES
-
-    def slab_copies(flip, picks, held):
-        return [
-            pltpu.make_async_copy(
-                windows.at[jnp.maximum(found, 0), pl.ds(pl.multiple_of(start, ROW_TILE), span), :],
-                held.at[pl.ds(step * span, span), :],
-                sem.at[flip, step],
-            )
-            for step, (found, start, _) in enumerate(picks)
-        ]
 
     route_copy = pltpu.make_async_copy(routes, meta, meta_sem)
     route_copy.start()
@@ -92,9 +94,9 @@
         weights.append(pltpu.make_async_copy(weight_hbm.at[at, :], weight.at[at, :], weight_sem.at[piece]))
     weights[0].start()
     route_copy.wait()
-    picks = picks_of(meta, 1, targets, last_start)
-    copies = slab_copies(1, picks, slabs)
-    own_copies = slab_copies(0, picks_of(meta, 0, targets, last_start), own)
+    picks = picks_of(meta, 1, range(1, targets + 1), last_start)
+    copies = slab_copies(windows, picks, slabs, sem.at[1])
+    own_copies = slab_copies(windows, picks_of(meta, 0, range(1, targets + 1), last_start), own, sem.at[0])
     for copy in copies + weights[1:] + own_copies:
         copy.start()
     for copy in copies:
@@ -102,7 +104,7 @@
     for piece, copy in enumerate(weights):
         copy.wait()
         multiply(slabs, weight.at[pl.ds(piece * columns, columns), :], products[piece])
-        cut_rows(products[piece], out, picks, piece * columns)
+        cut_rows(products[piece], [out.at[place] for place in range(targets)], picks, piece * columns)
     for copy in own_copies:
         copy.wait()
 
@@ -110,7 +112,7 @@
 def adapter_other(frames, routes, windows, weight):
     _, _, d_local = windows.shape
     width = weight.shape[0]
-    targets = lax.axis_size("dec") // 2
+    targets = lax.axis_size("dec") // 2 - 1
     span = frames + ROW_TILE
     return pl.pallas_call(
         other_kernel,
@@ -144,16 +146,16 @@
     route_copy.start()
     multiply(slabs, weight.at[pl.ds(0, columns), :], products[0])
     route_copy.wait()
-    picks = picks_of(meta, 0, out.shape[0], last_start)
+    picks = picks_of(meta, 0, range(1, out.shape[0] + 1), last_start)
     for piece, product in enumerate(products):
         if piece:
             multiply(slabs, weight.at[pl.ds(piece * columns, columns), :], product)
-        cut_rows(product, out, picks, piece * columns)
+        cut_rows(product, [out.at[place] for place in range(out.shape[0])], picks, piece * columns)
 
 
 def adapter_own(frames, seq_len, routes, slabs, weight):
     width, d_local = weight.shape
-    targets = lax.axis_size("dec") // 2
+    targets = lax.axis_size("dec") // 2 - 1
     span = frames + ROW_TILE
     return pl.pallas_call(
         functools.partial(own_kernel, seq_len - span),
@@ -169,6 +171,42 @@
     )(routes, slabs, weight)
 
 
+def home_kernel(routes, windows, weight, other, own, meta, slabs, product, meta_sem, sem):
+    route_copy = pltpu.make_async_copy(routes, meta, meta_sem)
+    route_copy.start()
+    route_copy.wait()
+    last_start = windows.shape[1] - slabs.shape[0] // 2
+    picks = [picks_of(meta, flip, [0], last_start)[0] for flip in (1, 0)]
+    copies = slab_copies(windows, picks, slabs, sem)
+    for copy in copies:
+        copy.start()
+    for copy in copies:
+        copy.wait()
+    multiply(slabs, weight, product)
+    cut_rows(product, [other, own], picks, 0)
+
+
+def adapter_home(frames, routes, windows, weight):
+    width, d_local = weight.shape
+    span = frames + ROW_TILE
+    return pl.pallas_call(
+        home_kernel,
+        out_shape=[jax.ShapeDtypeStruct((frames, width), BF16)] * 2,
+        in_specs=[HBM] * 2 + [VMEM],
+        out_specs=[VMEM] * 2,
+        scratch_shapes=[
+            pltpu.SMEM(routes.shape, jnp.int32),
+            pltpu.VMEM((2 * span, d_local), BF16),
+            pltpu.VMEM((width // LANES, 2 * span, LANES), F32),
+            pltpu.SemaphoreType.DMA,
+            pltpu.SemaphoreType.DMA((2,)),
+        ],
+        compiler_params=pltpu.CompilerParams(vmem_limit_bytes=HOME_VMEM << 20),
+        cost_estimate=matmul_cost(1, 1, 1),
+        name="adapter_home",
+    )(routes, windows, weight)
+
+
 def pair_sum_kernel(own, other, *outs):
     targets, frames, _ = own.shape
     size = frames // HALVES
@@ -191,34 +229,56 @@
     return [outs[half * targets : (half + 1) * targets] for half in range(HALVES)]
 
 
-def swish_kernel(parts, first, valid, project, *refs):
-    blocks, outs, stream = refs[:parts], refs[parts:-1], refs[-1]
-    frames, width = stream.shape
-    c_local = outs[0].shape[1] // 2
+def plane_sum_kernel(*refs):
+    blocks, out = refs[:-1], refs[-1]
     total = blocks[0][...].astype(F32)
     for block in blocks[1:]:
         total = total + block[...].astype(F32)
+    out[...] = total
+
+
+def plane_sum(blocks):
+    return pl.pallas_call(
+        plane_sum_kernel,
+        out_shape=jax.ShapeDtypeStruct(blocks[0].shape, F32),
+        in_specs=[VMEM] * len(blocks),
+        out_specs=VMEM,
+        compiler_params=pltpu.CompilerParams(vmem_limit_bytes=24 << 20),
+        name="plane_sum",
+    )(*blocks)
+
+
+def swish_kernel(parts, first, valid, project, *refs):
+    homes, blocks, outs, stream = refs[:2], refs[2:parts], refs[parts:-1], refs[-1]
+    groups = len(outs) // 2
+    frames, width = stream.shape
+    c_local = outs[0].shape[1]
+    total = sum(home[first : first + frames, :].astype(F32) for home in homes)
+    for block in blocks:
+        total = total + block[...].astype(F32)
     rows = first + lax.broadcasted_iota(jnp.int32, (frames, width), 0)
     stream[...] = jnp.where(rows < valid[0], total, 0.0).astype(BF16)
-    for step, out in enumerate(outs):
-        at = pl.ds(pl.multiple_of(partner(step, len(outs)) * c_local, c_local), c_local)
-        out[:, :c_local] = stream[:, at].astype(out.dtype)
-        out[:, c_local:] = dot(stream[...], project[step], NN).astype(out.dtype)
-
-
-def swish(first, valid, project, blocks):
+    for step in range(groups):
+        at = pl.ds(pl.multiple_of(partner(step, groups) * c_local, c_local), c_local)
+        outs[step][...] = dot(stream[...], project[step], NN).astype(outs[step].dtype)
+        outs[groups + step][...] = stream[:, at].astype(outs[groups + step].dtype)
+
+
+def swish(first, valid, project, homes, blocks):
     frames, width = blocks[0].shape
+    blocks = homes + blocks
     groups, _, c_local = project.shape
-    return pl.pallas_call(
+    outs = pl.pallas_call(
         functools.partial(swish_kernel, len(blocks), first),
-        out_shape=[jax.ShapeDtypeStruct((frames, 2 * c_local), F32 if step == 0 else BF16) for step in range(groups)],
+        out_shape=[jax.ShapeDtypeStruct((frames, c_local), F32 if step == 0 else BF16) for step in range(groups)] * 2,
         in_specs=[SMEM, VMEM] + [VMEM] * len(blocks),
-        out_specs=[VMEM] * groups,
+        out_specs=[VMEM] * (2 * groups),
         scratch_shapes=[pltpu.VMEM((frames, width), BF16)],
         compiler_params=pltpu.CompilerParams(vmem_limit_bytes=24 << 20),
         cost_estimate=matmul_cost(frames, width, width),
         name="stream_and_swish",
     )(valid, project, *blocks)
+    return outs[:groups], outs[groups:]
 
 
 def spread_rows(padded, rows):
@@ -253,7 +313,7 @@
         in_specs=[VMEM] * 2,
         out_specs=[VMEM] * 2,
         compiler_params=pltpu.CompilerParams(vmem_limit_bytes=24 << 20),
-        cost_estimate=matmul_cost(128, width, 3 * c_local),
+        cost_estimate=matmul_cost(1, 1, 1),
         name="transposed_weights",
     )(expand, project)
 
@@ -300,20 +360,15 @@
 
 
 def backward_kernel(parts, valid, expand_t, taps_ref, value_ref, gate_ref, slope, *refs):
-    blocks, stream_out, outs, padded = refs[: parts * HALVES], refs[parts * HALVES], refs[parts * HALVES + 1 : -1], refs[-1]
-    frames, c_local = stream_out.shape
-    size = frames // HALVES
+    blocks, outs, padded = refs[:parts], refs[parts:-1], refs[-1]
+    frames, c_local = value_ref.shape
     taps = taps_ref.shape[0]
     half = (taps - 1) // 2
     edge = (padded.shape[0] - frames) // 2
-    spread_rows(padded, jnp.zeros((frames, c_local), F32))
-    for at in range(HALVES):
-        total = blocks[at * parts][...].astype(F32)
-        for block in blocks[at * parts + 1 : (at + 1) * parts]:
-            total = total + block[...].astype(F32)
-        rows = pl.ds(at * size, size)
-        stream_out[rows, :] = total[:, :c_local].astype(BF16)
-        padded[pl.ds(edge + at * size, size), :] = total[:, c_local:] * slope[rows, :]
+    total = blocks[0][...].astype(F32)
+    for block in blocks[1:]:
+        total = total + block[...].astype(F32)
+    spread_rows(padded, total * slope[...])
     grad = jnp.zeros((frames, c_local), F32)
     for tap in range(taps):
         grad = grad + taps_ref[tap : tap + 1, :] * padded[pl.ds(edge + half - tap, frames), :]
@@ -327,20 +382,19 @@
         out[...] = dot(grad_expanded, expand_t[step], NN).astype(out.dtype)
 
 
-def backward(valid, expand_t, taps, value, gate, slope, halves):
+def backward(valid, expand_t, taps, value, gate, slope, blocks):
     frames, c_local = value.shape
     groups = expand_t.shape[0]
     return pl.pallas_call(
         functools.partial(backward_kernel, groups),
-        out_shape=[jax.ShapeDtypeStruct((frames, c_local), BF16)]
-        + [jax.ShapeDtypeStruct((frames, c_local), F32 if step == 0 else BF16) for step in range(groups)],
-        in_specs=[SMEM] + [VMEM] * (5 + groups * HALVES),
-        out_specs=[VMEM] * (1 + groups),
+        out_shape=[jax.ShapeDtypeStruct((frames, c_local), F32 if step == 0 else BF16) for step in range(groups)],
+        in_specs=[SMEM] + [VMEM] * (5 + groups),
+        out_specs=[VMEM] * groups,
         scratch_shapes=[pltpu.VMEM((frames + 2 * edge_of(taps.shape[0]), c_local), F32)],
         compiler_params=pltpu.CompilerParams(vmem_limit_bytes=16 << 20),
         cost_estimate=matmul_cost(frames, 2 * c_local, c_local * groups),
         name="backward_module",
-    )(valid, expand_t, taps, value, gate, slope, *[block for half in halves for block in half])
+    )(valid, expand_t, taps, value, gate, slope, *blocks)
 
 
 def partner(step, groups):
@@ -368,15 +422,17 @@
     held, mask = block, count // 2
     while mask:
         arrived = swap(held, "ch", count, mask)
-        if held is block:
-            pass
         held = jnp.concatenate([held, arrived], axis=0)
         mask //= 2
     return held, later
 
 
+def summed(blocks):
+    return sum(block.astype(F32) for block in blocks).astype(BF16)
+
+
 def plane_exchange(blocks, count):
-    return [blocks[0]] + [swap(block, "dec", count, 2 * step) for step, block in enumerate(blocks) if step]
+    return [swap(block, "dec", count, 2 * step) for step, block in enumerate(blocks, 1)]
 
 
 def body(
@@ -406,21 +462,19 @@
     for_other, own_slabs, weight = adapter_other(frames, routes, frame_cotangent, adapter_weight)
     from_other = swap(for_other, "dec", n_dec, 1)
     own = adapter_own(frames, seq_len, routes, own_slabs, weight)
-    first, second = pair_sum(own, from_other)
-    first, own_input = lax.optimization_barrier((first, normed_input.reshape(frames, c_local)))
-    arrived = [plane_exchange(first, n_dec)]
-    inputs, second = z_gather(own_input, n_ch, second)
-    arrived[0], second = lax.optimization_barrier((arrived[0], second))
-    arrived.append(plane_exchange(second, n_dec))
+    (sums,) = pair_sum(own, from_other)
+    sums, routes, own_input = lax.optimization_barrier((sums, routes, normed_input.reshape(frames, c_local)))
+    arrived = plane_exchange(sums, n_dec)
+    home_other, home_own = adapter_home(frames, routes, frame_cotangent, weight)
+    homes = [home_own, swap(home_other, "dec", n_dec, 1)]
+    inputs, _ = z_gather(own_input, n_ch, taps)
     expand_t, project_t = transposed(n_ch, expand, project_weight)
     value, gate, slope = forward(frames, utterance_frames, expand, taps, scale, shift, inputs)
-    value, gate, slope, project_t = lax.optimization_barrier((value, gate, slope, project_t))
-    halves = []
-    for at, half in enumerate(arrived):
-        halves.append(z_exchange(swish(at * frames // HALVES, utterance_frames, project_t, half)))
-    stream, *parts = backward(utterance_frames, expand_t, taps, value, gate, slope, halves)
-    total = sum(part.astype(F32) for part in z_exchange(parts))
-    return stream[None], total.astype(BF16)[None]
+    swish_parts, stream_parts = swish(0, utterance_frames, project_t, homes, [plane_sum(arrived)])
+    swish_parts = z_exchange(swish_parts)
+    stream_parts = z_exchange(stream_parts)
+    parts = z_exchange(backward(utterance_frames, expand_t, taps, value, gate, slope, swish_parts))
+    return summed(stream_parts)[None], summed(parts)[None]
 
 
 def solution(mesh):

time: 51.4 us -> 48.7 us (0.947)
  waiting for transfers between devices: 9.91 us -> 6.8 us
  starting transfers between devices: 25.8 us -> 24.6 us
  Pallas kernels: 12.4 us -> 13.3 us
  other arithmetic: 1.37 us -> 2.05 us
    ppermute x9, waiting for transfers between devices: 6.53 us -> 2.7 us  [turn(): lax.ppermute(block, 'ch', [(i, (i + step) % count) for i in range(count)])]
    ppermute x9 -> x7, starting transfers between devices: 12.2 us -> 8.62 us  [swap(): return lax.ppermute(block, axis, [(i, i ^ mask) for i in range(count)])]
    pallas_call x0 -> x2, Pallas kernels: none -> 3.49 us  [the longest x1 3.4 us: adapter_home(): pl.pallas_call(home_kernel, out_shape=[jax.ShapeDtypeStruct((frames, widt...]
    ppermute x9, starting transfers between devices: 13.6 us -> 16 us  [turn(): lax.ppermute(block, 'ch', [(i, (i + step) % count) for i in range(count)])]
    pallas_call x1, Pallas kernels: 5.6 us -> 4.72 us  [adapter_other(): pl.pallas_call(other_kernel, out_shape=[jax.ShapeDtypeStruct((targets, fr...]
    ppermute x9 -> x7, waiting for transfers between devices: 3.38 us -> 4.1 us  [swap(): return lax.ppermute(block, axis, [(i, i ^ mask) for i in range(count)])]
    pallas_call x1, Pallas kernels: 3.12 us -> 2.42 us  [adapter_own(): pl.pallas_call(functools.partial(own_kernel, seq_len - span), out_shape=j...]
    broadcast_in_dim x1 -> x2, other arithmetic: 0.66 us -> 1.33 us  [body(): return (summed(stream_parts)[None], summed(parts)[None])]
  transfers between devices with their start and end apart: 18 -> 16, of which waited for: 7 -> 4; matrix products, arithmetic and copies ran while one was open for 0% -> 2% of each run, Pallas kernels for 11% -> 17%
where the time goes in v4:
time: 48.7 us; the launch traced here: 48.5 us
  starting transfers between devices  24.6 us (51%)
  Pallas kernels  13.3 us (27%)
  waiting for transfers between devices  6.8 us (14%)
  other arithmetic  2.05 us (4%)
  between operations  1.52 us (3%)
    ppermute x9, starting transfers between devices, turn(): lax.ppermute(block, 'ch', [(i, (i + step) % count) for i in range(count)])  16 us
    ppermute x7, starting transfers between devices, swap(): return lax.ppermute(block, axis, [(i, i ^ mask) for i in range(count)])  8.62 us
    pallas_call x1, Pallas kernels, adapter_other(): pl.pallas_call(other_kernel, out_shape=[jax.ShapeDtypeStruct((targets, fr...  4.72 us
    ppermute x7, waiting for transfers between devices, swap(): return lax.ppermute(block, axis, [(i, i ^ mask) for i in range(count)])  4.1 us
    pallas_call x1, Pallas kernels, adapter_home(): pl.pallas_call(home_kernel, out_shape=[jax.ShapeDtypeStruct((frames, widt...  3.4 us
    ppermute x9, waiting for transfers between devices, turn(): lax.ppermute(block, 'ch', [(i, (i + step) % count) for i in range(count)])  2.7 us
    pallas_call x1, Pallas kernels, adapter_own(): pl.pallas_call(functools.partial(own_kernel, seq_len - span), out_shape=j...  2.42 us
    broadcast_in_dim x2, other arithmetic, body(): return (summed(stream_parts)[None], summed(parts)[None])  1.33 us
  transfers between devices with their start and end apart: 16, of which 4 were waited for; matrix products, arithmetic and copies ran while one was open for 2% of the time, Pallas kernels for 17%

profile of v4, /device:TPU:0, one launch (start us, length us, event | category | flops | bytes accessed | tf_op | source)
XLA Modules:
  0.0 48.5 jit_solution(18329809561683689)
XLA Ops:
  0.6 0.7 %pad_add_fusion.routes = s32[2,8]{1,0:T(2,128)S(1)} fusion(s32[1,8]{1,0:T(1,128)} %bitcast.19, s32[1,8]{1,0:T(1,128)} %bitcast.20), kind=kLoop, calls=%fused_computation.6 | loop fusion | flops 16 | bytes 128 | tf_op jit(solution)/shard_map/stack | solution.py:461
  1.3 4.7 %adapter_other.1 = (bf16[3,128,1024]{2,1,0:T(8,128)(2,1)S(1)}, bf16[432,2048]{1,0:T(8,128)(2,1)S(1)}, bf16[1024,2048]{1,0:T(8,128)(2,1)S(1)}) custom-call(s32[2,8]{1,0:T(2,128)S(1)} %pad_add_fusion.routes, bf16[8,160,2048]{2,1,0:T(8,128)(2,1)} %windows.3, bf16[1024,2048]{1,0:T(8,128)(2,1)} %weight_hbm.1), custom_call_target="tpu_custom_call" | custom-call | flops 1811939328 | bytes 6848512 | tf_op jit(solution)/shard_map/adapter_other/pallas_call | solution.py:117
  6.0 0.5 %collective-permute-start = (bf16[3,128,1024]{2,1,0:T(8,128)(2,1)S(1)}, bf16[3,128,1024]{2,1,0:T(8,128)(2,1)S(1)}, u32[]{:S(2)}, u32[]{:S(2)}) collective-permute-start(bf16[3,128,1024]{2,1,0:T(8,128)(2,1)S(1)} %get-tuple-element.35), channel_id=1, source_target_pairs={{0,4},{4,0},{8,12},{12,8},{16,20},{20,16},{24,28},{28,24},{1,5},{5... | collective-permute-start | bytes 2359304 | tf_op jit(solution)/shard_map/ppermute | solution.py:405
  6.6 2.4 %adapter_own.1.own = bf16[3,128,1024]{2,1,0:T(8,128)(2,1)S(1)} custom-call(s32[2,8]{1,0:T(2,128)S(1)} %pad_add_fusion.routes, bf16[432,2048]{1,0:T(8,128)(2,1)S(1)} %get-tuple-element.33.slabs, bf16[1024,2048]{1,0:T(8,128)(2,1)S(1)} %get-tuple-element.34.weight), custom_call_target="tpu_custom_call" | custom-call | flops 2 | bytes 6 | tf_op jit(solution)/shard_map/adapter_own/pallas_call | solution.py:160
  9.0 0.2 pair_sum.1
  9.2 2.6 %collective-permute-start.2 = (bf16[128,1024]{1,0:T(8,128)(2,1)S(1)}, bf16[128,1024]{1,0:T(8,128)(2,1)S(1)}, u32[]{:S(2)}, u32[]{:S(2)}) collective-permute-start(bf16[128,1024]{1,0:T(8,128)(2,1)S(1)} %get-tuple-element.42), channel_id=1, source_target_pairs={{0,8},{4,12},{8,0},{12,4},{16,24},{20,28},{24,16},{28,20},{1,9},{5... | collective-permute-start | bytes 786440 | tf_op jit(solution)/shard_map/ppermute | solution.py:405
  11.8 1.5 %collective-permute-start.3 = (bf16[128,1024]{1,0:T(8,128)(2,1)S(1)}, bf16[128,1024]{1,0:T(8,128)(2,1)S(1)}, u32[]{:S(2)}, u32[]{:S(2)}) collective-permute-start(bf16[128,1024]{1,0:T(8,128)(2,1)S(1)} %get-tuple-element.43), channel_id=1, source_target_pairs={{0,16},{4,20},{8,24},{12,28},{16,0},{20,4},{24,8},{28,12},{1,17},{... | collective-permute-start | bytes 786440 | tf_op jit(solution)/shard_map/ppermute | solution.py:405
  13.3 0.0 collective-permute-start.4
  13.3 3.4 %adapter_home.1 = (bf16[128,1024]{1,0:T(8,128)(2,1)S(1)}, bf16[128,1024]{1,0:T(8,128)(2,1)S(1)}) custom-call(s32[2,8]{1,0:T(2,128)S(1)} %pad_add_fusion.routes, bf16[8,160,2048]{2,1,0:T(8,128)(2,1)} %windows.3, bf16[1024,2048]{1,0:T(8,128)(2,1)S(1)} %get-tuple-element.34.weight), custom_call_target="tpu_custom_call" | custom-call | flops 2 | bytes 6 | tf_op jit(solution)/shard_map/adapter_home/pallas_call | solution.py:192
  16.8 0.1 collective-permute-start.1
  16.8 3.1 %collective-permute-start.8 = (bf16[128,256]{1,0:T(8,128)(2,1)S(1)}, bf16[128,256]{1,0:T(8,128)(2,1)S(1)}, u32[]{:S(2)}, u32[]{:S(2)}) collective-permute-start(bf16[128,256]{1,0:T(8,128)(2,1)S(1)} %bitcast.16), channel_id=1, source_target_pairs={{0,2},{1,3},{2,0},{3,1},{4,6},{5,7},{6,4},{7,5},{8,10},{9,11},{10,... | collective-permute-start | bytes 196616 | tf_op jit(solution)/shard_map/ppermute | solution.py:405
  19.9 4.1 %collective-permute-done.8 = bf16[128,256]{1,0:T(8,128)(2,1)S(1)} collective-permute-done((bf16[128,256]{1,0:T(8,128)(2,1)S(1)}, bf16[128,256]{1,0:T(8,128)(2,1)S(1)}, u32[]{:S(2)}, u32[]{:S(2)}) %collective-permute-start.8) | collective-permute-done | bytes 65568 | tf_op jit(solution)/shard_map/ppermute | solution.py:405
  24.0 0.8 %collective-permute-start.9 = (bf16[256,256]{1,0:T(8,128)(2,1)S(1)}, bf16[256,256]{1,0:T(8,128)(2,1)S(1)}, u32[]{:S(2)}, u32[]{:S(2)}) collective-permute-start(bf16[256,256]{1,0:T(8,128)(2,1)S(1)} %pad_maximum_fusion.1), channel_id=1, source_target_pairs={{0,1},{1,0},{2,3},{3,2},{4,5},{5,4},{6,7},{7,6},{8,9},{9,8},{10,11... | collective-permute-start | bytes 393224 | tf_op jit(solution)/shard_map/ppermute | solution.py:405
  24.9 0.2 copy.13
  25.2 0.9 %transposed_weights.1 = (bf16[4,512,256]{2,1,0:T(8,128)(2,1)S(1)}, bf16[4,1024,256]{2,1,0:T(8,128)(2,1)S(1)}) custom-call(bf16[1024,512]{1,0:T(8,128)(2,1)S(1)} %bitcast.11, bf16[1024,1024]{1,0:T(8,128)(2,1)S(1)} %copy-done), custom_call_target="tpu_custom_call" | custom-call | flops 2 | bytes 6 | tf_op jit(solution)/shard_map/transposed_weights/pallas_call | solution.py:307
  26.7 0.1 plane_sum.1.refs_2_
  26.8 0.5 %stream_and_swish.1 = (f32[128,256]{1,0:T(8,128)S(1)}, bf16[128,256]{1,0:T(8,128)(2,1)S(1)}, bf16[128,256]{1,0:T(8,128)(2,1)S(1)}, bf16[128,256]{1,0:T(8,128)(2,...) custom-call(s32[1]{0:T(128)S(6)} %copy.14.valid, ...), custom_call_target="tpu_custom_call" | custom-call | flops 268435456 | bytes 2621440 | tf_op jit(solution)/shard_map/stream_and_swish/pallas_call | solution.py:271
  27.3 3.4 %collective-permute-start.10 = (bf16[128,256]{1,0:T(8,128)(2,1)S(1)}, bf16[128,256]{1,0:T(8,128)(2,1)S(1)}, u32[]{:S(2)}, u32[]{:S(2)}) collective-permute-start(bf16[128,256]{1,0:T(8,128)(2,1)S(1)} %get-tuple-element.55), channel_id=1, source_target_pairs={{0,2},{1,3},{2,0},{3,1},{4,6},{5,7},{6,4},{7,5},{8,10},{9,11},{10,... | collective-permute-start | bytes 196616 | tf_op jit(solution)/shard_map/ppermute | solution.py:413
  30.8 0.0 collective-permute-start.11
  30.8 3.8 %collective-permute-start.12 = (bf16[128,256]{1,0:T(8,128)(2,1)S(1)}, bf16[128,256]{1,0:T(8,128)(2,1)S(1)}, u32[]{:S(2)}, u32[]{:S(2)}) collective-permute-start(bf16[128,256]{1,0:T(8,128)(2,1)S(1)} %get-tuple-element.57), channel_id=1, source_target_pairs={{0,3},{1,0},{2,1},{3,2},{4,7},{5,4},{6,5},{7,6},{8,11},{9,8},{10,9... | collective-permute-start | bytes 196616 | tf_op jit(solution)/shard_map/ppermute | solution.py:413
  34.6 0.6 %collective-permute-start.6 = (bf16[128,256]{1,0:T(8,128)(2,1)S(1)}, bf16[128,256]{1,0:T(8,128)(2,1)S(1)}, u32[]{:S(2)}, u32[]{:S(2)}) collective-permute-start(bf16[128,256]{1,0:T(8,128)(2,1)S(1)} %get-tuple-element.47), channel_id=1, source_target_pairs={{0,1},{1,2},{2,3},{3,0},{4,5},{5,6},{6,7},{7,4},{8,9},{9,10},{10,1... | collective-permute-start | bytes 196616 | tf_op jit(solution)/shard_map/ppermute | solution.py:413
  35.2 3.3 %collective-permute-start.7 = (bf16[128,256]{1,0:T(8,128)(2,1)S(1)}, bf16[128,256]{1,0:T(8,128)(2,1)S(1)}, u32[]{:S(2)}, u32[]{:S(2)}) collective-permute-start(bf16[128,256]{1,0:T(8,128)(2,1)S(1)} %get-tuple-element.48), channel_id=1, source_target_pairs={{0,3},{1,0},{2,1},{3,2},{4,7},{5,4},{6,5},{7,6},{8,11},{9,8},{10,9... | collective-permute-start | bytes 196616 | tf_op jit(solution)/shard_map/ppermute | solution.py:413
  38.5 0.6 %forward_gates.1 = (f32[128,256]{1,0:T(8,128)S(1)}, f32[128,256]{1,0:T(8,128)S(1)}, f32[128,256]{1,0:T(8,128)S(1)}) custom-call(s32[1]{0:T(128)S(6)} %copy.14.valid, bf16[1024,512]{1,0:T(8,128)(2,1)S(1)} %bitcast.12, f32[9,256]{1,0:T(8,128)S(1)} %convert_element_type.31.taps_ref, f32[1,256]{1,0:T(1,128)S(1)} %bitcast.13, f32[1,256]{1,0:T(1,128)S(1)} %bitcast.14, ...), custom_call_target="tpu_custom_call" | custom-call | flops 134217728 | bytes 1441792 | tf_op jit(solution)/shard_map/forward_gates/pallas_call | solution.py:350
  39.1 0.5 %backward_module.1 = (f32[128,256]{1,0:T(8,128)S(1)}, bf16[128,256]{1,0:T(8,128)(2,1)S(1)}, bf16[128,256]{1,0:T(8,128)(2,1)S(1)}, bf16[128,256]{1,0:T(8,128)(2,1)S(1)}) custom-call(s32[1]{0:T(128)S(6)} %copy.14.valid, bf16[4,512,256]{2,1,0:T(8,128)(2,1)S(1)} %get-tuple-element.49.expand_t, f32[9,256]{1,0:T(8,128)S(1)} %convert_element_type.31.taps_ref, ...), custom_call_target="tpu_custom_call" | custom-call | flops 134217728 | bytes 1441792 | tf_op jit(solution)/shard_map/backward_module/pallas_call | solution.py:388
  39.6 1.2 %collective-permute-start.13 = (bf16[128,256]{1,0:T(8,128)(2,1)S(1)}, bf16[128,256]{1,0:T(8,128)(2,1)S(1)}, u32[]{:S(2)}, u32[]{:S(2)}) collective-permute-start(bf16[128,256]{1,0:T(8,128)(2,1)S(1)} %get-tuple-element.59), channel_id=1, source_target_pairs={{0,2},{1,3},{2,0},{3,1},{4,6},{5,7},{6,4},{7,5},{8,10},{9,11},{10,... | collective-permute-start | bytes 196616 | tf_op jit(solution)/shard_map/ppermute | solution.py:413
  40.8 1.5 %collective-permute-start.14 = (bf16[128,256]{1,0:T(8,128)(2,1)S(1)}, bf16[128,256]{1,0:T(8,128)(2,1)S(1)}, u32[]{:S(2)}, u32[]{:S(2)}) collective-permute-start(bf16[128,256]{1,0:T(8,128)(2,1)S(1)} %get-tuple-element.60), channel_id=1, source_target_pairs={{0,1},{1,2},{2,3},{3,0},{4,5},{5,6},{6,7},{7,4},{8,9},{9,10},{10,1... | collective-permute-start | bytes 196616 | tf_op jit(solution)/shard_map/ppermute | solution.py:413
  42.3 0.2 collective-permute-done.5
  42.5 2.2 %collective-permute-start.15 = (bf16[128,256]{1,0:T(8,128)(2,1)S(1)}, bf16[128,256]{1,0:T(8,128)(2,1)S(1)}, u32[]{:S(2)}, u32[]{:S(2)}) collective-permute-start(bf16[128,256]{1,0:T(8,128)(2,1)S(1)} %get-tuple-element.61), channel_id=1, source_target_pairs={{0,3},{1,0},{2,1},{3,2},{4,7},{5,4},{6,5},{7,6},{8,11},{9,8},{10,9... | collective-permute-start | bytes 196616 | tf_op jit(solution)/shard_map/ppermute | solution.py:413
  44.7 0.7 %fusion = bf16[1,128,256]{2,1,0:T(8,128)(2,1)} fusion(bf16[128,256]{1,0:T(8,128)(2,1)S(1)} %collective-permute-done.7, bf16[128,256]{1,0:T(8,128)(2,1)S(1)} %collective-permute-done.6, f32[128,256]{1,0:T(8,128)S(1)} %get-tuple-element.45, bf16[128,256]{1,0:T(8,128)(2,1)S(1)} %collective-permute-done.5), kind=kLoop, calls=%fused_computation.4 | loop fusion | flops 229376 | bytes 393216 | tf_op jit(solution)/shard_map/broadcast_in_dim | solution.py:477
  45.4 2.1 %collective-permute-done.13 = bf16[128,256]{1,0:T(8,128)(2,1)S(1)} collective-permute-done((bf16[128,256]{1,0:T(8,128)(2,1)S(1)}, bf16[128,256]{1,0:T(8,128)(2,1)S(1)}, u32[]{:S(2)}, u32[]{:S(2)}) %collective-permute-start.13) | collective-permute-done | bytes 65568 | tf_op jit(solution)/shard_map/ppermute | solution.py:413
  47.4 0.4 collective-permute-done.15
  47.8 0.7 %fusion.1 = bf16[1,128,256]{2,1,0:T(8,128)(2,1)} fusion(bf16[128,256]{1,0:T(8,128)(2,1)S(1)} %collective-permute-done.15, bf16[128,256]{1,0:T(8,128)(2,1)S(1)} %collective-permute-done.14, f32[128,256]{1,0:T(8,128)S(1)} %get-tuple-element.58, bf16[128,256]{1,0:T(8,128)(2,1)S(1)} %collective-permute-done.13), kind=kLoop, calls=%fused_computation.5 | loop fusion | flops 229376 | bytes 393216 | tf_op jit(solution)/shard_map/broadcast_in_dim | solution.py:477
  (28 shorter events, 0.1 us)
Async XLA Ops:
  6.0 2.9 %collective-permute-start = (bf16[3,128,1024]{2,1,0:T(8,128)(2,1)S(1)}, bf16[3,128,1024]{2,1,0:T(8,128)(2,1)S(1)}, u32[]{:S(2)}, u32[]{:S(2)}) collective-permute-start(bf16[3,128,1024]{2,1,0:T(8,128)(2,1)S(1)} %get-tuple-element.35), channel_id=1, source_target_pairs={{0,4},{4,0},{8,12},{12,8},{16,20},{20,16},{24,28},{28,24},{1,5},{5... | collective-permute-start | bytes 2359304 | tf_op jit(solution)/shard_map/ppermute | solution.py:405
  9.2 7.6 %copy-start.4 = (bf16[1,128,256]{2,1,0:T(8,128)(2,1)S(1)}, bf16[1,128,256]{2,1,0:T(8,128)(2,1)}, u32[]{:S(2)}) copy-start(bf16[1,128,256]{2,1,0:T(8,128)(2,1)} %param.15) | copy-start | bytes 196612
  9.2 15.7 %copy-start.3 = (bf16[1024,2,256]{2,1,0:T(2,128)(2,1)S(1)}, bf16[1024,2,256]{2,1,0:T(2,128)(2,1)}, u32[]{:S(2)}) copy-start(bf16[1024,2,256]{2,1,0:T(2,128)(2,1)} %param.16) | copy-start | bytes 3145732
  9.2 15.9 %copy-start = (bf16[1024,1024]{1,0:T(8,128)(2,1)S(1)}, bf16[1024,1024]{1,0:T(8,128)(2,1)}, u32[]{:S(2)}) copy-start(bf16[1024,1024]{1,0:T(8,128)(2,1)} %project.1) | copy-start | bytes 6291460
  9.2 17.5 %collective-permute-start.2 = (bf16[128,1024]{1,0:T(8,128)(2,1)S(1)}, bf16[128,1024]{1,0:T(8,128)(2,1)S(1)}, u32[]{:S(2)}, u32[]{:S(2)}) collective-permute-start(bf16[128,1024]{1,0:T(8,128)(2,1)S(1)} %get-tuple-element.42), channel_id=1, source_target_pairs={{0,8},{4,12},{8,0},{12,4},{16,24},{20,28},{24,16},{28,20},{1,9},{5... | collective-permute-start | bytes 786440 | tf_op jit(solution)/shard_map/ppermute | solution.py:405
  11.8 14.9 %collective-permute-start.3 = (bf16[128,1024]{1,0:T(8,128)(2,1)S(1)}, bf16[128,1024]{1,0:T(8,128)(2,1)S(1)}, u32[]{:S(2)}, u32[]{:S(2)}) collective-permute-start(bf16[128,1024]{1,0:T(8,128)(2,1)S(1)} %get-tuple-element.43), channel_id=1, source_target_pairs={{0,16},{4,20},{8,24},{12,28},{16,0},{20,4},{24,8},{28,12},{1,17},{... | collective-permute-start | bytes 786440 | tf_op jit(solution)/shard_map/ppermute | solution.py:405
  13.3 13.4 %collective-permute-start.4 = (bf16[128,1024]{1,0:T(8,128)(2,1)S(1)}, bf16[128,1024]{1,0:T(8,128)(2,1)S(1)}, u32[]{:S(2)}, u32[]{:S(2)}) collective-permute-start(bf16[128,1024]{1,0:T(8,128)(2,1)S(1)} %get-tuple-element.44), channel_id=1, source_target_pairs={{0,24},{4,28},{8,16},{12,20},{16,8},{20,12},{24,0},{28,4},{1,25},{... | collective-permute-start | bytes 786440 | tf_op jit(solution)/shard_map/ppermute | solution.py:405
  16.8 10.1 %collective-permute-start.1 = (bf16[128,1024]{1,0:T(8,128)(2,1)S(1)}, bf16[128,1024]{1,0:T(8,128)(2,1)S(1)}, u32[]{:S(2)}, u32[]{:S(2)}) collective-permute-start(bf16[128,1024]{1,0:T(8,128)(2,1)S(1)} %get-tuple-element.41), channel_id=1, source_target_pairs={{0,4},{4,0},{8,12},{12,8},{16,20},{20,16},{24,28},{28,24},{1,5},{5... | collective-permute-start | bytes 786440 | tf_op jit(solution)/shard_map/ppermute | solution.py:405
  16.8 7.2 %collective-permute-start.8 = (bf16[128,256]{1,0:T(8,128)(2,1)S(1)}, bf16[128,256]{1,0:T(8,128)(2,1)S(1)}, u32[]{:S(2)}, u32[]{:S(2)}) collective-permute-start(bf16[128,256]{1,0:T(8,128)(2,1)S(1)} %bitcast.16), channel_id=1, source_target_pairs={{0,2},{1,3},{2,0},{3,1},{4,6},{5,7},{6,4},{7,5},{8,10},{9,11},{10,... | collective-permute-start | bytes 196616 | tf_op jit(solution)/shard_map/ppermute | solution.py:405
  24.0 10.6 %collective-permute-start.9 = (bf16[256,256]{1,0:T(8,128)(2,1)S(1)}, bf16[256,256]{1,0:T(8,128)(2,1)S(1)}, u32[]{:S(2)}, u32[]{:S(2)}) collective-permute-start(bf16[256,256]{1,0:T(8,128)(2,1)S(1)} %pad_maximum_fusion.1), channel_id=1, source_target_pairs={{0,1},{1,0},{2,3},{3,2},{4,5},{5,4},{6,7},{7,6},{8,9},{9,8},{10,11... | collective-permute-start | bytes 393224 | tf_op jit(solution)/shard_map/ppermute | solution.py:405
  25.1 5.7 %copy-start.5 = (bf16[9,256]{1,0:T(8,128)(2,1)S(1)}, bf16[9,256]{1,0:T(8,128)(2,1)}, u32[]{:S(2)}) copy-start(bf16[9,256]{1,0:T(8,128)(2,1)} %param.17) | copy-start | bytes 13828
  25.1 13.4 %copy-start.1 = (f32[256]{0:T(256)S(1)}, f32[256]{0:T(256)}, u32[]{:S(2)}) copy-start(f32[256]{0:T(256)} %param.18) | copy-start | bytes 3076
  25.1 13.4 %copy-start.2 = (f32[256]{0:T(256)S(1)}, f32[256]{0:T(256)}, u32[]{:S(2)}) copy-start(f32[256]{0:T(256)} %param.19) | copy-start | bytes 3076
  27.3 7.8 %collective-permute-start.10 = (bf16[128,256]{1,0:T(8,128)(2,1)S(1)}, bf16[128,256]{1,0:T(8,128)(2,1)S(1)}, u32[]{:S(2)}, u32[]{:S(2)}) collective-permute-start(bf16[128,256]{1,0:T(8,128)(2,1)S(1)} %get-tuple-element.55), channel_id=1, source_target_pairs={{0,2},{1,3},{2,0},{3,1},{4,6},{5,7},{6,4},{7,5},{8,10},{9,11},{10,... | collective-permute-start | bytes 196616 | tf_op jit(solution)/shard_map/ppermute | solution.py:413
  30.8 8.3 %collective-permute-start.11 = (bf16[128,256]{1,0:T(8,128)(2,1)S(1)}, bf16[128,256]{1,0:T(8,128)(2,1)S(1)}, u32[]{:S(2)}, u32[]{:S(2)}) collective-permute-start(bf16[128,256]{1,0:T(8,128)(2,1)S(1)} %get-tuple-element.56), channel_id=1, source_target_pairs={{0,1},{1,2},{2,3},{3,0},{4,5},{5,6},{6,7},{7,4},{8,9},{9,10},{10,1... | collective-permute-start | bytes 196616 | tf_op jit(solution)/shard_map/ppermute | solution.py:413
  30.8 8.3 %collective-permute-start.12 = (bf16[128,256]{1,0:T(8,128)(2,1)S(1)}, bf16[128,256]{1,0:T(8,128)(2,1)S(1)}, u32[]{:S(2)}, u32[]{:S(2)}) collective-permute-start(bf16[128,256]{1,0:T(8,128)(2,1)S(1)} %get-tuple-element.57), channel_id=1, source_target_pairs={{0,3},{1,0},{2,1},{3,2},{4,7},{5,4},{6,5},{7,6},{8,11},{9,8},{10,9... | collective-permute-start | bytes 196616 | tf_op jit(solution)/shard_map/ppermute | solution.py:413
  34.6 7.9 %collective-permute-start.5 = (bf16[128,256]{1,0:T(8,128)(2,1)S(1)}, bf16[128,256]{1,0:T(8,128)(2,1)S(1)}, u32[]{:S(2)}, u32[]{:S(2)}) collective-permute-start(bf16[128,256]{1,0:T(8,128)(2,1)S(1)} %get-tuple-element.46), channel_id=1, source_target_pairs={{0,2},{1,3},{2,0},{3,1},{4,6},{5,7},{6,4},{7,5},{8,10},{9,11},{10,... | collective-permute-start | bytes 196616 | tf_op jit(solution)/shard_map/ppermute | solution.py:413
  34.6 10.1 %collective-permute-start.6 = (bf16[128,256]{1,0:T(8,128)(2,1)S(1)}, bf16[128,256]{1,0:T(8,128)(2,1)S(1)}, u32[]{:S(2)}, u32[]{:S(2)}) collective-permute-start(bf16[128,256]{1,0:T(8,128)(2,1)S(1)} %get-tuple-element.47), channel_id=1, source_target_pairs={{0,1},{1,2},{2,3},{3,0},{4,5},{5,6},{6,7},{7,4},{8,9},{9,10},{10,1... | collective-permute-start | bytes 196616 | tf_op jit(solution)/shard_map/ppermute | solution.py:413
  35.2 9.5 %collective-permute-start.7 = (bf16[128,256]{1,0:T(8,128)(2,1)S(1)}, bf16[128,256]{1,0:T(8,128)(2,1)S(1)}, u32[]{:S(2)}, u32[]{:S(2)}) collective-permute-start(bf16[128,256]{1,0:T(8,128)(2,1)S(1)} %get-tuple-element.48), channel_id=1, source_target_pairs={{0,3},{1,0},{2,1},{3,2},{4,7},{5,4},{6,5},{7,6},{8,11},{9,8},{10,9... | collective-permute-start | bytes 196616 | tf_op jit(solution)/shard_map/ppermute | solution.py:413
  39.6 7.9 %collective-permute-start.13 = (bf16[128,256]{1,0:T(8,128)(2,1)S(1)}, bf16[128,256]{1,0:T(8,128)(2,1)S(1)}, u32[]{:S(2)}, u32[]{:S(2)}) collective-permute-start(bf16[128,256]{1,0:T(8,128)(2,1)S(1)} %get-tuple-element.59), channel_id=1, source_target_pairs={{0,2},{1,3},{2,0},{3,1},{4,6},{5,7},{6,4},{7,5},{8,10},{9,11},{10,... | collective-permute-start | bytes 196616 | tf_op jit(solution)/shard_map/ppermute | solution.py:413
  40.8 6.7 %collective-permute-start.14 = (bf16[128,256]{1,0:T(8,128)(2,1)S(1)}, bf16[128,256]{1,0:T(8,128)(2,1)S(1)}, u32[]{:S(2)}, u32[]{:S(2)}) collective-permute-start(bf16[128,256]{1,0:T(8,128)(2,1)S(1)} %get-tuple-element.60), channel_id=1, source_target_pairs={{0,1},{1,2},{2,3},{3,0},{4,5},{5,6},{6,7},{7,4},{8,9},{9,10},{10,1... | collective-permute-start | bytes 196616 | tf_op jit(solution)/shard_map/ppermute | solution.py:413
  42.5 5.3 %collective-permute-start.15 = (bf16[128,256]{1,0:T(8,128)(2,1)S(1)}, bf16[128,256]{1,0:T(8,128)(2,1)S(1)}, u32[]{:S(2)}, u32[]{:S(2)}) collective-permute-start(bf16[128,256]{1,0:T(8,128)(2,1)S(1)} %get-tuple-element.61), channel_id=1, source_target_pairs={{0,3},{1,0},{2,1},{3,2},{4,7},{5,4},{6,5},{7,6},{8,11},{9,8},{10,9... | collective-permute-start | bytes 196616 | tf_op jit(solution)/shard_map/ppermute | solution.py:413

commit v5 on v4

--- a/solution.py
+++ b/solution.py
@@ -20,7 +20,6 @@
 HALVES = 1
 OTHER_VMEM = 45
 OWN_VMEM = 24
-HOME_VMEM = 48
 
 
 def dot(a, b, dims):
@@ -79,7 +78,7 @@
             outs[place][:, at : at + LANES] = jnp.where(found >= 0, rows, 0.0).astype(BF16)
 
 
-def other_kernel(routes, windows, weight_hbm, out, own, weight, meta, slabs, *refs):
+def other_kernel(routes, windows, weight_hbm, out, own, home, weight, meta, slabs, *refs):
     products, (meta_sem, sem, weight_sem) = refs[:PIECES], refs[PIECES:]
     targets = out.shape[0]
     span = slabs.shape[0] // targets
@@ -97,6 +96,8 @@
     picks = picks_of(meta, 1, range(1, targets + 1), last_start)
     copies = slab_copies(windows, picks, slabs, sem.at[1])
     own_copies = slab_copies(windows, picks_of(meta, 0, range(1, targets + 1), last_start), own, sem.at[0])
+    home_picks = [picks_of(meta, flip, [0], last_start)[0] for flip in (1, 0)]
+    own_copies += slab_copies(windows, home_picks, home, sem.at[2])
     for copy in copies + weights[1:] + own_copies:
         copy.start()
     for copy in copies:
@@ -119,10 +120,11 @@
         out_shape=[
             jax.ShapeDtypeStruct((targets, frames, width), BF16),
             jax.ShapeDtypeStruct((targets * span, d_local), BF16),
+            jax.ShapeDtypeStruct((2 * span, d_local), BF16),
             jax.ShapeDtypeStruct((width, d_local), BF16),
         ],
         in_specs=[HBM] * 3,
-        out_specs=[VMEM] * 3,
+        out_specs=[VMEM] * 4,
         scratch_shapes=[
             pltpu.SMEM(routes.shape, jnp.int32),
             pltpu.VMEM((targets * span, d_local), BF16),
@@ -130,7 +132,7 @@
         + [pltpu.VMEM((width // PIECES // LANES, targets * span, LANES), F32)] * PIECES
         + [
             pltpu.SemaphoreType.DMA,
-            pltpu.SemaphoreType.DMA((2, targets)),
+            pltpu.SemaphoreType.DMA((3, max(targets, 2))),
             pltpu.SemaphoreType.DMA((PIECES,)),
         ],
         compiler_params=pltpu.CompilerParams(vmem_limit_bytes=OTHER_VMEM << 20),
@@ -171,40 +173,32 @@
     )(routes, slabs, weight)
 
 
-def home_kernel(routes, windows, weight, other, own, meta, slabs, product, meta_sem, sem):
+def home_kernel(last_start, routes, slabs, weight, other, own, meta, product, meta_sem):
     route_copy = pltpu.make_async_copy(routes, meta, meta_sem)
     route_copy.start()
+    multiply(slabs, weight, product)
     route_copy.wait()
-    last_start = windows.shape[1] - slabs.shape[0] // 2
     picks = [picks_of(meta, flip, [0], last_start)[0] for flip in (1, 0)]
-    copies = slab_copies(windows, picks, slabs, sem)
-    for copy in copies:
-        copy.start()
-    for copy in copies:
-        copy.wait()
-    multiply(slabs, weight, product)
     cut_rows(product, [other, own], picks, 0)
 
 
-def adapter_home(frames, routes, windows, weight):
-    width, d_local = weight.shape
+def adapter_home(frames, seq_len, routes, slabs, weight):
+    width = weight.shape[0]
     span = frames + ROW_TILE
     return pl.pallas_call(
-        home_kernel,
+        functools.partial(home_kernel, seq_len - span),
         out_shape=[jax.ShapeDtypeStruct((frames, width), BF16)] * 2,
-        in_specs=[HBM] * 2 + [VMEM],
+        in_specs=[HBM] + [VMEM] * 2,
         out_specs=[VMEM] * 2,
         scratch_shapes=[
             pltpu.SMEM(routes.shape, jnp.int32),
-            pltpu.VMEM((2 * span, d_local), BF16),
             pltpu.VMEM((width // LANES, 2 * span, LANES), F32),
             pltpu.SemaphoreType.DMA,
-            pltpu.SemaphoreType.DMA((2,)),
         ],
-        compiler_params=pltpu.CompilerParams(vmem_limit_bytes=HOME_VMEM << 20),
+        compiler_params=pltpu.CompilerParams(vmem_limit_bytes=OWN_VMEM << 20),
         cost_estimate=matmul_cost(1, 1, 1),
         name="adapter_home",
-    )(routes, windows, weight)
+    )(routes, slabs, weight)
 
 
 def pair_sum_kernel(own, other, *outs):
@@ -246,6 +240,68 @@
         compiler_params=pltpu.CompilerParams(vmem_limit_bytes=24 << 20),
         name="plane_sum",
     )(*blocks)
+
+
+def square_sum_kernel(own, other, along_x, along_y, keep_x, keep_y):
+    size = keep_x.shape[0]
+    first, second = pl.ds(0, size), pl.ds(size, size)
+
+    def both(place, rows):
+        return (own[place, rows, :].astype(F32) + other[place, rows, :].astype(F32)).astype(BF16)
+
+    along_x[0, :, :] = both(0, first)
+    along_x[1, :, :] = both(2, first)
+    along_y[0, :, :] = both(1, second)
+    along_y[1, :, :] = both(2, second)
+    keep_x[...] = both(1, first)
+    keep_y[...] = both(0, second)
+
+
+def square_sum(own, other):
+    _, frames, width = own.shape
+    pair = jax.ShapeDtypeStruct((2, frames // 2, width), BF16)
+    single = jax.ShapeDtypeStruct((frames // 2, width), BF16)
+    return pl.pallas_call(
+        square_sum_kernel,
+        out_shape=[pair, pair, single, single],
+        in_specs=[VMEM] * 2,
+        out_specs=[VMEM] * 4,
+        compiler_params=pltpu.CompilerParams(vmem_limit_bytes=24 << 20),
+        name="pair_sum",
+    )(own, other)
+
+
+def relay_kernel(keep, arrived, out):
+    out[...] = (keep[...].astype(F32) + arrived[1].astype(F32)).astype(BF16)
+
+
+def relay(keep, arrived):
+    return pl.pallas_call(
+        relay_kernel,
+        out_shape=jax.ShapeDtypeStruct(keep.shape, BF16),
+        in_specs=[VMEM] * 2,
+        out_specs=VMEM,
+        compiler_params=pltpu.CompilerParams(vmem_limit_bytes=24 << 20),
+        name="relay",
+    )(keep, arrived)
+
+
+def square_total_kernel(from_x, relayed_x, from_y, relayed_y, out):
+    size = relayed_x.shape[0]
+    out[:size, :] = from_x[0].astype(F32) + relayed_x[...].astype(F32)
+    out[size:, :] = from_y[0].astype(F32) + relayed_y[...].astype(F32)
+
+
+def square_total(from_x, relayed_x, from_y, relayed_y):
+    size, width = relayed_x.shape
+    return pl.pallas_call(
+        square_total_kernel,
+        out_shape=jax.ShapeDtypeStruct((2 * size, width), F32),
+        in_specs=[VMEM] * 4,
+        out_specs=VMEM,
+        compiler_params=pltpu.CompilerParams(vmem_limit_bytes=24 << 20),
+        name="plane_sum",
+    )(from_x, relayed_x, from_y, relayed_y)
 
 
 def swish_kernel(parts, first, valid, project, *refs):
@@ -418,13 +474,13 @@
     return [blocks[0]] + [turn(blocks[step], count, step) for step in turns(count)]
 
 
-def z_gather(block, count, later):
+def z_gather(block, count):
     held, mask = block, count // 2
     while mask:
         arrived = swap(held, "ch", count, mask)
         held = jnp.concatenate([held, arrived], axis=0)
         mask //= 2
-    return held, later
+    return held
 
 
 def summed(blocks):
@@ -459,18 +515,25 @@
 
     seq_len = frame_cotangent.shape[1]
     routes = jnp.stack([rollout_utterance, frame_offset])
-    for_other, own_slabs, weight = adapter_other(frames, routes, frame_cotangent, adapter_weight)
+    for_other, own_slabs, home_slabs, weight = adapter_other(frames, routes, frame_cotangent, adapter_weight)
     from_other = swap(for_other, "dec", n_dec, 1)
     own = adapter_own(frames, seq_len, routes, own_slabs, weight)
-    (sums,) = pair_sum(own, from_other)
+    square = chips == 4
+    sums = square_sum(own, from_other) if square else pair_sum(own, from_other)[0]
     sums, routes, own_input = lax.optimization_barrier((sums, routes, normed_input.reshape(frames, c_local)))
-    arrived = plane_exchange(sums, n_dec)
-    home_other, home_own = adapter_home(frames, routes, frame_cotangent, weight)
+    if square:
+        from_x, from_y = swap(sums[0], "dec", n_dec, 2), swap(sums[1], "dec", n_dec, 4)
+        relayed_x = swap(relay(sums[2], from_x), "dec", n_dec, 4)
+        relayed_y = swap(relay(sums[3], from_y), "dec", n_dec, 2)
+        arrived = square_total(from_x, relayed_x, from_y, relayed_y)
+    else:
+        arrived = plane_sum(plane_exchange(sums, n_dec))
+    home_other, home_own = adapter_home(frames, seq_len, routes, home_slabs, weight)
     homes = [home_own, swap(home_other, "dec", n_dec, 1)]
-    inputs, _ = z_gather(own_input, n_ch, taps)
+    inputs = z_gather(own_input, n_ch)
     expand_t, project_t = transposed(n_ch, expand, project_weight)
     value, gate, slope = forward(frames, utterance_frames, expand, taps, scale, shift, inputs)
-    swish_parts, stream_parts = swish(0, utterance_frames, project_t, homes, [plane_sum(arrived)])
+    swish_parts, stream_parts = swish(0, utterance_frames, project_t, homes, [arrived])
     swish_parts = z_exchange(swish_parts)
     stream_parts = z_exchange(stream_parts)
     parts = z_exchange(backward(utterance_frames, expand_t, taps, value, gate, slope, swish_parts))

time: 48.7 us -> 47.7 us (0.979)
  starting transfers between devices: 24.6 us -> 29.3 us
  waiting for transfers between devices: 6.8 us -> 2.88 us
  Pallas kernels: 13.3 us -> 11.5 us
    ppermute x7 -> x8, starting transfers between devices: 8.62 us -> 12.3 us  [swap(): return lax.ppermute(block, axis, [(i, i ^ mask) for i in range(count)])]
    ppermute x7 -> x8, waiting for transfers between devices: 4.1 us -> 1.12 us  [swap(): return lax.ppermute(block, axis, [(i, i ^ mask) for i in range(count)])]
    pallas_call x3 -> x5, Pallas kernels: 3.7 us -> 1.91 us  [the longest x1 1.6 us: adapter_home(): pl.pallas_call(functools.partial(home_kernel, seq_len - span), out_shape=...]
    ppermute x9, starting transfers between devices: 16 us -> 17 us  [turn(): lax.ppermute(block, 'ch', [(i, (i + step) % count) for i in range(count)])]
    ppermute x9, waiting for transfers between devices: 2.7 us -> 1.76 us  [turn(): lax.ppermute(block, 'ch', [(i, (i + step) % count) for i in range(count)])]
  transfers between devices with their start and end apart: 16 -> 17, of which waited for: 4 -> 3; matrix products, arithmetic and copies ran while one was open for 2% -> 2% of each run, Pallas kernels for 17% -> 14%
where the time goes in v5:
time: 47.7 us; the launch traced here: 47.5 us
  starting transfers between devices  29.3 us (61%)
  Pallas kernels  11.5 us (24%)
  waiting for transfers between devices  2.88 us (6%)
  other arithmetic  2.04 us (4%)
  between operations  1.51 us (3%)
    ppermute x9, starting transfers between devices, turn(): lax.ppermute(block, 'ch', [(i, (i + step) % count) for i in range(count)])  17 us
    ppermute x8, starting transfers between devices, swap(): return lax.ppermute(block, axis, [(i, i ^ mask) for i in range(count)])  12.3 us
    pallas_call x1, Pallas kernels, adapter_other(): pl.pallas_call(other_kernel, out_shape=[jax.ShapeDtypeStruct((targets, fr...  4.78 us
    pallas_call x1, Pallas kernels, adapter_own(): pl.pallas_call(functools.partial(own_kernel, seq_len - span), out_shape=j...  2.42 us
    ppermute x9, waiting for transfers between devices, turn(): lax.ppermute(block, 'ch', [(i, (i + step) % count) for i in range(count)])  1.76 us
    pallas_call x1, Pallas kernels, adapter_home(): pl.pallas_call(functools.partial(home_kernel, seq_len - span), out_shape=...  1.6 us
    broadcast_in_dim x2, other arithmetic, body(): return (summed(stream_parts)[None], summed(parts)[None])  1.32 us
    ppermute x8, waiting for transfers between devices, swap(): return lax.ppermute(block, axis, [(i, i ^ mask) for i in range(count)])  1.12 us
  transfers between devices with their start and end apart: 17, of which 3 were waited for; matrix products, arithmetic and copies ran while one was open for 2% of the time, Pallas kernels for 14%

profile of v5, /device:TPU:0, one launch (start us, length us, event | category | flops | bytes accessed | tf_op | source)
XLA Modules:
  0.0 47.5 jit_solution(820055105609584269)
XLA Ops:
  0.6 0.7 %pad_add_fusion.routes = s32[2,8]{1,0:T(2,128)S(1)} fusion(s32[1,8]{1,0:T(1,128)} %bitcast.19, s32[1,8]{1,0:T(1,128)} %bitcast.20), kind=kLoop, calls=%fused_computation.6 | loop fusion | flops 16 | bytes 128 | tf_op jit(solution)/shard_map/stack | solution.py:517
  1.3 4.8 %adapter_other.1 = (bf16[3,128,1024]{2,1,0:T(8,128)(2,1)S(1)}, bf16[432,2048]{1,0:T(8,128)(2,1)S(1)}, bf16[288,2048]{1,0:T(8,128)(2,1)S(1)}, bf16[1024,2048]{1,0:T(8,128)(2,1)S(1)}) custom-call(s32[2,8]{1,0:T(2,128)S(1)} %pad_add_fusion.routes, bf16[8,160,2048]{2,1,0:T(8,128)(2,1)} %windows.1, bf16[1024,2048]{1,0:T(8,128)(2,1)} %weight_hbm.1), custom_call_target="tpu_custom_call" | custom-call | flops 1811939328 | bytes 6848512 | tf_op jit(solution)/shard_map/adapter_other/pallas_call | solution.py:118
  6.1 0.5 %collective-permute-start = (bf16[3,128,1024]{2,1,0:T(8,128)(2,1)S(1)}, bf16[3,128,1024]{2,1,0:T(8,128)(2,1)S(1)}, u32[]{:S(2)}, u32[]{:S(2)}) collective-permute-start(bf16[3,128,1024]{2,1,0:T(8,128)(2,1)S(1)} %get-tuple-element.38), channel_id=1, source_target_pairs={{0,4},{4,0},{8,12},{12,8},{16,20},{20,16},{24,28},{28,24},{1,5},{5... | collective-permute-start | bytes 2359304 | tf_op jit(solution)/shard_map/ppermute | solution.py:461
  6.6 2.4 %adapter_own.1.own = bf16[3,128,1024]{2,1,0:T(8,128)(2,1)S(1)} custom-call(s32[2,8]{1,0:T(2,128)S(1)} %pad_add_fusion.routes, bf16[432,2048]{1,0:T(8,128)(2,1)S(1)} %get-tuple-element.36.slabs, bf16[1024,2048]{1,0:T(8,128)(2,1)S(1)} %get-tuple-element.37.weight), custom_call_target="tpu_custom_call" | custom-call | flops 2 | bytes 6 | tf_op jit(solution)/shard_map/adapter_own/pallas_call | solution.py:162
  9.1 0.2 pair_sum.1
  9.2 2.6 %collective-permute-start.4 = (bf16[2,64,1024]{2,1,0:T(8,128)(2,1)S(1)}, bf16[2,64,1024]{2,1,0:T(8,128)(2,1)S(1)}, u32[]{:S(2)}, u32[]{:S(2)}) collective-permute-start(bf16[2,64,1024]{2,1,0:T(8,128)(2,1)S(1)} %get-tuple-element.49), channel_id=1, source_target_pairs={{0,16},{4,20},{8,24},{12,28},{16,0},{20,4},{24,8},{28,12},{1,17},{... | collective-permute-start | bytes 786440 | tf_op jit(solution)/shard_map/ppermute | solution.py:461
  11.8 1.5 %collective-permute-start.2 = (bf16[2,64,1024]{2,1,0:T(8,128)(2,1)S(1)}, bf16[2,64,1024]{2,1,0:T(8,128)(2,1)S(1)}, u32[]{:S(2)}, u32[]{:S(2)}) collective-permute-start(bf16[2,64,1024]{2,1,0:T(8,128)(2,1)S(1)} %get-tuple-element.47), channel_id=1, source_target_pairs={{0,8},{4,12},{8,0},{12,4},{16,24},{20,28},{24,16},{28,20},{1,9},{5... | collective-permute-start | bytes 786440 | tf_op jit(solution)/shard_map/ppermute | solution.py:461
  13.3 1.6 %adapter_home.1 = (bf16[128,1024]{1,0:T(8,128)(2,1)S(1)}, bf16[128,1024]{1,0:T(8,128)(2,1)S(1)}) custom-call(s32[2,8]{1,0:T(2,128)S(1)} %pad_add_fusion.routes, bf16[288,2048]{1,0:T(8,128)(2,1)S(1)} %get-tuple-element.44.slabs, bf16[1024,2048]{1,0:T(8,128)(2,1)S(1)} %get-tuple-element.37.weight), custom_call_target="tpu_custom_call" | custom-call | flops 2 | bytes 6 | tf_op jit(solution)/shard_map/adapter_home/pallas_call | solution.py:188
  15.0 0.1 collective-permute-start.1
  15.0 2.7 %collective-permute-start.9 = (bf16[128,256]{1,0:T(8,128)(2,1)S(1)}, bf16[128,256]{1,0:T(8,128)(2,1)S(1)}, u32[]{:S(2)}, u32[]{:S(2)}) collective-permute-start(bf16[128,256]{1,0:T(8,128)(2,1)S(1)} %bitcast.16), channel_id=1, source_target_pairs={{0,2},{1,3},{2,0},{3,1},{4,6},{5,7},{6,4},{7,5},{8,10},{9,11},{10,... | collective-permute-start | bytes 196616 | tf_op jit(solution)/shard_map/ppermute | solution.py:461
  17.7 1.1 %collective-permute-done.4.arrived.from_y = bf16[2,64,1024]{2,1,0:T(8,128)(2,1)S(1)} collective-permute-done((bf16[2,64,1024]{2,1,0:T(8,128)(2,1)S(1)}, bf16[2,64,1024]{2,1,0:T(8,128)(2,1)S(1)}, u32[]{:S(2)}, u32[]{:S(2)}) %collective-permute-start.4) | collective-permute-done | bytes 262176 | tf_op jit(solution)/shard_map/ppermute | solution.py:461
  18.8 1.8 %collective-permute-start.5 = (bf16[64,1024]{1,0:T(8,128)(2,1)S(1)}, bf16[64,1024]{1,0:T(8,128)(2,1)S(1)}, u32[]{:S(2)}, u32[]{:S(2)}) collective-permute-start(bf16[64,1024]{1,0:T(8,128)(2,1)S(1)} %relay.3), channel_id=1, source_target_pairs={{0,8},{4,12},{8,0},{12,4},{16,24},{20,28},{24,16},{28,20},{1,9},{5... | collective-permute-start | bytes 393224 | tf_op jit(solution)/shard_map/ppermute | solution.py:461
  20.7 1.6 %collective-permute-start.3 = (bf16[64,1024]{1,0:T(8,128)(2,1)S(1)}, bf16[64,1024]{1,0:T(8,128)(2,1)S(1)}, u32[]{:S(2)}, u32[]{:S(2)}) collective-permute-start(bf16[64,1024]{1,0:T(8,128)(2,1)S(1)} %relay.2), channel_id=1, source_target_pairs={{0,16},{4,20},{8,24},{12,28},{16,0},{20,4},{24,8},{28,12},{1,17},{... | collective-permute-start | bytes 393224 | tf_op jit(solution)/shard_map/ppermute | solution.py:461
  22.3 1.6 %collective-permute-start.10 = (bf16[256,256]{1,0:T(8,128)(2,1)S(1)}, bf16[256,256]{1,0:T(8,128)(2,1)S(1)}, u32[]{:S(2)}, u32[]{:S(2)}) collective-permute-start(bf16[256,256]{1,0:T(8,128)(2,1)S(1)} %pad_maximum_fusion.1), channel_id=1, source_target_pairs={{0,1},{1,0},{2,3},{3,2},{4,5},{5,4},{6,7},{7,6},{8,9},{9,8},{10,11... | collective-permute-start | bytes 393224 | tf_op jit(solution)/shard_map/ppermute | solution.py:461
  23.9 0.2 copy.13
  24.1 0.9 %transposed_weights.1 = (bf16[4,512,256]{2,1,0:T(8,128)(2,1)S(1)}, bf16[4,1024,256]{2,1,0:T(8,128)(2,1)S(1)}) custom-call(bf16[1024,512]{1,0:T(8,128)(2,1)S(1)} %bitcast.11, bf16[1024,1024]{1,0:T(8,128)(2,1)S(1)} %copy-done), custom_call_target="tpu_custom_call" | custom-call | flops 2 | bytes 6 | tf_op jit(solution)/shard_map/transposed_weights/pallas_call | solution.py:363
  25.7 0.1 plane_sum.1.refs_2_
  25.8 0.5 %stream_and_swish.1 = (f32[128,256]{1,0:T(8,128)S(1)}, bf16[128,256]{1,0:T(8,128)(2,1)S(1)}, bf16[128,256]{1,0:T(8,128)(2,1)S(1)}, bf16[128,256]{1,0:T(8,128)(2,...) custom-call(s32[1]{0:T(128)S(6)} %copy.14.valid, ...), custom_call_target="tpu_custom_call" | custom-call | flops 268435456 | bytes 2621440 | tf_op jit(solution)/shard_map/stream_and_swish/pallas_call | solution.py:327
  26.3 2.7 %collective-permute-start.11 = (bf16[128,256]{1,0:T(8,128)(2,1)S(1)}, bf16[128,256]{1,0:T(8,128)(2,1)S(1)}, u32[]{:S(2)}, u32[]{:S(2)}) collective-permute-start(bf16[128,256]{1,0:T(8,128)(2,1)S(1)} %get-tuple-element.61), channel_id=1, source_target_pairs={{0,2},{1,3},{2,0},{3,1},{4,6},{5,7},{6,4},{7,5},{8,10},{9,11},{10,... | collective-permute-start | bytes 196616 | tf_op jit(solution)/shard_map/ppermute | solution.py:469
  29.0 1.6 %collective-permute-start.12 = (bf16[128,256]{1,0:T(8,128)(2,1)S(1)}, bf16[128,256]{1,0:T(8,128)(2,1)S(1)}, u32[]{:S(2)}, u32[]{:S(2)}) collective-permute-start(bf16[128,256]{1,0:T(8,128)(2,1)S(1)} %get-tuple-element.62), channel_id=1, source_target_pairs={{0,1},{1,2},{2,3},{3,0},{4,5},{5,6},{6,7},{7,4},{8,9},{9,10},{10,1... | collective-permute-start | bytes 196616 | tf_op jit(solution)/shard_map/ppermute | solution.py:469
  30.5 2.3 %collective-permute-start.13 = (bf16[128,256]{1,0:T(8,128)(2,1)S(1)}, bf16[128,256]{1,0:T(8,128)(2,1)S(1)}, u32[]{:S(2)}, u32[]{:S(2)}) collective-permute-start(bf16[128,256]{1,0:T(8,128)(2,1)S(1)} %get-tuple-element.63), channel_id=1, source_target_pairs={{0,3},{1,0},{2,1},{3,2},{4,7},{5,4},{6,5},{7,6},{8,11},{9,8},{10,9... | collective-permute-start | bytes 196616 | tf_op jit(solution)/shard_map/ppermute | solution.py:469
  32.8 0.6 %collective-permute-start.7 = (bf16[128,256]{1,0:T(8,128)(2,1)S(1)}, bf16[128,256]{1,0:T(8,128)(2,1)S(1)}, u32[]{:S(2)}, u32[]{:S(2)}) collective-permute-start(bf16[128,256]{1,0:T(8,128)(2,1)S(1)} %get-tuple-element.53), channel_id=1, source_target_pairs={{0,1},{1,2},{2,3},{3,0},{4,5},{5,6},{6,7},{7,4},{8,9},{9,10},{10,1... | collective-permute-start | bytes 196616 | tf_op jit(solution)/shard_map/ppermute | solution.py:469
  33.4 0.2 collective-permute-done.11.refs_1_
  33.6 3.4 %collective-permute-start.8 = (bf16[128,256]{1,0:T(8,128)(2,1)S(1)}, bf16[128,256]{1,0:T(8,128)(2,1)S(1)}, u32[]{:S(2)}, u32[]{:S(2)}) collective-permute-start(bf16[128,256]{1,0:T(8,128)(2,1)S(1)} %get-tuple-element.54), channel_id=1, source_target_pairs={{0,3},{1,0},{2,1},{3,2},{4,7},{5,4},{6,5},{7,6},{8,11},{9,8},{10,9... | collective-permute-start | bytes 196616 | tf_op jit(solution)/shard_map/ppermute | solution.py:469
  37.0 0.6 %forward_gates.1 = (f32[128,256]{1,0:T(8,128)S(1)}, f32[128,256]{1,0:T(8,128)S(1)}, f32[128,256]{1,0:T(8,128)S(1)}) custom-call(s32[1]{0:T(128)S(6)} %copy.14.valid, bf16[1024,512]{1,0:T(8,128)(2,1)S(1)} %bitcast.12, f32[9,256]{1,0:T(8,128)S(1)} %convert_element_type.31.taps_ref, f32[1,256]{1,0:T(1,128)S(1)} %bitcast.13, f32[1,256]{1,0:T(1,128)S(1)} %bitcast.14, ...), custom_call_target="tpu_custom_call" | custom-call | flops 134217728 | bytes 1441792 | tf_op jit(solution)/shard_map/forward_gates/pallas_call | solution.py:406
  37.5 0.5 %backward_module.1 = (f32[128,256]{1,0:T(8,128)S(1)}, bf16[128,256]{1,0:T(8,128)(2,1)S(1)}, bf16[128,256]{1,0:T(8,128)(2,1)S(1)}, bf16[128,256]{1,0:T(8,128)(2,1)S(1)}) custom-call(s32[1]{0:T(128)S(6)} %copy.14.valid, bf16[4,512,256]{2,1,0:T(8,128)(2,1)S(1)} %get-tuple-element.55.expand_t, f32[9,256]{1,0:T(8,128)S(1)} %convert_element_type.31.taps_ref, ...), custom_call_target="tpu_custom_call" | custom-call | flops 134217728 | bytes 1441792 | tf_op jit(solution)/shard_map/backward_module/pallas_call | solution.py:444
  38.0 2.7 %collective-permute-start.14 = (bf16[128,256]{1,0:T(8,128)(2,1)S(1)}, bf16[128,256]{1,0:T(8,128)(2,1)S(1)}, u32[]{:S(2)}, u32[]{:S(2)}) collective-permute-start(bf16[128,256]{1,0:T(8,128)(2,1)S(1)} %get-tuple-element.65), channel_id=1, source_target_pairs={{0,2},{1,3},{2,0},{3,1},{4,6},{5,7},{6,4},{7,5},{8,10},{9,11},{10,... | collective-permute-start | bytes 196616 | tf_op jit(solution)/shard_map/ppermute | solution.py:469
  40.8 0.1 collective-permute-start.15
  40.9 3.7 %collective-permute-start.16 = (bf16[128,256]{1,0:T(8,128)(2,1)S(1)}, bf16[128,256]{1,0:T(8,128)(2,1)S(1)}, u32[]{:S(2)}, u32[]{:S(2)}) collective-permute-start(bf16[128,256]{1,0:T(8,128)(2,1)S(1)} %get-tuple-element.67), channel_id=1, source_target_pairs={{0,3},{1,0},{2,1},{3,2},{4,7},{5,4},{6,5},{7,6},{8,11},{9,8},{10,9... | collective-permute-start | bytes 196616 | tf_op jit(solution)/shard_map/ppermute | solution.py:469
  44.6 0.7 %fusion = bf16[1,128,256]{2,1,0:T(8,128)(2,1)} fusion(bf16[128,256]{1,0:T(8,128)(2,1)S(1)} %collective-permute-done.8, bf16[128,256]{1,0:T(8,128)(2,1)S(1)} %collective-permute-done.7, f32[128,256]{1,0:T(8,128)S(1)} %get-tuple-element.51, bf16[128,256]{1,0:T(8,128)(2,1)S(1)} %collective-permute-done.6), kind=kLoop, calls=%fused_computation.4 | loop fusion | flops 229376 | bytes 393216 | tf_op jit(solution)/shard_map/broadcast_in_dim | solution.py:540
  45.3 1.6 %collective-permute-done.15 = bf16[128,256]{1,0:T(8,128)(2,1)S(1)} collective-permute-done((bf16[128,256]{1,0:T(8,128)(2,1)S(1)}, bf16[128,256]{1,0:T(8,128)(2,1)S(1)}, u32[]{:S(2)}, u32[]{:S(2)}) %collective-permute-start.15) | collective-permute-done | bytes 65568 | tf_op jit(solution)/shard_map/ppermute | solution.py:469
  46.8 0.7 %fusion.1 = bf16[1,128,256]{2,1,0:T(8,128)(2,1)} fusion(bf16[128,256]{1,0:T(8,128)(2,1)S(1)} %collective-permute-done.16, bf16[128,256]{1,0:T(8,128)(2,1)S(1)} %collective-permute-done.15, f32[128,256]{1,0:T(8,128)S(1)} %get-tuple-element.64, bf16[128,256]{1,0:T(8,128)(2,1)S(1)} %collective-permute-done.14), kind=kLoop, calls=%fused_computation.5 | loop fusion | flops 229376 | bytes 393216 | tf_op jit(solution)/shard_map/broadcast_in_dim | solution.py:540
  (32 shorter events, 0.2 us)
Async XLA Ops:
  6.1 2.9 %collective-permute-start = (bf16[3,128,1024]{2,1,0:T(8,128)(2,1)S(1)}, bf16[3,128,1024]{2,1,0:T(8,128)(2,1)S(1)}, u32[]{:S(2)}, u32[]{:S(2)}) collective-permute-start(bf16[3,128,1024]{2,1,0:T(8,128)(2,1)S(1)} %get-tuple-element.38), channel_id=1, source_target_pairs={{0,4},{4,0},{8,12},{12,8},{16,20},{20,16},{24,28},{28,24},{1,5},{5... | collective-permute-start | bytes 2359304 | tf_op jit(solution)/shard_map/ppermute | solution.py:461
  9.2 9.6 %collective-permute-start.4 = (bf16[2,64,1024]{2,1,0:T(8,128)(2,1)S(1)}, bf16[2,64,1024]{2,1,0:T(8,128)(2,1)S(1)}, u32[]{:S(2)}, u32[]{:S(2)}) collective-permute-start(bf16[2,64,1024]{2,1,0:T(8,128)(2,1)S(1)} %get-tuple-element.49), channel_id=1, source_target_pairs={{0,16},{4,20},{8,24},{12,28},{16,0},{20,4},{24,8},{28,12},{1,17},{... | collective-permute-start | bytes 786440 | tf_op jit(solution)/shard_map/ppermute | solution.py:461
  11.8 8.8 %collective-permute-start.2 = (bf16[2,64,1024]{2,1,0:T(8,128)(2,1)S(1)}, bf16[2,64,1024]{2,1,0:T(8,128)(2,1)S(1)}, u32[]{:S(2)}, u32[]{:S(2)}) collective-permute-start(bf16[2,64,1024]{2,1,0:T(8,128)(2,1)S(1)} %get-tuple-element.47), channel_id=1, source_target_pairs={{0,8},{4,12},{8,0},{12,4},{16,24},{20,28},{24,16},{28,20},{1,9},{5... | collective-permute-start | bytes 786440 | tf_op jit(solution)/shard_map/ppermute | solution.py:461
  13.3 1.7 %copy-start.4 = (bf16[1,128,256]{2,1,0:T(8,128)(2,1)S(1)}, bf16[1,128,256]{2,1,0:T(8,128)(2,1)}, u32[]{:S(2)}) copy-start(bf16[1,128,256]{2,1,0:T(8,128)(2,1)} %param.15) | copy-start | bytes 196612
  13.3 10.6 %copy-start.3 = (bf16[1024,2,256]{2,1,0:T(2,128)(2,1)S(1)}, bf16[1024,2,256]{2,1,0:T(2,128)(2,1)}, u32[]{:S(2)}) copy-start(bf16[1024,2,256]{2,1,0:T(2,128)(2,1)} %param.16) | copy-start | bytes 3145732
  14.9 9.2 %copy-start = (bf16[1024,1024]{1,0:T(8,128)(2,1)S(1)}, bf16[1024,1024]{1,0:T(8,128)(2,1)}, u32[]{:S(2)}) copy-start(bf16[1024,1024]{1,0:T(8,128)(2,1)} %project.1) | copy-start | bytes 6291460
  15.0 10.8 %collective-permute-start.1 = (bf16[128,1024]{1,0:T(8,128)(2,1)S(1)}, bf16[128,1024]{1,0:T(8,128)(2,1)S(1)}, u32[]{:S(2)}, u32[]{:S(2)}) collective-permute-start(bf16[128,1024]{1,0:T(8,128)(2,1)S(1)} %get-tuple-element.46), channel_id=1, source_target_pairs={{0,4},{4,0},{8,12},{12,8},{16,20},{20,16},{24,28},{28,24},{1,5},{5... | collective-permute-start | bytes 786440 | tf_op jit(solution)/shard_map/ppermute | solution.py:461
  15.0 7.2 %collective-permute-start.9 = (bf16[128,256]{1,0:T(8,128)(2,1)S(1)}, bf16[128,256]{1,0:T(8,128)(2,1)S(1)}, u32[]{:S(2)}, u32[]{:S(2)}) collective-permute-start(bf16[128,256]{1,0:T(8,128)(2,1)S(1)} %bitcast.16), channel_id=1, source_target_pairs={{0,2},{1,3},{2,0},{3,1},{4,6},{5,7},{6,4},{7,5},{8,10},{9,11},{10,... | collective-permute-start | bytes 196616 | tf_op jit(solution)/shard_map/ppermute | solution.py:461
  18.8 6.8 %collective-permute-start.5 = (bf16[64,1024]{1,0:T(8,128)(2,1)S(1)}, bf16[64,1024]{1,0:T(8,128)(2,1)S(1)}, u32[]{:S(2)}, u32[]{:S(2)}) collective-permute-start(bf16[64,1024]{1,0:T(8,128)(2,1)S(1)} %relay.3), channel_id=1, source_target_pairs={{0,8},{4,12},{8,0},{12,4},{16,24},{20,28},{24,16},{28,20},{1,9},{5... | collective-permute-start | bytes 393224 | tf_op jit(solution)/shard_map/ppermute | solution.py:461
  20.7 5.0 %collective-permute-start.3 = (bf16[64,1024]{1,0:T(8,128)(2,1)S(1)}, bf16[64,1024]{1,0:T(8,128)(2,1)S(1)}, u32[]{:S(2)}, u32[]{:S(2)}) collective-permute-start(bf16[64,1024]{1,0:T(8,128)(2,1)S(1)} %relay.2), channel_id=1, source_target_pairs={{0,16},{4,20},{8,24},{12,28},{16,0},{20,4},{24,8},{28,12},{1,17},{... | collective-permute-start | bytes 393224 | tf_op jit(solution)/shard_map/ppermute | solution.py:461
  22.3 10.6 %collective-permute-start.10 = (bf16[256,256]{1,0:T(8,128)(2,1)S(1)}, bf16[256,256]{1,0:T(8,128)(2,1)S(1)}, u32[]{:S(2)}, u32[]{:S(2)}) collective-permute-start(bf16[256,256]{1,0:T(8,128)(2,1)S(1)} %pad_maximum_fusion.1), channel_id=1, source_target_pairs={{0,1},{1,0},{2,3},{3,2},{4,5},{5,4},{6,7},{7,6},{8,9},{9,8},{10,11... | collective-permute-start | bytes 393224 | tf_op jit(solution)/shard_map/ppermute | solution.py:461
  25.7 3.3 %copy-start.5 = (bf16[9,256]{1,0:T(8,128)(2,1)S(1)}, bf16[9,256]{1,0:T(8,128)(2,1)}, u32[]{:S(2)}) copy-start(bf16[9,256]{1,0:T(8,128)(2,1)} %param.17) | copy-start | bytes 13828
  25.8 11.2 %copy-start.1 = (f32[256]{0:T(256)S(1)}, f32[256]{0:T(256)}, u32[]{:S(2)}) copy-start(f32[256]{0:T(256)} %param.18) | copy-start | bytes 3076
  25.8 11.2 %copy-start.2 = (f32[256]{0:T(256)S(1)}, f32[256]{0:T(256)}, u32[]{:S(2)}) copy-start(f32[256]{0:T(256)} %param.19) | copy-start | bytes 3076
  26.3 7.2 %collective-permute-start.11 = (bf16[128,256]{1,0:T(8,128)(2,1)S(1)}, bf16[128,256]{1,0:T(8,128)(2,1)S(1)}, u32[]{:S(2)}, u32[]{:S(2)}) collective-permute-start(bf16[128,256]{1,0:T(8,128)(2,1)S(1)} %get-tuple-element.61), channel_id=1, source_target_pairs={{0,2},{1,3},{2,0},{3,1},{4,6},{5,7},{6,4},{7,5},{8,10},{9,11},{10,... | collective-permute-start | bytes 196616 | tf_op jit(solution)/shard_map/ppermute | solution.py:469
  29.0 8.5 %collective-permute-start.12 = (bf16[128,256]{1,0:T(8,128)(2,1)S(1)}, bf16[128,256]{1,0:T(8,128)(2,1)S(1)}, u32[]{:S(2)}, u32[]{:S(2)}) collective-permute-start(bf16[128,256]{1,0:T(8,128)(2,1)S(1)} %get-tuple-element.62), channel_id=1, source_target_pairs={{0,1},{1,2},{2,3},{3,0},{4,5},{5,6},{6,7},{7,4},{8,9},{9,10},{10,1... | collective-permute-start | bytes 196616 | tf_op jit(solution)/shard_map/ppermute | solution.py:469
  30.5 7.0 %collective-permute-start.13 = (bf16[128,256]{1,0:T(8,128)(2,1)S(1)}, bf16[128,256]{1,0:T(8,128)(2,1)S(1)}, u32[]{:S(2)}, u32[]{:S(2)}) collective-permute-start(bf16[128,256]{1,0:T(8,128)(2,1)S(1)} %get-tuple-element.63), channel_id=1, source_target_pairs={{0,3},{1,0},{2,1},{3,2},{4,7},{5,4},{6,5},{7,6},{8,11},{9,8},{10,9... | collective-permute-start | bytes 196616 | tf_op jit(solution)/shard_map/ppermute | solution.py:469
  32.8 8.1 %collective-permute-start.6 = (bf16[128,256]{1,0:T(8,128)(2,1)S(1)}, bf16[128,256]{1,0:T(8,128)(2,1)S(1)}, u32[]{:S(2)}, u32[]{:S(2)}) collective-permute-start(bf16[128,256]{1,0:T(8,128)(2,1)S(1)} %get-tuple-element.52), channel_id=1, source_target_pairs={{0,2},{1,3},{2,0},{3,1},{4,6},{5,7},{6,4},{7,5},{8,10},{9,11},{10,... | collective-permute-start | bytes 196616 | tf_op jit(solution)/shard_map/ppermute | solution.py:469
  32.8 11.8 %collective-permute-start.7 = (bf16[128,256]{1,0:T(8,128)(2,1)S(1)}, bf16[128,256]{1,0:T(8,128)(2,1)S(1)}, u32[]{:S(2)}, u32[]{:S(2)}) collective-permute-start(bf16[128,256]{1,0:T(8,128)(2,1)S(1)} %get-tuple-element.53), channel_id=1, source_target_pairs={{0,1},{1,2},{2,3},{3,0},{4,5},{5,6},{6,7},{7,4},{8,9},{9,10},{10,1... | collective-permute-start | bytes 196616 | tf_op jit(solution)/shard_map/ppermute | solution.py:469
  33.6 11.0 %collective-permute-start.8 = (bf16[128,256]{1,0:T(8,128)(2,1)S(1)}, bf16[128,256]{1,0:T(8,128)(2,1)S(1)}, u32[]{:S(2)}, u32[]{:S(2)}) collective-permute-start(bf16[128,256]{1,0:T(8,128)(2,1)S(1)} %get-tuple-element.54), channel_id=1, source_target_pairs={{0,3},{1,0},{2,1},{3,2},{4,7},{5,4},{6,5},{7,6},{8,11},{9,8},{10,9... | collective-permute-start | bytes 196616 | tf_op jit(solution)/shard_map/ppermute | solution.py:469
  38.0 7.2 %collective-permute-start.14 = (bf16[128,256]{1,0:T(8,128)(2,1)S(1)}, bf16[128,256]{1,0:T(8,128)(2,1)S(1)}, u32[]{:S(2)}, u32[]{:S(2)}) collective-permute-start(bf16[128,256]{1,0:T(8,128)(2,1)S(1)} %get-tuple-element.65), channel_id=1, source_target_pairs={{0,2},{1,3},{2,0},{3,1},{4,6},{5,7},{6,4},{7,5},{8,10},{9,11},{10,... | collective-permute-start | bytes 196616 | tf_op jit(solution)/shard_map/ppermute | solution.py:469
  40.8 6.1 %collective-permute-start.15 = (bf16[128,256]{1,0:T(8,128)(2,1)S(1)}, bf16[128,256]{1,0:T(8,128)(2,1)S(1)}, u32[]{:S(2)}, u32[]{:S(2)}) collective-permute-start(bf16[128,256]{1,0:T(8,128)(2,1)S(1)} %get-tuple-element.66), channel_id=1, source_target_pairs={{0,1},{1,2},{2,3},{3,0},{4,5},{5,6},{6,7},{7,4},{8,9},{9,10},{10,1... | collective-permute-start | bytes 196616 | tf_op jit(solution)/shard_map/ppermute | solution.py:469
  40.9 6.0 %collective-permute-start.16 = (bf16[128,256]{1,0:T(8,128)(2,1)S(1)}, bf16[128,256]{1,0:T(8,128)(2,1)S(1)}, u32[]{:S(2)}, u32[]{:S(2)}) collective-permute-start(bf16[128,256]{1,0:T(8,128)(2,1)S(1)} %get-tuple-element.67), channel_id=1, source_target_pairs={{0,3},{1,0},{2,1},{3,2},{4,7},{5,4},{6,5},{7,6},{8,11},{9,8},{10,9... | collective-permute-start | bytes 196616 | tf_op jit(solution)/shard_map/ppermute | solution.py:469

commit v6 on v5

--- a/solution.py
+++ b/solution.py
@@ -535,8 +535,12 @@
     value, gate, slope = forward(frames, utterance_frames, expand, taps, scale, shift, inputs)
     swish_parts, stream_parts = swish(0, utterance_frames, project_t, homes, [arrived])
     swish_parts = z_exchange(swish_parts)
-    stream_parts = z_exchange(stream_parts)
-    parts = z_exchange(backward(utterance_frames, expand_t, taps, value, gate, slope, swish_parts))
+    *early, late = turns(n_ch)
+    stream_arrived = [stream_parts[0]] + [turn(stream_parts[step], n_ch, step) for step in early]
+    parts = backward(utterance_frames, expand_t, taps, value, gate, slope, swish_parts)
+    parts, late_part = lax.optimization_barrier((parts, stream_parts[late]))
+    parts = z_exchange(parts)
+    stream_parts = stream_arrived + [turn(late_part, n_ch, late)]
     return summed(stream_parts)[None], summed(parts)[None]
 
 

time: 47.7 us -> 49.6 us (1.040)
  waiting for transfers between devices: 2.88 us -> 7.55 us
  starting transfers between devices: 29.3 us -> 26.6 us
    ppermute x9, waiting for transfers between devices: 1.76 us -> 6.36 us  [turn(): lax.ppermute(block, 'ch', [(i, (i + step) % count) for i in range(count)])]
    ppermute x9, starting transfers between devices: 17 us -> 14.3 us  [turn(): lax.ppermute(block, 'ch', [(i, (i + step) % count) for i in range(count)])]
  transfers between devices with their start and end apart: 17 -> 17, of which waited for: 3 -> 7; matrix products, arithmetic and copies ran while one was open for 2% -> 2% of each run, Pallas kernels for 14% -> 12%
where the time goes in v6:
time: 49.6 us; the launch traced here: 49.5 us
  starting transfers between devices  26.6 us (54%)
  Pallas kernels  11.5 us (23%)
  waiting for transfers between devices  7.55 us (15%)
  other arithmetic  2.05 us (4%)
  between operations  1.5 us (3%)
    ppermute x9, starting transfers between devices, turn(): lax.ppermute(block, 'ch', [(i, (i + step) % count) for i in range(count)])  14.3 us
    ppermute x8, starting transfers between devices, swap(): return lax.ppermute(block, axis, [(i, i ^ mask) for i in range(count)])  12.3 us
    ppermute x9, waiting for transfers between devices, turn(): lax.ppermute(block, 'ch', [(i, (i + step) % count) for i in range(count)])  6.36 us
    pallas_call x1, Pallas kernels, adapter_other(): pl.pallas_call(other_kernel, out_shape=[jax.ShapeDtypeStruct((targets, fr...  4.78 us
    pallas_call x1, Pallas kernels, adapter_own(): pl.pallas_call(functools.partial(own_kernel, seq_len - span), out_shape=j...  2.42 us
    pallas_call x1, Pallas kernels, adapter_home(): pl.pallas_call(functools.partial(home_kernel, seq_len - span), out_shape=...  1.6 us
    broadcast_in_dim x2, other arithmetic, body(): return (summed(stream_parts)[None], summed(parts)[None])  1.33 us
    ppermute x8, waiting for transfers between devices, swap(): return lax.ppermute(block, axis, [(i, i ^ mask) for i in range(count)])  1.19 us
  transfers between devices with their start and end apart: 17, of which 7 were waited for; matrix products, arithmetic and copies ran while one was open for 2% of the time, Pallas kernels for 12%

profile of v6, /device:TPU:0, one launch (start us, length us, event | category | flops | bytes accessed | tf_op | source)
XLA Modules:
  0.0 49.5 jit_solution(17140268092836272225)
XLA Ops:
  0.6 0.7 %pad_add_fusion.routes = s32[2,8]{1,0:T(2,128)S(1)} fusion(s32[1,8]{1,0:T(1,128)} %bitcast.19, s32[1,8]{1,0:T(1,128)} %bitcast.20), kind=kLoop, calls=%fused_computation.6 | loop fusion | flops 16 | bytes 128 | tf_op jit(solution)/shard_map/stack | solution.py:517
  1.3 4.8 %adapter_other.1 = (bf16[3,128,1024]{2,1,0:T(8,128)(2,1)S(1)}, bf16[432,2048]{1,0:T(8,128)(2,1)S(1)}, bf16[288,2048]{1,0:T(8,128)(2,1)S(1)}, bf16[1024,2048]{1,0:T(8,128)(2,1)S(1)}) custom-call(s32[2,8]{1,0:T(2,128)S(1)} %pad_add_fusion.routes, bf16[8,160,2048]{2,1,0:T(8,128)(2,1)} %windows.1, bf16[1024,2048]{1,0:T(8,128)(2,1)} %weight_hbm.1), custom_call_target="tpu_custom_call" | custom-call | flops 1811939328 | bytes 6848512 | tf_op jit(solution)/shard_map/adapter_other/pallas_call | solution.py:118
  6.1 0.5 %collective-permute-start = (bf16[3,128,1024]{2,1,0:T(8,128)(2,1)S(1)}, bf16[3,128,1024]{2,1,0:T(8,128)(2,1)S(1)}, u32[]{:S(2)}, u32[]{:S(2)}) collective-permute-start(bf16[3,128,1024]{2,1,0:T(8,128)(2,1)S(1)} %get-tuple-element.43), channel_id=1, source_target_pairs={{0,4},{4,0},{8,12},{12,8},{16,20},{20,16},{24,28},{28,24},{1,5},{5... | collective-permute-start | bytes 2359304 | tf_op jit(solution)/shard_map/ppermute | solution.py:461
  6.6 2.4 %adapter_own.1.own = bf16[3,128,1024]{2,1,0:T(8,128)(2,1)S(1)} custom-call(s32[2,8]{1,0:T(2,128)S(1)} %pad_add_fusion.routes, bf16[432,2048]{1,0:T(8,128)(2,1)S(1)} %get-tuple-element.41.slabs, bf16[1024,2048]{1,0:T(8,128)(2,1)S(1)} %get-tuple-element.42.weight), custom_call_target="tpu_custom_call" | custom-call | flops 2 | bytes 6 | tf_op jit(solution)/shard_map/adapter_own/pallas_call | solution.py:162
  9.2 2.6 %collective-permute-start.4 = (bf16[2,64,1024]{2,1,0:T(8,128)(2,1)S(1)}, bf16[2,64,1024]{2,1,0:T(8,128)(2,1)S(1)}, u32[]{:S(2)}, u32[]{:S(2)}) collective-permute-start(bf16[2,64,1024]{2,1,0:T(8,128)(2,1)S(1)} %get-tuple-element.54), channel_id=1, source_target_pairs={{0,16},{4,20},{8,24},{12,28},{16,0},{20,4},{24,8},{28,12},{1,17},{... | collective-permute-start | bytes 786440 | tf_op jit(solution)/shard_map/ppermute | solution.py:461
  11.9 1.5 %collective-permute-start.2 = (bf16[2,64,1024]{2,1,0:T(8,128)(2,1)S(1)}, bf16[2,64,1024]{2,1,0:T(8,128)(2,1)S(1)}, u32[]{:S(2)}, u32[]{:S(2)}) collective-permute-start(bf16[2,64,1024]{2,1,0:T(8,128)(2,1)S(1)} %get-tuple-element.52), channel_id=1, source_target_pairs={{0,8},{4,12},{8,0},{12,4},{16,24},{20,28},{24,16},{28,20},{1,9},{5... | collective-permute-start | bytes 786440 | tf_op jit(solution)/shard_map/ppermute | solution.py:461
  13.3 2.6 %collective-permute-start.8 = (bf16[128,256]{1,0:T(8,128)(2,1)S(1)}, bf16[128,256]{1,0:T(8,128)(2,1)S(1)}, u32[]{:S(2)}, u32[]{:S(2)}) collective-permute-start(bf16[128,256]{1,0:T(8,128)(2,1)S(1)} %bitcast.16), channel_id=1, source_target_pairs={{0,2},{1,3},{2,0},{3,1},{4,6},{5,7},{6,4},{7,5},{8,10},{9,11},{10,... | collective-permute-start | bytes 196616 | tf_op jit(solution)/shard_map/ppermute | solution.py:461
  15.9 1.6 %adapter_home.1 = (bf16[128,1024]{1,0:T(8,128)(2,1)S(1)}, bf16[128,1024]{1,0:T(8,128)(2,1)S(1)}) custom-call(s32[2,8]{1,0:T(2,128)S(1)} %pad_add_fusion.routes, bf16[288,2048]{1,0:T(8,128)(2,1)S(1)} %get-tuple-element.49.slabs, bf16[1024,2048]{1,0:T(8,128)(2,1)S(1)} %get-tuple-element.42.weight), custom_call_target="tpu_custom_call" | custom-call | flops 2 | bytes 6 | tf_op jit(solution)/shard_map/adapter_home/pallas_call | solution.py:188
  17.6 1.2 %collective-permute-done.4.arrived.from_y = bf16[2,64,1024]{2,1,0:T(8,128)(2,1)S(1)} collective-permute-done((bf16[2,64,1024]{2,1,0:T(8,128)(2,1)S(1)}, bf16[2,64,1024]{2,1,0:T(8,128)(2,1)S(1)}, u32[]{:S(2)}, u32[]{:S(2)}) %collective-permute-start.4) | collective-permute-done | bytes 262176 | tf_op jit(solution)/shard_map/ppermute | solution.py:461
  18.9 1.8 %collective-permute-start.5 = (bf16[64,1024]{1,0:T(8,128)(2,1)S(1)}, bf16[64,1024]{1,0:T(8,128)(2,1)S(1)}, u32[]{:S(2)}, u32[]{:S(2)}) collective-permute-start(bf16[64,1024]{1,0:T(8,128)(2,1)S(1)} %relay.3), channel_id=1, source_target_pairs={{0,8},{4,12},{8,0},{12,4},{16,24},{20,28},{24,16},{28,20},{1,9},{5... | collective-permute-start | bytes 393224 | tf_op jit(solution)/shard_map/ppermute | solution.py:461
  20.7 1.6 %collective-permute-start.3 = (bf16[64,1024]{1,0:T(8,128)(2,1)S(1)}, bf16[64,1024]{1,0:T(8,128)(2,1)S(1)}, u32[]{:S(2)}, u32[]{:S(2)}) collective-permute-start(bf16[64,1024]{1,0:T(8,128)(2,1)S(1)} %relay.2), channel_id=1, source_target_pairs={{0,16},{4,20},{8,24},{12,28},{16,0},{20,4},{24,8},{28,12},{1,17},{... | collective-permute-start | bytes 393224 | tf_op jit(solution)/shard_map/ppermute | solution.py:461
  22.3 1.6 %collective-permute-start.9 = (bf16[256,256]{1,0:T(8,128)(2,1)S(1)}, bf16[256,256]{1,0:T(8,128)(2,1)S(1)}, u32[]{:S(2)}, u32[]{:S(2)}) collective-permute-start(bf16[256,256]{1,0:T(8,128)(2,1)S(1)} %pad_maximum_fusion.1), channel_id=1, source_target_pairs={{0,1},{1,0},{2,3},{3,2},{4,5},{5,4},{6,7},{7,6},{8,9},{9,8},{10,11... | collective-permute-start | bytes 393224 | tf_op jit(solution)/shard_map/ppermute | solution.py:461
  24.2 0.9 %transposed_weights.1 = (bf16[4,512,256]{2,1,0:T(8,128)(2,1)S(1)}, bf16[4,1024,256]{2,1,0:T(8,128)(2,1)S(1)}) custom-call(bf16[1024,512]{1,0:T(8,128)(2,1)S(1)} %bitcast.11, bf16[1024,1024]{1,0:T(8,128)(2,1)S(1)} %copy-done), custom_call_target="tpu_custom_call" | custom-call | flops 2 | bytes 6 | tf_op jit(solution)/shard_map/transposed_weights/pallas_call | solution.py:363
  25.8 0.5 stream_and_swish.1
  26.3 2.7 %collective-permute-start.10 = (bf16[128,256]{1,0:T(8,128)(2,1)S(1)}, bf16[128,256]{1,0:T(8,128)(2,1)S(1)}, u32[]{:S(2)}, u32[]{:S(2)}) collective-permute-start(bf16[128,256]{1,0:T(8,128)(2,1)S(1)} %get-tuple-element.65), channel_id=1, source_target_pairs={{0,2},{1,3},{2,0},{3,1},{4,6},{5,7},{6,4},{7,5},{8,10},{9,11},{10,... | collective-permute-start | bytes 196616 | tf_op jit(solution)/shard_map/ppermute | solution.py:469
  29.0 1.5 %collective-permute-start.11 = (bf16[128,256]{1,0:T(8,128)(2,1)S(1)}, bf16[128,256]{1,0:T(8,128)(2,1)S(1)}, u32[]{:S(2)}, u32[]{:S(2)}) collective-permute-start(bf16[128,256]{1,0:T(8,128)(2,1)S(1)} %get-tuple-element.66), channel_id=1, source_target_pairs={{0,1},{1,2},{2,3},{3,0},{4,5},{5,6},{6,7},{7,4},{8,9},{9,10},{10,1... | collective-permute-start | bytes 196616 | tf_op jit(solution)/shard_map/ppermute | solution.py:469
  30.5 2.3 %collective-permute-start.12 = (bf16[128,256]{1,0:T(8,128)(2,1)S(1)}, bf16[128,256]{1,0:T(8,128)(2,1)S(1)}, u32[]{:S(2)}, u32[]{:S(2)}) collective-permute-start(bf16[128,256]{1,0:T(8,128)(2,1)S(1)} %get-tuple-element.67), channel_id=1, source_target_pairs={{0,3},{1,0},{2,1},{3,2},{4,7},{5,4},{6,5},{7,6},{8,11},{9,8},{10,9... | collective-permute-start | bytes 196616 | tf_op jit(solution)/shard_map/ppermute | solution.py:469
  32.9 0.5 %forward_gates.1 = (f32[128,256]{1,0:T(8,128)S(1)}, f32[128,256]{1,0:T(8,128)S(1)}, f32[128,256]{1,0:T(8,128)S(1)}) custom-call(s32[1]{0:T(128)S(6)} %copy.14.valid, bf16[1024,512]{1,0:T(8,128)(2,1)S(1)} %bitcast.12, f32[9,256]{1,0:T(8,128)S(1)} %convert_element_type.29.taps_ref, f32[1,256]{1,0:T(1,128)S(1)} %bitcast.13, f32[1,256]{1,0:T(1,128)S(1)} %bitcast.14, ...), custom_call_target="tpu_custom_call" | custom-call | flops 134217728 | bytes 1441792 | tf_op jit(solution)/shard_map/forward_gates/pallas_call | solution.py:406
  33.7 1.5 %collective-permute-done.11.refs_2_ = bf16[128,256]{1,0:T(8,128)(2,1)S(1)} collective-permute-done((bf16[128,256]{1,0:T(8,128)(2,1)S(1)}, bf16[128,256]{1,0:T(8,128)(2,1)S(1)}, u32[]{:S(2)}, u32[]{:S(2)}) %collective-permute-start.11) | collective-permute-done | bytes 65568 | tf_op jit(solution)/shard_map/ppermute | solution.py:469
  35.2 0.3 collective-permute-done.12.refs_3_
  35.5 0.5 backward_module.1
  36.0 0.9 %collective-permute-start.14 = (bf16[128,256]{1,0:T(8,128)(2,1)S(1)}, bf16[128,256]{1,0:T(8,128)(2,1)S(1)}, u32[]{:S(2)}, u32[]{:S(2)}) collective-permute-start(bf16[128,256]{1,0:T(8,128)(2,1)S(1)} %get-tuple-element.75), channel_id=1, source_target_pairs={{0,2},{1,3},{2,0},{3,1},{4,6},{5,7},{6,4},{7,5},{8,10},{9,11},{10,... | collective-permute-start | bytes 196616 | tf_op jit(solution)/shard_map/ppermute | solution.py:469
  36.9 3.1 %collective-permute-start.15 = (bf16[128,256]{1,0:T(8,128)(2,1)S(1)}, bf16[128,256]{1,0:T(8,128)(2,1)S(1)}, u32[]{:S(2)}, u32[]{:S(2)}) collective-permute-start(bf16[128,256]{1,0:T(8,128)(2,1)S(1)} %get-tuple-element.76), channel_id=1, source_target_pairs={{0,1},{1,2},{2,3},{3,0},{4,5},{5,6},{6,7},{7,4},{8,9},{9,10},{10,1... | collective-permute-start | bytes 196616 | tf_op jit(solution)/shard_map/ppermute | solution.py:469
  40.0 0.7 %collective-permute-start.16 = (bf16[128,256]{1,0:T(8,128)(2,1)S(1)}, bf16[128,256]{1,0:T(8,128)(2,1)S(1)}, u32[]{:S(2)}, u32[]{:S(2)}) collective-permute-start(bf16[128,256]{1,0:T(8,128)(2,1)S(1)} %get-tuple-element.77), channel_id=1, source_target_pairs={{0,3},{1,0},{2,1},{3,2},{4,7},{5,4},{6,5},{7,6},{8,11},{9,8},{10,9... | collective-permute-start | bytes 196616 | tf_op jit(solution)/shard_map/ppermute | solution.py:469
  40.7 0.8 %collective-permute-start.6 = (bf16[128,256]{1,0:T(8,128)(2,1)S(1)}, bf16[128,256]{1,0:T(8,128)(2,1)S(1)}, u32[]{:S(2)}, u32[]{:S(2)}) collective-permute-start(bf16[128,256]{1,0:T(8,128)(2,1)S(1)} %get-tuple-element.57), channel_id=1, source_target_pairs={{0,2},{1,3},{2,0},{3,1},{4,6},{5,7},{6,4},{7,5},{8,10},{9,11},{10,... | collective-permute-start | bytes 196616 | tf_op jit(solution)/shard_map/ppermute | solution.py:469
  41.5 0.6 %collective-permute-start.7 = (bf16[128,256]{1,0:T(8,128)(2,1)S(1)}, bf16[128,256]{1,0:T(8,128)(2,1)S(1)}, u32[]{:S(2)}, u32[]{:S(2)}) collective-permute-start(bf16[128,256]{1,0:T(8,128)(2,1)S(1)} %get-tuple-element.58), channel_id=1, source_target_pairs={{0,1},{1,2},{2,3},{3,0},{4,5},{5,6},{6,7},{7,4},{8,9},{9,10},{10,1... | collective-permute-start | bytes 196616 | tf_op jit(solution)/shard_map/ppermute | solution.py:469
  42.1 2.1 %collective-permute-done.14 = bf16[128,256]{1,0:T(8,128)(2,1)S(1)} collective-permute-done((bf16[128,256]{1,0:T(8,128)(2,1)S(1)}, bf16[128,256]{1,0:T(8,128)(2,1)S(1)}, u32[]{:S(2)}, u32[]{:S(2)}) %collective-permute-start.14) | collective-permute-done | bytes 65568 | tf_op jit(solution)/shard_map/ppermute | solution.py:469
  44.2 1.7 %collective-permute-start.13 = (bf16[128,256]{1,0:T(8,128)(2,1)S(1)}, bf16[128,256]{1,0:T(8,128)(2,1)S(1)}, u32[]{:S(2)}, u32[]{:S(2)}) collective-permute-start(bf16[128,256]{1,0:T(8,128)(2,1)S(1)} %get-tuple-element.73), channel_id=1, source_target_pairs={{0,3},{1,0},{2,1},{3,2},{4,7},{5,4},{6,5},{7,6},{8,11},{9,8},{10,9... | collective-permute-start | bytes 196616 | tf_op jit(solution)/shard_map/ppermute | solution.py:469
  46.0 0.7 %fusion.1 = bf16[1,128,256]{2,1,0:T(8,128)(2,1)} fusion(bf16[128,256]{1,0:T(8,128)(2,1)S(1)} %collective-permute-done.16, bf16[128,256]{1,0:T(8,128)(2,1)S(1)} %collective-permute-done.15, f32[128,256]{1,0:T(8,128)S(1)} %get-tuple-element.74, bf16[128,256]{1,0:T(8,128)(2,1)S(1)} %collective-permute-done.14), kind=kLoop, calls=%fused_computation.5 | loop fusion | flops 229376 | bytes 393216 | tf_op jit(solution)/shard_map/broadcast_in_dim | solution.py:544
  46.7 1.7 %collective-permute-done.6 = bf16[128,256]{1,0:T(8,128)(2,1)S(1)} collective-permute-done((bf16[128,256]{1,0:T(8,128)(2,1)S(1)}, bf16[128,256]{1,0:T(8,128)(2,1)S(1)}, u32[]{:S(2)}, u32[]{:S(2)}) %collective-permute-start.6) | collective-permute-done | bytes 65568 | tf_op jit(solution)/shard_map/ppermute | solution.py:469
  48.4 0.4 collective-permute-done.13
  48.8 0.7 %fusion = bf16[1,128,256]{2,1,0:T(8,128)(2,1)} fusion(bf16[128,256]{1,0:T(8,128)(2,1)S(1)} %collective-permute-done.13, bf16[128,256]{1,0:T(8,128)(2,1)S(1)} %collective-permute-done.7, f32[128,256]{1,0:T(8,128)S(1)} %get-tuple-element.56, bf16[128,256]{1,0:T(8,128)(2,1)S(1)} %collective-permute-done.6), kind=kLoop, calls=%fused_computation.4 | loop fusion | flops 229376 | bytes 393216 | tf_op jit(solution)/shard_map/broadcast_in_dim | solution.py:544
  (32 shorter events, 0.9 us)
Async XLA Ops:
  6.1 2.9 %collective-permute-start = (bf16[3,128,1024]{2,1,0:T(8,128)(2,1)S(1)}, bf16[3,128,1024]{2,1,0:T(8,128)(2,1)S(1)}, u32[]{:S(2)}, u32[]{:S(2)}) collective-permute-start(bf16[3,128,1024]{2,1,0:T(8,128)(2,1)S(1)} %get-tuple-element.43), channel_id=1, source_target_pairs={{0,4},{4,0},{8,12},{12,8},{16,20},{20,16},{24,28},{28,24},{1,5},{5... | collective-permute-start | bytes 2359304 | tf_op jit(solution)/shard_map/ppermute | solution.py:461
  6.6 6.7 %copy-start.4 = (bf16[1,128,256]{2,1,0:T(8,128)(2,1)S(1)}, bf16[1,128,256]{2,1,0:T(8,128)(2,1)}, u32[]{:S(2)}) copy-start(bf16[1,128,256]{2,1,0:T(8,128)(2,1)} %param.15) | copy-start | bytes 196612
  9.2 9.6 %collective-permute-start.4 = (bf16[2,64,1024]{2,1,0:T(8,128)(2,1)S(1)}, bf16[2,64,1024]{2,1,0:T(8,128)(2,1)S(1)}, u32[]{:S(2)}, u32[]{:S(2)}) collective-permute-start(bf16[2,64,1024]{2,1,0:T(8,128)(2,1)S(1)} %get-tuple-element.54), channel_id=1, source_target_pairs={{0,16},{4,20},{8,24},{12,28},{16,0},{20,4},{24,8},{28,12},{1,17},{... | collective-permute-start | bytes 786440 | tf_op jit(solution)/shard_map/ppermute | solution.py:461
  11.9 8.8 %collective-permute-start.2 = (bf16[2,64,1024]{2,1,0:T(8,128)(2,1)S(1)}, bf16[2,64,1024]{2,1,0:T(8,128)(2,1)S(1)}, u32[]{:S(2)}, u32[]{:S(2)}) collective-permute-start(bf16[2,64,1024]{2,1,0:T(8,128)(2,1)S(1)} %get-tuple-element.52), channel_id=1, source_target_pairs={{0,8},{4,12},{8,0},{12,4},{16,24},{20,28},{24,16},{28,20},{1,9},{5... | collective-permute-start | bytes 786440 | tf_op jit(solution)/shard_map/ppermute | solution.py:461
  13.3 8.9 %collective-permute-start.8 = (bf16[128,256]{1,0:T(8,128)(2,1)S(1)}, bf16[128,256]{1,0:T(8,128)(2,1)S(1)}, u32[]{:S(2)}, u32[]{:S(2)}) collective-permute-start(bf16[128,256]{1,0:T(8,128)(2,1)S(1)} %bitcast.16), channel_id=1, source_target_pairs={{0,2},{1,3},{2,0},{3,1},{4,6},{5,7},{6,4},{7,5},{8,10},{9,11},{10,... | collective-permute-start | bytes 196616 | tf_op jit(solution)/shard_map/ppermute | solution.py:461
  15.9 8.0 %copy-start.3 = (bf16[1024,2,256]{2,1,0:T(2,128)(2,1)S(1)}, bf16[1024,2,256]{2,1,0:T(2,128)(2,1)}, u32[]{:S(2)}) copy-start(bf16[1024,2,256]{2,1,0:T(2,128)(2,1)} %param.16) | copy-start | bytes 3145732
  17.6 6.6 %copy-start = (bf16[1024,1024]{1,0:T(8,128)(2,1)S(1)}, bf16[1024,1024]{1,0:T(8,128)(2,1)}, u32[]{:S(2)}) copy-start(bf16[1024,1024]{1,0:T(8,128)(2,1)} %project.1) | copy-start | bytes 6291460
  17.6 8.3 %collective-permute-start.1 = (bf16[128,1024]{1,0:T(8,128)(2,1)S(1)}, bf16[128,1024]{1,0:T(8,128)(2,1)S(1)}, u32[]{:S(2)}, u32[]{:S(2)}) collective-permute-start(bf16[128,1024]{1,0:T(8,128)(2,1)S(1)} %get-tuple-element.51), channel_id=1, source_target_pairs={{0,4},{4,0},{8,12},{12,8},{16,20},{20,16},{24,28},{28,24},{1,5},{5... | collective-permute-start | bytes 786440 | tf_op jit(solution)/shard_map/ppermute | solution.py:461
  18.9 6.9 %collective-permute-start.5 = (bf16[64,1024]{1,0:T(8,128)(2,1)S(1)}, bf16[64,1024]{1,0:T(8,128)(2,1)S(1)}, u32[]{:S(2)}, u32[]{:S(2)}) collective-permute-start(bf16[64,1024]{1,0:T(8,128)(2,1)S(1)} %relay.3), channel_id=1, source_target_pairs={{0,8},{4,12},{8,0},{12,4},{16,24},{20,28},{24,16},{28,20},{1,9},{5... | collective-permute-start | bytes 393224 | tf_op jit(solution)/shard_map/ppermute | solution.py:461
  20.7 5.1 %collective-permute-start.3 = (bf16[64,1024]{1,0:T(8,128)(2,1)S(1)}, bf16[64,1024]{1,0:T(8,128)(2,1)S(1)}, u32[]{:S(2)}, u32[]{:S(2)}) collective-permute-start(bf16[64,1024]{1,0:T(8,128)(2,1)S(1)} %relay.2), channel_id=1, source_target_pairs={{0,16},{4,20},{8,24},{12,28},{16,0},{20,4},{24,8},{28,12},{1,17},{... | collective-permute-start | bytes 393224 | tf_op jit(solution)/shard_map/ppermute | solution.py:461
  22.3 10.6 %collective-permute-start.9 = (bf16[256,256]{1,0:T(8,128)(2,1)S(1)}, bf16[256,256]{1,0:T(8,128)(2,1)S(1)}, u32[]{:S(2)}, u32[]{:S(2)}) collective-permute-start(bf16[256,256]{1,0:T(8,128)(2,1)S(1)} %pad_maximum_fusion.1), channel_id=1, source_target_pairs={{0,1},{1,0},{2,3},{3,2},{4,5},{5,4},{6,7},{7,6},{8,9},{9,8},{10,11... | collective-permute-start | bytes 393224 | tf_op jit(solution)/shard_map/ppermute | solution.py:461
  24.1 1.6 %copy-start.5 = (bf16[9,256]{1,0:T(8,128)(2,1)S(1)}, bf16[9,256]{1,0:T(8,128)(2,1)}, u32[]{:S(2)}) copy-start(bf16[9,256]{1,0:T(8,128)(2,1)} %param.17) | copy-start | bytes 13828
  25.8 7.1 %copy-start.1 = (f32[256]{0:T(256)S(1)}, f32[256]{0:T(256)}, u32[]{:S(2)}) copy-start(f32[256]{0:T(256)} %param.18) | copy-start | bytes 3076
  25.8 7.1 %copy-start.2 = (f32[256]{0:T(256)S(1)}, f32[256]{0:T(256)}, u32[]{:S(2)}) copy-start(f32[256]{0:T(256)} %param.19) | copy-start | bytes 3076
  26.3 7.3 %collective-permute-start.10 = (bf16[128,256]{1,0:T(8,128)(2,1)S(1)}, bf16[128,256]{1,0:T(8,128)(2,1)S(1)}, u32[]{:S(2)}, u32[]{:S(2)}) collective-permute-start(bf16[128,256]{1,0:T(8,128)(2,1)S(1)} %get-tuple-element.65), channel_id=1, source_target_pairs={{0,2},{1,3},{2,0},{3,1},{4,6},{5,7},{6,4},{7,5},{8,10},{9,11},{10,... | collective-permute-start | bytes 196616 | tf_op jit(solution)/shard_map/ppermute | solution.py:469
  29.0 6.2 %collective-permute-start.11 = (bf16[128,256]{1,0:T(8,128)(2,1)S(1)}, bf16[128,256]{1,0:T(8,128)(2,1)S(1)}, u32[]{:S(2)}, u32[]{:S(2)}) collective-permute-start(bf16[128,256]{1,0:T(8,128)(2,1)S(1)} %get-tuple-element.66), channel_id=1, source_target_pairs={{0,1},{1,2},{2,3},{3,0},{4,5},{5,6},{6,7},{7,4},{8,9},{9,10},{10,1... | collective-permute-start | bytes 196616 | tf_op jit(solution)/shard_map/ppermute | solution.py:469
  30.5 5.0 %collective-permute-start.12 = (bf16[128,256]{1,0:T(8,128)(2,1)S(1)}, bf16[128,256]{1,0:T(8,128)(2,1)S(1)}, u32[]{:S(2)}, u32[]{:S(2)}) collective-permute-start(bf16[128,256]{1,0:T(8,128)(2,1)S(1)} %get-tuple-element.67), channel_id=1, source_target_pairs={{0,3},{1,0},{2,1},{3,2},{4,7},{5,4},{6,5},{7,6},{8,11},{9,8},{10,9... | collective-permute-start | bytes 196616 | tf_op jit(solution)/shard_map/ppermute | solution.py:469
  36.0 8.2 %collective-permute-start.14 = (bf16[128,256]{1,0:T(8,128)(2,1)S(1)}, bf16[128,256]{1,0:T(8,128)(2,1)S(1)}, u32[]{:S(2)}, u32[]{:S(2)}) collective-permute-start(bf16[128,256]{1,0:T(8,128)(2,1)S(1)} %get-tuple-element.75), channel_id=1, source_target_pairs={{0,2},{1,3},{2,0},{3,1},{4,6},{5,7},{6,4},{7,5},{8,10},{9,11},{10,... | collective-permute-start | bytes 196616 | tf_op jit(solution)/shard_map/ppermute | solution.py:469
  36.9 9.1 %collective-permute-start.15 = (bf16[128,256]{1,0:T(8,128)(2,1)S(1)}, bf16[128,256]{1,0:T(8,128)(2,1)S(1)}, u32[]{:S(2)}, u32[]{:S(2)}) collective-permute-start(bf16[128,256]{1,0:T(8,128)(2,1)S(1)} %get-tuple-element.76), channel_id=1, source_target_pairs={{0,1},{1,2},{2,3},{3,0},{4,5},{5,6},{6,7},{7,4},{8,9},{9,10},{10,1... | collective-permute-start | bytes 196616 | tf_op jit(solution)/shard_map/ppermute | solution.py:469
  40.0 6.0 %collective-permute-start.16 = (bf16[128,256]{1,0:T(8,128)(2,1)S(1)}, bf16[128,256]{1,0:T(8,128)(2,1)S(1)}, u32[]{:S(2)}, u32[]{:S(2)}) collective-permute-start(bf16[128,256]{1,0:T(8,128)(2,1)S(1)} %get-tuple-element.77), channel_id=1, source_target_pairs={{0,3},{1,0},{2,1},{3,2},{4,7},{5,4},{6,5},{7,6},{8,11},{9,8},{10,9... | collective-permute-start | bytes 196616 | tf_op jit(solution)/shard_map/ppermute | solution.py:469
  40.7 7.6 %collective-permute-start.6 = (bf16[128,256]{1,0:T(8,128)(2,1)S(1)}, bf16[128,256]{1,0:T(8,128)(2,1)S(1)}, u32[]{:S(2)}, u32[]{:S(2)}) collective-permute-start(bf16[128,256]{1,0:T(8,128)(2,1)S(1)} %get-tuple-element.57), channel_id=1, source_target_pairs={{0,2},{1,3},{2,0},{3,1},{4,6},{5,7},{6,4},{7,5},{8,10},{9,11},{10,... | collective-permute-start | bytes 196616 | tf_op jit(solution)/shard_map/ppermute | solution.py:469
  41.5 6.9 %collective-permute-start.7 = (bf16[128,256]{1,0:T(8,128)(2,1)S(1)}, bf16[128,256]{1,0:T(8,128)(2,1)S(1)}, u32[]{:S(2)}, u32[]{:S(2)}) collective-permute-start(bf16[128,256]{1,0:T(8,128)(2,1)S(1)} %get-tuple-element.58), channel_id=1, source_target_pairs={{0,1},{1,2},{2,3},{3,0},{4,5},{5,6},{6,7},{7,4},{8,9},{9,10},{10,1... | collective-permute-start | bytes 196616 | tf_op jit(solution)/shard_map/ppermute | solution.py:469
  44.2 4.6 %collective-permute-start.13 = (bf16[128,256]{1,0:T(8,128)(2,1)S(1)}, bf16[128,256]{1,0:T(8,128)(2,1)S(1)}, u32[]{:S(2)}, u32[]{:S(2)}) collective-permute-start(bf16[128,256]{1,0:T(8,128)(2,1)S(1)} %get-tuple-element.73), channel_id=1, source_target_pairs={{0,3},{1,0},{2,1},{3,2},{4,7},{5,4},{6,5},{7,6},{8,11},{9,8},{10,9... | collective-permute-start | bytes 196616 | tf_op jit(solution)/shard_map/ppermute | solution.py:469
